TPU v7x, 32 devices: a whole 2x2x4 slice. The times are simulated.
32 devices in a mesh: sea: 2 (over x), body: 4 (over z), harm: 4 (over y, core).
Axes of the slice: x: 2, y: 2, z: 4, core: 2. Of those that a mesh axis runs over, the one named last changes fastest.
Arguments:
- vel: float32 [2, 128, 256, 128], P(None, 'harm', 'body', 'sea'), parts along dimension 3, may hold values from -4 to 4
- imped: bfloat16 [2, 128, 256, 256], P(None, 'harm', 'body'), may hold values from -3 to 3, as said below
- excite: float32 [2, 128, 256, 128], P(None, 'harm', 'body', 'sea'), parts along dimension 3, may hold values from -16 to 16
- quad_coef: float32 [256], P('body'), may hold values from 0.3 to 3
- coul_coef: float32 [256], P('body'), may hold values from 0.3 to 3
Outputs:
- vel_new: float32 [2, 128, 256, 128], P(None, 'harm', 'body', 'sea'), parts along dimension 3
- rms: float32 [2], P('sea'), parts along dimension 0
There are 2 independent parts, one for each index of `sea`. A program takes and returns all parts, laid end to end along the dimension named above; an argument that names none is the same for every part. Nothing has to cross between parts.
Inputs may be any that keep to these rules, and one draw needn't show every extreme that they name: imped[c, h, a, b] equals imped[c, h, b, a] for all c, h, a, b, and every diagonal real part imped[0, h, b, b] lies between 1 and 3.
All inputs are finite; a program needn't handle non-finite values.
Results may differ from a plain program's by a relative error of at most 0.0039.
Values may be sent and summed in bfloat16 or wider, within the bound.
No kernel may reach another device: no remote copies, remote signals or barrier semaphores. Data moves between devices by JAX's collectives and lax.ppermute only.
A program may use at most 192 MiB of HBM per device.

v0:
```python
import functools
import math

import ml_dtypes
import numpy as np
import jax
import jax.numpy as jnp
from jax import lax
from jax.experimental import pallas as pl
from jax.experimental.pallas import tpu as pltpu
from jax.sharding import PartitionSpec as P

H = 128
NT = 512
DELTA = 0.1
F32 = jnp.float32
BF16 = jnp.bfloat16


def split(x):
    high = x.astype(BF16)
    return high, (x - high.astype(F32)).astype(BF16)


def wave_constants(groups):
    k = np.arange(1, H + 1)
    phase = np.arange(NT)[None, :] * k[:, None] % NT
    angle = phase * (2.0 * math.pi / NT)
    per = H // groups
    waves = np.stack([np.cos(angle), -np.sin(angle)]).reshape(2, groups, per, NT)
    table = np.swapaxes(waves, 0, 1).reshape(2 * H, NT) / math.sqrt(H)
    table = table.astype(np.float32)
    high = table.astype(ml_dtypes.bfloat16)
    low = (table - high.astype(np.float32)).astype(ml_dtypes.bfloat16)
    forward = np.concatenate([high.T, low.T], axis=0)
    size = 2 * per
    inverse = np.stack([high.reshape(groups, size, NT), low.reshape(groups, size, NT)], axis=1).reshape(4 * H, NT)
    return forward, inverse


def pack_couple(harm, bodies, reals, vel_ref, out_ref):
    for h in range(harm):
        rows = pl.ds(h * bodies, bodies)
        re = vel_ref[rows, :]
        im = vel_ref[pl.ds((harm + h) * bodies, bodies), :]
        out_ref[rows, :] = jnp.concatenate([re, im], axis=1).astype(BF16)


def pack_time(harm, bodies, reals, vel_ref, full_ref, low_ref):
    half = bodies // 2
    for j in range(half):
        one = vel_ref[pl.ds(j, 2 * harm, stride=bodies), :]
        two = vel_ref[pl.ds(j + half, 2 * harm, stride=bodies), :]
        both = jnp.concatenate([one, two], axis=1)
        cols = pl.ds(j * 2 * reals, 2 * reals)
        full_ref[:, cols] = both
        low_ref[:, cols] = both.astype(BF16)


def time_kernel(harm, bodies, reals, quad_ref, coul_ref, own_ref, core_ref, far_ref, far_core_ref, fwd_ref, inv_ref,
                force_ref, slope_ref, high_ref, low_ref):
    step = pl.program_id(0)
    me = lax.axis_index("harm")
    size = 2 * harm
    width = own_ref.shape[1]
    group = 2 * reals
    half = bodies // 2

    def rows(index):
        return pl.ds(pl.multiple_of(index * size, size), size)

    low_ref[...] = jnp.zeros_like(low_ref)
    for ref, flip in ((own_ref, 0), (core_ref, 1)):
        high, low = split(ref[...])
        high_ref[rows(me ^ flip), :] = high
        low_ref[rows(me ^ flip), :] = low
    high_ref[rows(me ^ 2), :] = far_ref[...]
    high_ref[rows(me ^ 3), :] = far_core_ref[...]

    high = high_ref[...]
    both = jnp.dot(fwd_ref[...], high, preferred_element_type=F32)
    signal = both[:NT] + both[NT:] + jnp.dot(fwd_ref[:NT, :], low_ref[...], preferred_element_type=F32)

    lane = lax.broadcasted_iota(jnp.int32, (1, group), 1)
    quads, couls = [], []
    for g in range(width // group):
        first = step * (width // group) + g
        quads.append(jnp.where(lane < reals, quad_ref[first], quad_ref[first + half]))
        couls.append(jnp.where(lane < reals, coul_ref[first], coul_ref[first + half]))
    quad = jnp.concatenate(quads, axis=1)
    coul = jnp.concatenate(couls, axis=1)

    square = signal * signal + DELTA * DELTA
    inverse = lax.rsqrt(square)
    force_time = signal * inverse * (quad * square + coul)
    slope = inverse * ((2.0 * quad) * square - (DELTA * DELTA) * quad + (DELTA * DELTA) * coul * (inverse * inverse))
    mean = jnp.sum(slope, axis=0, keepdims=True) * (1.0 / NT)

    high, low = split(force_time)
    table = inv_ref[pl.ds(pl.multiple_of(me * 2 * size, 2 * size), 2 * size), :]
    back = jnp.dot(table, high, preferred_element_type=F32)
    back = back[:size] + back[size:] + jnp.dot(table[:size], low, preferred_element_type=F32)
    back = back * (2.0 * H / NT)

    for g in range(width // group):
        first = step * (width // group) + g
        re = back[:harm, g * group:(g + 1) * group]
        im = back[harm:, g * group:(g + 1) * group]
        force_ref[pl.ds(first, harm, stride=bodies), :] = jnp.concatenate([re[:, :reals], im[:, :reals]], axis=1)
        force_ref[pl.ds(first + half, harm, stride=bodies), :] = jnp.concatenate([re[:, reals:], im[:, reals:]], axis=1)
        part = mean[:, g * group:(g + 1) * group]
        slope_ref[pl.ds(first, 1), :] = jnp.concatenate([part[:, :reals], part[:, :reals]], axis=1)
        slope_ref[pl.ds(first + half, 1), :] = jnp.concatenate([part[:, reals:], part[:, reals:]], axis=1)


def prepare_kernel(bodies, reals, imped_ref, force_ref, slope_ref, exre_ref, exim_ref, vre_ref, vim_ref,
                   rest_ref, p_ref, q_ref, vel_ref):
    count = imped_ref.shape[1]
    everyone = imped_ref.shape[3]
    first = lax.axis_index("body") * bodies
    row = lax.broadcasted_iota(jnp.int32, (bodies, everyone), 0)
    col = lax.broadcasted_iota(jnp.int32, (bodies, everyone), 1)
    mine = col == row + first
    ones = jnp.ones((everyone, 2 * reals), BF16)
    sign = jnp.where(lax.broadcasted_iota(jnp.int32, (bodies, 2 * reals), 1) < reals, 1.0, -1.0)
    slope = slope_ref[...]
    for h in range(count):
        rows = pl.ds(h * bodies, bodies)
        real = jnp.where(mine, imped_ref[0, h], jnp.zeros((), BF16))
        imag = jnp.where(mine, imped_ref[1, h], jnp.zeros((), BF16))
        den_re = jnp.dot(real, ones, preferred_element_type=F32) + slope
        den_im = jnp.dot(imag, ones, preferred_element_type=F32)
        inverse = 1.0 / (den_re * den_re + den_im * den_im)
        p_ref[rows, :] = den_re * inverse
        q_ref[rows, :] = den_im * inverse * sign
        rest_ref[rows, :] = force_ref[rows, :] - jnp.concatenate([exre_ref[rows, :], exim_ref[rows, :]], axis=1)
        vel_ref[rows, :] = jnp.concatenate([vre_ref[rows, :], vim_ref[rows, :]], axis=1)


def couple_kernel(bodies, reals, flips, imped_ref, *refs):
    pieces, (rest_ref, res_ref, total_ref, held_ref, sum_ref) = refs[:-5], refs[-5:]
    count = imped_ref.shape[1]
    step = pl.program_id(0)
    me = lax.axis_index("body")
    sign = jnp.where(lax.broadcasted_iota(jnp.int32, (bodies, 2 * reals), 1) < reals, -1.0, 1.0)
    total = jnp.zeros((bodies, 2 * reals), F32)
    for h in range(count):
        rows = pl.ds(h * bodies, bodies)
        if flips is None:
            vels = pieces[0][:, h].reshape(-1, 2 * reals)
        else:
            slot = h % 2
            for flip, ref in zip(flips, pieces[:-2]):
                held_ref[slot, pl.ds(pl.multiple_of((me ^ flip) * bodies, bodies), bodies), :] = ref[rows, :]
            ends = jnp.logical_or(me == 0, me == 3)
            held_ref[slot, pl.ds(pl.multiple_of((me ^ 2) * bodies, bodies), bodies), :] = jnp.where(
                ends, pieces[-2][rows, :], pieces[-1][rows, :])
            vels = held_ref[slot]
        both = imped_ref[:, h].reshape(2 * bodies, imped_ref.shape[3])
        out = jnp.dot(both, vels, preferred_element_type=F32)
        coupled = out[:bodies] + sign * pltpu.roll(out[bodies:], reals, 1)
        res = coupled + rest_ref[rows, :]
        res_ref[rows, :] = res
        total = total + res * res
    kept = jnp.sum(total.reshape(bodies // 8, 8, 2 * reals), axis=0)

    @pl.when(step == 0)
    def _():
        sum_ref[...] = kept

    @pl.when(step > 0)
    def _():
        sum_ref[...] = sum_ref[...] + kept

    @pl.when(step == pl.num_programs(0) - 1)
    def _():
        total_ref[...] = jnp.broadcast_to(jnp.sum(sum_ref[...]), total_ref.shape)


def finish_kernel(bodies, reals, res_ref, p_ref, q_ref, vel_ref, out_ref):
    res = res_ref[...]
    new = vel_ref[...] - (res * p_ref[...] + pltpu.roll(res, reals, 1) * q_ref[...])
    out_ref[0] = new[:, :reals]
    out_ref[1] = new[:, reals:]


def gather_line(x, axis):
    near = lax.ppermute(x, axis, [(0, 1), (1, 0), (2, 3), (3, 2)])
    cross = lax.ppermute(x, axis, [(1, 2), (2, 1), (0, 3), (3, 0)])
    outer = lax.ppermute(cross, axis, [(1, 0), (2, 3)])
    inner = lax.ppermute(near, axis, [(1, 2), (2, 1)])
    return x, near, cross, outer, inner


def params(mib=24):
    return pltpu.CompilerParams(vmem_limit_bytes=mib << 20)


def cost(flops, moved):
    return pl.CostEstimate(flops=flops, bytes_accessed=moved, transcendentals=0)


def make_local(mesh):
    body_count = mesh.shape["body"]

    def local(vel, imped, excite, quad_coef, coul_coef):
        _, harm, bodies, reals = vel.shape
        everyone = imped.shape[3]
        group = 2 * reals
        total_rows = harm * bodies
        columns = bodies * reals
        forward, inverse = wave_constants(H // harm)
        flat = vel.reshape(2 * total_rows, reals)
        flat_excite = excite.reshape(2 * total_rows, reals)
        dense = jax.ShapeDtypeStruct((total_rows, group), F32)

        low = pl.pallas_call(
            functools.partial(pack_couple, harm, bodies, reals),
            out_shape=jax.ShapeDtypeStruct((total_rows, group), BF16),
            compiler_params=params(),
            cost_estimate=cost(0, 3 << 20),
            name="pack_couple",
        )(flat)
        if body_count == 4:
            pieces = gather_line(low, "body")
            flips = (0, 1, 3)
        else:
            pieces = (lax.all_gather(low, "body").reshape(body_count, harm, bodies, group),)
            flips = None

        own, own_low = pl.pallas_call(
            functools.partial(pack_time, harm, bodies, reals),
            out_shape=(
                jax.ShapeDtypeStruct((2 * harm, columns), F32),
                jax.ShapeDtypeStruct((2 * harm, columns), BF16),
            ),
            compiler_params=params(),
            cost_estimate=cost(0, 4 << 20),
            name="pack_time",
        )(flat)
        far = lax.ppermute(own_low, "harm", [(i, i ^ 2) for i in range(4)])
        core = lax.ppermute(own, "harm", [(i, i ^ 1) for i in range(4)])
        far_core = lax.ppermute(far, "harm", [(i, i ^ 1) for i in range(4)])

        width = 4 * group
        tile = pl.BlockSpec((2 * harm, width), lambda i: (0, i))
        force, slope = pl.pallas_call(
            functools.partial(time_kernel, harm, bodies, reals),
            grid=(columns // width,),
            in_specs=[
                pl.BlockSpec(memory_space=pltpu.SMEM),
                pl.BlockSpec(memory_space=pltpu.SMEM),
                tile, tile, tile, tile,
                pl.BlockSpec(forward.shape, lambda i: (0, 0)),
                pl.BlockSpec(inverse.shape, lambda i: (0, 0)),
            ],
            out_specs=[
                pl.BlockSpec((total_rows, group), lambda i: (0, 0)),
                pl.BlockSpec((bodies, group), lambda i: (0, 0)),
            ],
            out_shape=(dense, jax.ShapeDtypeStruct((bodies, group), F32)),
            scratch_shapes=[pltpu.VMEM((2 * H, width), BF16), pltpu.VMEM((2 * H, width), BF16)],
            compiler_params=params(),
            cost_estimate=cost(10**10, 6 << 20),
            name="time_kernel",
        )(quad_coef, coul_coef, own, core, far, far_core, jnp.asarray(forward), jnp.asarray(inverse))

        count = 8
        steps = harm // count
        block = pl.BlockSpec((count * bodies, group), lambda i: (i, 0))
        slim = pl.BlockSpec((count * bodies, reals), lambda i: (i, 0))
        slim_im = pl.BlockSpec((count * bodies, reals), lambda i: (i + steps, 0))
        wide = pl.BlockSpec((2, count, bodies, everyone), lambda i: (0, i, 0, 0))
        rest, factor_p, factor_q, vel_dense = pl.pallas_call(
            functools.partial(prepare_kernel, bodies, reals),
            grid=(steps,),
            in_specs=[wide, block, pl.BlockSpec((bodies, group), lambda i: (0, 0)), slim, slim_im, slim, slim_im],
            out_specs=[block] * 4,
            out_shape=(dense,) * 4,
            compiler_params=params(),
            cost_estimate=cost(10**9, 12 << 20),
            name="prepare",
        )(imped, force, slope, flat_excite, flat_excite, flat, flat)

        if flips is None:
            piece_specs = [pl.BlockSpec((body_count, count, bodies, group), lambda i: (0, i, 0, 0))]
        else:
            piece_specs = [block] * len(pieces)
        res, total = pl.pallas_call(
            functools.partial(couple_kernel, bodies, reals, flips),
            grid=(steps,),
            in_specs=[wide, *piece_specs, block],
            out_specs=[block, pl.BlockSpec((8, 128), lambda i: (0, 0))],
            out_shape=(dense, jax.ShapeDtypeStruct((8, 128), F32)),
            scratch_shapes=[pltpu.VMEM((2, everyone, group), BF16), pltpu.VMEM((8, group), F32)],
            compiler_params=params(),
            cost_estimate=cost(10**9, 8 << 20),
            name="couple",
        )(imped, *pieces, rest)

        new = pl.pallas_call(
            functools.partial(finish_kernel, bodies, reals),
            grid=(steps,),
            in_specs=[block] * 4,
            out_specs=pl.BlockSpec((2, count * bodies, reals), lambda i: (0, i, 0)),
            out_shape=jax.ShapeDtypeStruct((2, total_rows, reals), F32),
            compiler_params=params(),
            cost_estimate=cost(0, 6 << 20),
            name="finish",
        )(res, factor_p, factor_q, vel_dense)

        for axis, flip in (("harm", 1), ("harm", 2)):
            total = total + lax.ppermute(total, axis, [(i, i ^ flip) for i in range(4)])
        flip = 1
        while flip < body_count:
            total = total + lax.ppermute(total, "body", [(i, i ^ flip) for i in range(body_count)])
            flip *= 2
        rms = jnp.sqrt(total[0, :1] * (1.0 / (2.0 * H * everyone * reals)))
        return new.reshape(vel.shape), rms

    return local


def solution(mesh):
    in_specs = (
        P(None, "harm", "body", "sea"),
        P(None, "harm", "body", None),
        P(None, "harm", "body", "sea"),
        P("body"),
        P("body"),
    )
    out_specs = (P(None, "harm", "body", "sea"), P("sea"))
    return jax.shard_map(make_local(mesh), mesh=mesh, in_specs=in_specs, out_specs=out_specs, check_vma=False)
```

profile of v0, /device:TPU:0, one launch (start us, length us, event | category | flops | bytes accessed | tf_op | source)
XLA Modules:
  0.0 68.1 jit_solution(17743738830304214854)
XLA Ops:
  0.6 0.0 copy-start
  0.6 1.6 %copy-done = f32[2,32,64,64]{3,2,1,0:T(8,128)S(1)} copy-done((f32[2,32,64,64]{3,2,1,0:T(8,128)S(1)}, f32[2,32,64,64]{3,2,1,0:T(8,128)}, u32[]{:S(2)}) %copy-start) | copy-done | bytes 1048600
  2.2 0.0 copy-start.4
  2.2 0.0 copy-start.5
  2.2 0.0 copy-start.6
  2.2 0.0 copy-start.7
  2.2 1.2 %pack_time.1 = (f32[64,4096]{1,0:T(8,128)S(1)}, bf16[64,4096]{1,0:T(8,128)(2,1)S(1)}) custom-call(f32[4096,64]{1,0:T(8,128)S(1)} %bitcast.4), custom_call_target="tpu_custom_call" | custom-call | bytes 4194304 | tf_op jit(solution)/shard_map/pack_time/pallas_call | solution.py:231
  3.5 3.0 %collective-permute-start.5 = (bf16[64,4096]{1,0:T(8,128)(2,1)S(1)}, bf16[64,4096]{1,0:T(8,128)(2,1)S(1)}, u32[]{:S(2)}, u32[]{:S(2)}) collective-permute-start(bf16[64,4096]{1,0:T(8,128)(2,1)S(1)} %get-tuple-element.13), channel_id=1, source_target_pairs={{0,2},{1,3},{2,0},{3,1},{4,6},{5,7},{6,4},{7,5},{8,10},{9,11},{10,... | collective-permute-start | bytes 1572872 | tf_op jit(solution)/shard_map/ppermute | solution.py:241
  6.5 0.0 collective-permute-start.4
  6.5 0.2 pack_couple.1.refs_0_
  6.7 0.0 copy-start.1
  6.7 0.0 copy-start.2
  6.8 0.0 copy-start.3
  6.8 3.7 %collective-permute-start.1 = (bf16[2048,128]{1,0:T(8,128)(2,1)S(1)}, bf16[2048,128]{1,0:T(8,128)(2,1)S(1)}, u32[]{:S(2)}, u32[]{:S(2)}) collective-permute-start(bf16[2048,128]{1,0:T(8,128)(2,1)S(1)} %pack_couple.1.refs_0_), channel_id=1, source_target_pairs={{4,8},{8,4},{0,12},{12,0},{5,9},{9,5},{1,13},{13,1},{6,10},{10,6},... | collective-permute-start | bytes 1572872 | tf_op jit(solution)/shard_map/ppermute | solution.py:189
  10.4 0.0 collective-permute-start
  10.4 8.0 %collective-permute-done.5.far_ref = bf16[64,4096]{1,0:T(8,128)(2,1)S(1)} collective-permute-done((bf16[64,4096]{1,0:T(8,128)(2,1)S(1)}, bf16[64,4096]{1,0:T(8,128)(2,1)S(1)}, u32[]{:S(2)}, u32[]{:S(2)}) %collective-permute-start.5) | collective-permute-done | bytes 524320 | tf_op jit(solution)/shard_map/ppermute | solution.py:241
  18.4 0.0 collective-permute-start.6
  18.4 5.0 %collective-permute-done.1.refs_2_ = bf16[2048,128]{1,0:T(8,128)(2,1)S(1)} collective-permute-done((bf16[2048,128]{1,0:T(8,128)(2,1)S(1)}, bf16[2048,128]{1,0:T(8,128)(2,1)S(1)}, u32[]{:S(2)}, u32[]{:S(2)}) %collective-permute-start.1) | collective-permute-done | bytes 524320 | tf_op jit(solution)/shard_map/ppermute | solution.py:189
  23.4 1.3 %collective-permute-start.2 = (bf16[2048,128]{1,0:T(8,128)(2,1)S(1)}, bf16[2048,128]{1,0:T(8,128)(2,1)S(1)}, u32[]{:S(2)}, u32[]{:S(2)}) collective-permute-start(bf16[2048,128]{1,0:T(8,128)(2,1)S(1)} %collective-permute-done.1.refs_2_), channel_id=1, source_target_pairs={{4,0},{8,12},{5,1},{9,13},{6,2},{10,14},{7,3},{11,15},{20,16},{24,... | collective-permute-start | bytes 1572872 | tf_op jit(solution)/shard_map/ppermute | solution.py:190
  24.7 9.7 %collective-permute-done.refs_1_ = bf16[2048,128]{1,0:T(8,128)(2,1)S(1)} collective-permute-done((bf16[2048,128]{1,0:T(8,128)(2,1)S(1)}, bf16[2048,128]{1,0:T(8,128)(2,1)S(1)}, u32[]{:S(2)}, u32[]{:S(2)}) %collective-permute-start) | collective-permute-done | bytes 524320 | tf_op jit(solution)/shard_map/ppermute | solution.py:188
  34.4 0.7 %collective-permute-start.3 = (bf16[2048,128]{1,0:T(8,128)(2,1)S(1)}, bf16[2048,128]{1,0:T(8,128)(2,1)S(1)}, u32[]{:S(2)}, u32[]{:S(2)}) collective-permute-start(bf16[2048,128]{1,0:T(8,128)(2,1)S(1)} %collective-permute-done.refs_1_), channel_id=1, source_target_pairs={{4,8},{8,4},{5,9},{9,5},{6,10},{10,6},{7,11},{11,7},{20,24},{24,20... | collective-permute-start | bytes 1572872 | tf_op jit(solution)/shard_map/ppermute | solution.py:191
  35.1 0.0 collective-permute-done.6.far_core_ref
  35.1 0.0 collective-permute-done.4.core_ref
  35.1 0.0 copy-done.4
  35.1 0.0 copy-done.5
  35.1 0.0 copy-done.6
  35.1 0.0 copy-done.7
  35.1 12.1 %time_kernel.1 = (f32[2048,128]{1,0:T(8,128)S(1)}, f32[64,128]{1,0:T(8,128)S(1)}) custom-call(f32[64]{0:T(128)S(1)} %copy-done.4, f32[64]{0:T(128)S(1)} %copy-done.5, f32[64,4096]{1,0:T(8,128)S(1)} %get-tuple-element.12.own_ref, f32[64,4096]{1,0:T(8,128)S(1)} %collective-permute-done.4.core_ref, bf16[64,4096]{1,0:T(8,128)(2,1)S(1)} %collective-permute-done.5.far_ref, ...), custom_call_target="tpu_custom_call" | custom-call | flops 10000000000 | bytes 6291456 | tf_op jit(solution)/shard_map/time_kernel/pallas_call | solution.py:247
  47.2 0.0 copy-done.1
  47.3 0.0 copy-done.2
  47.3 0.0 copy-done.3
  47.3 1.5 %prepare.1 = (f32[2048,128]{1,0:T(8,128)S(1)}, f32[2048,128]{1,0:T(8,128)S(1)}, f32[2048,128]{1,0:T(8,128)S(1)}, f32[2048,128]{1,0:T(8,128)S(1)}) custom-call(bf16[2,32,64,256]{3,2,1,0:T(8,128)(2,1)S(1)} %copy-done.3, f32[2048,128]{1,0:T(8,128)S(1)} %get-tuple-element.14.force_ref, f32[64,128]{1,0:T(8,128)S(1)} %get-tuple-element.15.slope_ref, ...), custom_call_target="tpu_custom_call" | custom-call | flops 1000000000 | bytes 12582912 | tf_op jit(solution)/shard_map/prepare/pallas_call | solution.py:274
  48.7 0.0 collective-permute-done.2.refs_3_
  48.8 0.0 collective-permute-done.3.refs_4_
  48.8 1.9 %couple.1 = (f32[2048,128]{1,0:T(8,128)S(1)}, f32[8,128]{1,0:T(8,128)S(1)}) custom-call(bf16[2,32,64,256]{3,2,1,0:T(8,128)(2,1)S(1)} %copy-done.3, bf16[2048,128]{1,0:T(8,128)(2,1)S(1)} %pack_couple.1.refs_0_, bf16[2048,128]{1,0:T(8,128)(2,1)S(1)} %collective-permute-done.refs_1_, bf16[2048,128]{1,0:T(8,128)(2,1)S(1)} %collective-permute-done.1.refs_2_, ...), custom_call_target="tpu_custom_call" | custom-call | flops 1000000000 | bytes 8388608 | tf_op jit(solution)/shard_map/couple/pallas_call | solution.py:289
  50.7 0.1 collective-permute-start.7
  50.8 1.1 %collective-permute-done.7 = f32[8,128]{1,0:T(8,128)S(1)} collective-permute-done((f32[8,128]{1,0:T(8,128)S(1)}, f32[8,128]{1,0:T(8,128)S(1)}, u32[]{:S(2)}, u32[]{:S(2)}) %collective-permute-start.7) | collective-permute-done | bytes 4128 | tf_op jit(solution)/shard_map/ppermute | solution.py:313
  52.0 0.5 collective-permute-start.8
  52.5 3.1 %collective-permute-done.8 = f32[8,128]{1,0:T(8,128)S(1)} collective-permute-done((f32[8,128]{1,0:T(8,128)S(1)}, f32[8,128]{1,0:T(8,128)S(1)}, u32[]{:S(2)}, u32[]{:S(2)}) %collective-permute-start.8) | collective-permute-done | bytes 4128 | tf_op jit(solution)/shard_map/ppermute | solution.py:313
  55.6 3.8 %collective-permute-start.9 = (f32[8,128]{1,0:T(8,128)S(1)}, f32[8,128]{1,0:T(8,128)S(1)}, u32[]{:S(2)}, u32[]{:S(2)}) collective-permute-start(f32[8,128]{1,0:T(8,128)S(1)} %add.13), channel_id=1, source_target_pairs={{0,4},{4,0},{8,12},{12,8},{1,5},{5,1},{9,13},{13,9},{2,6},{6,2},{1... | collective-permute-start | bytes 12296 | tf_op jit(solution)/shard_map/ppermute | solution.py:316
  59.3 1.6 %collective-permute-done.9 = f32[8,128]{1,0:T(8,128)S(1)} collective-permute-done((f32[8,128]{1,0:T(8,128)S(1)}, f32[8,128]{1,0:T(8,128)S(1)}, u32[]{:S(2)}, u32[]{:S(2)}) %collective-permute-start.9) | collective-permute-done | bytes 4128 | tf_op jit(solution)/shard_map/ppermute | solution.py:316
  60.9 2.6 %collective-permute-start.10 = (f32[8,128]{1,0:T(8,128)S(1)}, f32[8,128]{1,0:T(8,128)S(1)}, u32[]{:S(2)}, u32[]{:S(2)}) collective-permute-start(f32[8,128]{1,0:T(8,128)S(1)} %add.14), channel_id=1, source_target_pairs={{0,8},{4,12},{8,0},{12,4},{1,9},{5,13},{9,1},{13,5},{2,10},{6,14},... | collective-permute-start | bytes 12296 | tf_op jit(solution)/shard_map/ppermute | solution.py:316
  63.6 2.2 %finish.1 = f32[2,2048,64]{2,1,0:T(8,128)} custom-call(f32[2048,128]{1,0:T(8,128)S(1)} %get-tuple-element.17.res_ref, f32[2048,128]{1,0:T(8,128)S(1)} %get-tuple-element.18.p_ref, f32[2048,128]{1,0:T(8,128)S(1)} %get-tuple-element.19.q_ref, f32[2048,128]{1,0:T(8,128)S(1)} %get-tuple-element.20.vel_ref), custom_call_target="tpu_custom_call" | custom-call | bytes 6291456 | tf_op jit(solution)/shard_map/finish/pallas_call | solution.py:301
  65.8 0.0 collective-permute-done.10
  65.8 0.5 slice.3
  (4 shorter events, 0.0 us)
Async XLA Ops:
  0.6 1.6 %copy-start = (f32[2,32,64,64]{3,2,1,0:T(8,128)S(1)}, f32[2,32,64,64]{3,2,1,0:T(8,128)}, u32[]{:S(2)}) copy-start(f32[2,32,64,64]{3,2,1,0:T(8,128)} %param.7) | copy-start | bytes 3145732
  2.2 32.9 %copy-start.4 = (f32[64]{0:T(128)S(1)}, f32[64]{0:T(128)}, u32[]{:S(2)}) copy-start(f32[64]{0:T(128)} %quad_ref.1) | copy-start | bytes 772
  2.2 32.9 %copy-start.5 = (f32[64]{0:T(128)S(1)}, f32[64]{0:T(128)}, u32[]{:S(2)}) copy-start(f32[64]{0:T(128)} %coul_ref.1) | copy-start | bytes 772
  2.2 32.9 %copy-start.6 = (bf16[1024,256]{1,0:T(8,128)(2,1)S(1)}, bf16[1024,256]{1,0:T(8,128)(2,1)}, u32[]{:S(2)}) copy-start(bf16[1024,256]{1,0:T(8,128)(2,1)} %constant.7.clone.fwd_ref) | copy-start | bytes 1572868
  2.2 32.9 %copy-start.7 = (bf16[512,512]{1,0:T(8,128)(2,1)S(1)}, bf16[512,512]{1,0:T(8,128)(2,1)}, u32[]{:S(2)}) copy-start(bf16[512,512]{1,0:T(8,128)(2,1)} %constant.8.clone.inv_ref) | copy-start | bytes 1572868
  3.5 15.0 %collective-permute-start.5 = (bf16[64,4096]{1,0:T(8,128)(2,1)S(1)}, bf16[64,4096]{1,0:T(8,128)(2,1)S(1)}, u32[]{:S(2)}, u32[]{:S(2)}) collective-permute-start(bf16[64,4096]{1,0:T(8,128)(2,1)S(1)} %get-tuple-element.13), channel_id=1, source_target_pairs={{0,2},{1,3},{2,0},{3,1},{4,6},{5,7},{6,4},{7,5},{8,10},{9,11},{10,... | collective-permute-start | bytes 1572872 | tf_op jit(solution)/shard_map/ppermute | solution.py:241
  6.5 28.6 %collective-permute-start.4 = (f32[64,4096]{1,0:T(8,128)S(1)}, f32[64,4096]{1,0:T(8,128)S(1)}, u32[]{:S(2)}, u32[]{:S(2)}) collective-permute-start(f32[64,4096]{1,0:T(8,128)S(1)} %get-tuple-element.12.own_ref), channel_id=1, source_target_pairs={{0,1},{1,0},{2,3},{3,2},{4,5},{5,4},{6,7},{7,6},{8,9},{9,8},{10,11... | collective-permute-start | bytes 3145736 | tf_op jit(solution)/shard_map/ppermute | solution.py:242
  6.7 40.5 %copy-start.1 = (f32[2,32,64,64]{3,2,1,0:T(8,128)S(1)}, f32[2,32,64,64]{3,2,1,0:T(8,128)}, u32[]{:S(2)}) copy-start(f32[2,32,64,64]{3,2,1,0:T(8,128)} %param.7) | copy-start | bytes 3145732
  6.7 40.5 %copy-start.2 = (f32[2,32,64,64]{3,2,1,0:T(8,128)S(1)}, f32[2,32,64,64]{3,2,1,0:T(8,128)}, u32[]{:S(2)}) copy-start(f32[2,32,64,64]{3,2,1,0:T(8,128)} %param.9) | copy-start | bytes 3145732
  6.8 40.5 %copy-start.3 = (bf16[2,32,64,256]{3,2,1,0:T(8,128)(2,1)S(1)}, bf16[2,32,64,256]{3,2,1,0:T(8,128)(2,1)}, u32[]{:S(2)}) copy-start(bf16[2,32,64,256]{3,2,1,0:T(8,128)(2,1)} %imped_ref.3) | copy-start | bytes 6291460
  6.8 16.7 %collective-permute-start.1 = (bf16[2048,128]{1,0:T(8,128)(2,1)S(1)}, bf16[2048,128]{1,0:T(8,128)(2,1)S(1)}, u32[]{:S(2)}, u32[]{:S(2)}) collective-permute-start(bf16[2048,128]{1,0:T(8,128)(2,1)S(1)} %pack_couple.1.refs_0_), channel_id=1, source_target_pairs={{4,8},{8,4},{0,12},{12,0},{5,9},{9,5},{1,13},{13,1},{6,10},{10,6},... | collective-permute-start | bytes 1572872 | tf_op jit(solution)/shard_map/ppermute | solution.py:189
  10.4 23.9 %collective-permute-start = (bf16[2048,128]{1,0:T(8,128)(2,1)S(1)}, bf16[2048,128]{1,0:T(8,128)(2,1)S(1)}, u32[]{:S(2)}, u32[]{:S(2)}) collective-permute-start(bf16[2048,128]{1,0:T(8,128)(2,1)S(1)} %pack_couple.1.refs_0_), channel_id=1, source_target_pairs={{0,4},{4,0},{8,12},{12,8},{1,5},{5,1},{9,13},{13,9},{2,6},{6,2},{1... | collective-permute-start | bytes 1572872 | tf_op jit(solution)/shard_map/ppermute | solution.py:188
  18.4 16.6 %collective-permute-start.6 = (bf16[64,4096]{1,0:T(8,128)(2,1)S(1)}, bf16[64,4096]{1,0:T(8,128)(2,1)S(1)}, u32[]{:S(2)}, u32[]{:S(2)}) collective-permute-start(bf16[64,4096]{1,0:T(8,128)(2,1)S(1)} %collective-permute-done.5.far_ref), channel_id=1, source_target_pairs={{0,1},{1,0},{2,3},{3,2},{4,5},{5,4},{6,7},{7,6},{8,9},{9,8},{10,11... | collective-permute-start | bytes 1572872 | tf_op jit(solution)/shard_map/ppermute | solution.py:243
  23.4 25.3 %collective-permute-start.2 = (bf16[2048,128]{1,0:T(8,128)(2,1)S(1)}, bf16[2048,128]{1,0:T(8,128)(2,1)S(1)}, u32[]{:S(2)}, u32[]{:S(2)}) collective-permute-start(bf16[2048,128]{1,0:T(8,128)(2,1)S(1)} %collective-permute-done.1.refs_2_), channel_id=1, source_target_pairs={{4,0},{8,12},{5,1},{9,13},{6,2},{10,14},{7,3},{11,15},{20,16},{24,... | collective-permute-start | bytes 1572872 | tf_op jit(solution)/shard_map/ppermute | solution.py:190
  34.4 14.4 %collective-permute-start.3 = (bf16[2048,128]{1,0:T(8,128)(2,1)S(1)}, bf16[2048,128]{1,0:T(8,128)(2,1)S(1)}, u32[]{:S(2)}, u32[]{:S(2)}) collective-permute-start(bf16[2048,128]{1,0:T(8,128)(2,1)S(1)} %collective-permute-done.refs_1_), channel_id=1, source_target_pairs={{4,8},{8,4},{5,9},{9,5},{6,10},{10,6},{7,11},{11,7},{20,24},{24,20... | collective-permute-start | bytes 1572872 | tf_op jit(solution)/shard_map/ppermute | solution.py:191
  50.7 1.2 %collective-permute-start.7 = (f32[8,128]{1,0:T(8,128)S(1)}, f32[8,128]{1,0:T(8,128)S(1)}, u32[]{:S(2)}, u32[]{:S(2)}) collective-permute-start(f32[8,128]{1,0:T(8,128)S(1)} %get-tuple-element.21), channel_id=1, source_target_pairs={{0,1},{1,0},{2,3},{3,2},{4,5},{5,4},{6,7},{7,6},{8,9},{9,8},{10,11... | collective-permute-start | bytes 12296 | tf_op jit(solution)/shard_map/ppermute | solution.py:313
  52.0 3.6 %collective-permute-start.8 = (f32[8,128]{1,0:T(8,128)S(1)}, f32[8,128]{1,0:T(8,128)S(1)}, u32[]{:S(2)}, u32[]{:S(2)}) collective-permute-start(f32[8,128]{1,0:T(8,128)S(1)} %add.12), channel_id=1, source_target_pairs={{0,2},{1,3},{2,0},{3,1},{4,6},{5,7},{6,4},{7,5},{8,10},{9,11},{10,... | collective-permute-start | bytes 12296 | tf_op jit(solution)/shard_map/ppermute | solution.py:313
  55.6 5.3 %collective-permute-start.9 = (f32[8,128]{1,0:T(8,128)S(1)}, f32[8,128]{1,0:T(8,128)S(1)}, u32[]{:S(2)}, u32[]{:S(2)}) collective-permute-start(f32[8,128]{1,0:T(8,128)S(1)} %add.13), channel_id=1, source_target_pairs={{0,4},{4,0},{8,12},{12,8},{1,5},{5,1},{9,13},{13,9},{2,6},{6,2},{1... | collective-permute-start | bytes 12296 | tf_op jit(solution)/shard_map/ppermute | solution.py:316
  60.9 4.9 %collective-permute-start.10 = (f32[8,128]{1,0:T(8,128)S(1)}, f32[8,128]{1,0:T(8,128)S(1)}, u32[]{:S(2)}, u32[]{:S(2)}) collective-permute-start(f32[8,128]{1,0:T(8,128)S(1)} %add.14), channel_id=1, source_target_pairs={{0,8},{4,12},{8,0},{12,4},{1,9},{5,13},{9,1},{13,5},{2,10},{6,14},... | collective-permute-start | bytes 12296 | tf_op jit(solution)/shard_map/ppermute | solution.py:316
where the time goes:
time: 68.3 us; the launch traced here: 68.1 us
  waiting for transfers between devices  28.4 us (42%)
  Pallas kernels  19.2 us (28%)
  starting transfers between devices  15.7 us (23%)
  between operations  2.64 us (4%)
  local copies, waits for them, and re-layouts  2.14 us (3%)
    pallas_call x1, Pallas kernels, local(): pl.pallas_call(functools.partial(time_kernel, harm, bodies, reals), grid=...  12.1 us
    ppermute x1, waiting for transfers between devices, gather_line(): near = lax.ppermute(x, axis, [(0, 1), (1, 0), (2, 3), (3, 2)])  9.65 us
    ppermute x1, waiting for transfers between devices, local(): far = lax.ppermute(own_low, 'harm', [(i, i ^ 2) for i in range(4)])  8 us
    ppermute x2, starting transfers between devices, local(): lax.ppermute(total, 'body', [(i, i ^ flip) for i in range(body_count)])  6.4 us
    ppermute x1, waiting for transfers between devices, gather_line(): cross = lax.ppermute(x, axis, [(1, 2), (2, 1), (0, 3), (3, 0)])  4.98 us
    ppermute x2, waiting for transfers between devices, local(): total = total + lax.ppermute(total, axis, [(i, i ^ flip) for i in range(4)])  4.2 us
    ppermute x1, starting transfers between devices, gather_line(): cross = lax.ppermute(x, axis, [(1, 2), (2, 1), (0, 3), (3, 0)])  3.67 us
    ppermute x1, starting transfers between devices, local(): far = lax.ppermute(own_low, 'harm', [(i, i ^ 2) for i in range(4)])  3.03 us
  transfers between devices with their start and end apart: 11, of which 6 were waited for; matrix products, arithmetic and copies ran while one was open for 0% of the time, Pallas kernels for 24%

commit v1 on v0

v1 whole, which is shorter than its diff:
```python
import functools
import math

import ml_dtypes
import numpy as np
import jax
import jax.numpy as jnp
from jax import lax
from jax.experimental import pallas as pl
from jax.experimental.pallas import tpu as pltpu
from jax.sharding import PartitionSpec as P

H = 128
NT = 512
DELTA = 0.1
F32 = jnp.float32
BF16 = jnp.bfloat16
VMEM = pl.BlockSpec(memory_space=pltpu.VMEM)
SMEM = pl.BlockSpec(memory_space=pltpu.SMEM)


def split(x):
    high = x.astype(BF16)
    return high, (x - high.astype(F32)).astype(BF16)


def wave_constants(groups):
    k = np.arange(1, H + 1)
    phase = np.arange(NT)[None, :] * k[:, None] % NT
    angle = phase * (2.0 * math.pi / NT)
    per = H // groups
    waves = np.stack([np.cos(angle), -np.sin(angle)]).reshape(2, groups, per, NT)
    table = np.swapaxes(waves, 0, 1).reshape(2 * H, NT) / math.sqrt(H)
    table = table.astype(np.float32)
    high = table.astype(ml_dtypes.bfloat16)
    low = (table - high.astype(np.float32)).astype(ml_dtypes.bfloat16)
    forward = np.concatenate([high.T, low.T], axis=0)
    size = 2 * per
    inverse = np.stack([high.reshape(groups, size, NT), low.reshape(groups, size, NT)], axis=1).reshape(4 * H, NT)
    return forward, inverse


def pack_couple(harm, bodies, reals, vel_ref, out_ref):
    for h in range(harm):
        rows = pl.ds(h * bodies, bodies)
        re = vel_ref[rows, :]
        im = vel_ref[pl.ds((harm + h) * bodies, bodies), :]
        out_ref[rows, :] = jnp.concatenate([re, im], axis=1).astype(BF16)


def pack_time(harm, bodies, reals, vel_ref, low_ref, own_ref, send_ref, own_low_ref, send_low_ref):
    core = lax.axis_index("harm") % 2
    half = bodies // 2
    pair = bodies // 4
    outs = ((core, own_ref, own_low_ref), (1 - core, send_ref, send_low_ref))
    for which, full, low in outs:
        for j in range(pair):
            one = vel_ref[pl.ds(which * half + j, 2 * harm, stride=bodies), :]
            two = vel_ref[pl.ds(which * half + pair + j, 2 * harm, stride=bodies), :]
            both = jnp.concatenate([one, two], axis=1)
            cols = pl.ds(j * 2 * reals, 2 * reals)
            full[:, cols] = both
            low[:, cols] = both.astype(BF16)


def time_kernel(harm, bodies, reals, quad_ref, coul_ref, own_ref, core_ref, far_ref, far_core_ref, fwd_ref, inv_ref,
                mine_ref, other_ref, high_ref, low_ref):
    step = pl.program_id(0)
    me = lax.axis_index("harm")
    size = 2 * harm
    width = own_ref.shape[1]
    group = 2 * reals
    half = bodies // 2
    pair = bodies // 4
    base = (me % 2) * half

    def rows(index):
        return pl.ds(pl.multiple_of(index * size, size), size)

    @pl.when(step == 0)
    def _():
        low_ref[...] = jnp.zeros_like(low_ref)

    for ref, flip in ((own_ref, 0), (core_ref, 1)):
        high, low = split(ref[...])
        high_ref[rows(me ^ flip), :] = high
        low_ref[rows(me ^ flip), :] = low
    high_ref[rows(me ^ 2), :] = far_ref[...]
    high_ref[rows(me ^ 3), :] = far_core_ref[...]

    both = jnp.dot(fwd_ref[...], high_ref[...], preferred_element_type=F32)
    signal = both[:NT] + both[NT:] + jnp.dot(fwd_ref[:NT, :], low_ref[...], preferred_element_type=F32)

    lane = lax.broadcasted_iota(jnp.int32, (1, group), 1)
    quads, couls = [], []
    for g in range(width // group):
        first = base + step * (width // group) + g
        quads.append(jnp.where(lane < reals, quad_ref[first], quad_ref[first + pair]))
        couls.append(jnp.where(lane < reals, coul_ref[first], coul_ref[first + pair]))
    quad = jnp.concatenate(quads, axis=1)
    coul = jnp.concatenate(couls, axis=1)

    square = signal * signal + DELTA * DELTA
    inverse = lax.rsqrt(square)
    force_time = signal * inverse * (quad * square + coul)
    slope = inverse * ((2.0 * quad) * square - (DELTA * DELTA) * quad + (DELTA * DELTA) * coul * (inverse * inverse))
    mean = jnp.sum(slope, axis=0, keepdims=True) * (1.0 / NT)

    high, low = split(force_time)
    for flip, out_ref in ((0, mine_ref), (1, other_ref)):
        table = inv_ref[pl.ds(pl.multiple_of((me ^ flip) * 2 * size, 2 * size), 2 * size), :]
        back = jnp.dot(table, high, preferred_element_type=F32)
        back = back[:size] + back[size:] + jnp.dot(table[:size], low, preferred_element_type=F32)
        back = back * (2.0 * H / NT)
        for g in range(width // group):
            first = step * (width // group) + g
            re = back[:harm, g * group:(g + 1) * group]
            im = back[harm:, g * group:(g + 1) * group]
            out_ref[pl.ds(first, harm, stride=half), :] = jnp.concatenate([re[:, :reals], im[:, :reals]], axis=1)
            out_ref[pl.ds(first + pair, harm, stride=half), :] = jnp.concatenate([re[:, reals:], im[:, reals:]], axis=1)
            part = mean[:, g * group:(g + 1) * group]
            last = harm * half + first
            out_ref[pl.ds(last, 1), :] = jnp.concatenate([part[:, :reals], part[:, :reals]], axis=1)
            out_ref[pl.ds(last + pair, 1), :] = jnp.concatenate([part[:, reals:], part[:, reals:]], axis=1)


def prepare_kernel(harm, bodies, reals, imped_ref, mine_ref, other_ref, excite_ref, velocity_ref,
                   rest_ref, p_ref, q_ref, vel_ref):
    everyone = imped_ref.shape[3]
    half = bodies // 2
    core = lax.axis_index("harm") % 2
    first = lax.axis_index("body") * bodies
    row = lax.broadcasted_iota(jnp.int32, (bodies, everyone), 0)
    col = lax.broadcasted_iota(jnp.int32, (bodies, everyone), 1)
    mine = col == row + first
    ones = jnp.ones((everyone, 2 * reals), BF16)
    sign = jnp.where(lax.broadcasted_iota(jnp.int32, (bodies, 2 * reals), 1) < reals, 1.0, -1.0)
    lower = core == 0

    def halves(at):
        one = mine_ref[pl.ds(at, half), :]
        two = other_ref[pl.ds(at, half), :]
        return jnp.concatenate([jnp.where(lower, one, two), jnp.where(lower, two, one)], axis=0)

    slope = halves(harm * half)
    for h in range(harm):
        rows = pl.ds(h * bodies, bodies)
        rows_im = pl.ds((harm + h) * bodies, bodies)
        real = jnp.where(mine, imped_ref[0, h], jnp.zeros((), BF16))
        imag = jnp.where(mine, imped_ref[1, h], jnp.zeros((), BF16))
        den = jnp.dot(jnp.concatenate([real, imag], axis=0), ones, preferred_element_type=F32)
        den_re = den[:bodies] + slope
        den_im = den[bodies:]
        inverse = 1.0 / (den_re * den_re + den_im * den_im)
        p_ref[rows, :] = den_re * inverse
        q_ref[rows, :] = den_im * inverse * sign
        rest_ref[rows, :] = halves(h * half) - jnp.concatenate([excite_ref[rows, :], excite_ref[rows_im, :]], axis=1)
        vel_ref[rows, :] = jnp.concatenate([velocity_ref[rows, :], velocity_ref[rows_im, :]], axis=1)


def couple_kernel(harm, bodies, reals, flips, imped_ref, *refs):
    pieces, (rest_ref, res_ref, total_ref, held_ref) = refs[:-4], refs[-4:]
    me = lax.axis_index("body")
    sign = jnp.where(lax.broadcasted_iota(jnp.int32, (bodies, 2 * reals), 1) < reals, -1.0, 1.0)
    total = jnp.zeros((8, 2 * reals), F32)
    ends = jnp.logical_or(me == 0, me == 3)
    for h in range(harm):
        rows = pl.ds(h * bodies, bodies)
        if flips is None:
            vels = pieces[0][:, h].reshape(-1, 2 * reals)
        else:
            slot = h % 4
            for flip, ref in zip(flips, pieces[:-2]):
                held_ref[slot, pl.ds(pl.multiple_of((me ^ flip) * bodies, bodies), bodies), :] = ref[rows, :]
            held_ref[slot, pl.ds(pl.multiple_of((me ^ 2) * bodies, bodies), bodies), :] = jnp.where(
                ends, pieces[-2][rows, :], pieces[-1][rows, :])
            vels = held_ref[slot]
        both = imped_ref[:, h].reshape(2 * bodies, imped_ref.shape[3])
        out = jnp.dot(both, vels, preferred_element_type=F32)
        res = out[:bodies] + sign * pltpu.roll(out[bodies:], reals, 1) + rest_ref[rows, :]
        res_ref[rows, :] = res
        total = total + jnp.sum((res * res).reshape(bodies // 8, 8, 2 * reals), axis=0)
    total_ref[...] = jnp.broadcast_to(jnp.sum(total), total_ref.shape)


def finish_kernel(harm, bodies, reals, res_ref, p_ref, q_ref, vel_ref, out_ref):
    rows = out_ref.shape[1]
    at = pl.ds(pl.multiple_of(pl.program_id(0) * rows, rows), rows)
    res = res_ref[at, :]
    new = vel_ref[at, :] - (res * p_ref[at, :] + pltpu.roll(res, reals, 1) * q_ref[at, :])
    out_ref[0] = new[:, :reals]
    out_ref[1] = new[:, reals:]


def rms_kernel(scale, one_ref, two_ref, out_ref):
    mean = (one_ref[...] + two_ref[...]) * scale
    out_ref[0] = jnp.sqrt(mean)[0, 0]


def gather_line(x, axis):
    near = lax.ppermute(x, axis, [(0, 1), (1, 0), (2, 3), (3, 2)])
    cross = lax.ppermute(x, axis, [(1, 2), (2, 1), (0, 3), (3, 0)])
    outer = lax.ppermute(cross, axis, [(1, 0), (2, 3)])
    inner = lax.ppermute(near, axis, [(1, 2), (2, 1)])
    return x, near, cross, outer, inner


def params(mib=24):
    return pltpu.CompilerParams(vmem_limit_bytes=mib << 20)


def cost(flops, moved):
    return pl.CostEstimate(flops=flops, bytes_accessed=moved, transcendentals=0)


def make_local(mesh):
    body_count = mesh.shape["body"]

    def local(vel, imped, excite, quad_coef, coul_coef):
        _, harm, bodies, reals = vel.shape
        everyone = imped.shape[3]
        group = 2 * reals
        total_rows = harm * bodies
        forward, inverse = wave_constants(H // harm)
        flat = vel.reshape(2 * total_rows, reals)
        flat_excite = excite.reshape(2 * total_rows, reals)
        dense = jax.ShapeDtypeStruct((total_rows, group), F32)

        low = pl.pallas_call(
            functools.partial(pack_couple, harm, bodies, reals),
            out_shape=jax.ShapeDtypeStruct((total_rows, group), BF16),
            compiler_params=params(),
            cost_estimate=cost(0, 3 << 20),
            name="pack_couple",
        )(flat)
        if body_count == 4:
            pieces = gather_line(low, "body")
            flips = (0, 1, 3)
        else:
            pieces = (lax.all_gather(low, "body").reshape(body_count, harm, bodies, group),)
            flips = None

        columns = bodies * reals // 2
        packed = jax.ShapeDtypeStruct((2 * harm, columns), F32)
        packed_low = jax.ShapeDtypeStruct((2 * harm, columns), BF16)
        own, send, own_low, send_low = pl.pallas_call(
            functools.partial(pack_time, harm, bodies, reals),
            in_specs=[VMEM, pl.BlockSpec(memory_space=pl.ANY)],
            out_shape=(packed, packed, packed_low, packed_low),
            compiler_params=params(),
            cost_estimate=cost(0, 4 << 20),
            name="pack_time",
        )(flat, low)

        def flipped(x, flip):
            return lax.ppermute(x, "harm", [(i, i ^ flip) for i in range(4)])

        far = flipped(own_low, 2)
        far_core = flipped(send_low, 3)
        core = flipped(send, 1)

        width = 4 * group
        tile = pl.BlockSpec((2 * harm, width), lambda i: (0, i))
        half_rows = (harm + 1) * bodies // 2
        half_spec = pl.BlockSpec((half_rows, group), lambda i: (0, 0))
        half_shape = jax.ShapeDtypeStruct((half_rows, group), F32)
        mine, other = pl.pallas_call(
            functools.partial(time_kernel, harm, bodies, reals),
            grid=(columns // width,),
            in_specs=[SMEM, SMEM, tile, tile, tile, tile, VMEM, VMEM],
            out_specs=[half_spec, half_spec],
            out_shape=(half_shape, half_shape),
            scratch_shapes=[pltpu.VMEM((2 * H, width), BF16), pltpu.VMEM((2 * H, width), BF16)],
            compiler_params=params(),
            cost_estimate=cost(5 * 10**9, 4 << 20),
            name="time_kernel",
        )(quad_coef, coul_coef, own, core, far, far_core, jnp.asarray(forward), jnp.asarray(inverse))
        other = flipped(other, 1)

        rest, factor_p, factor_q, vel_dense = pl.pallas_call(
            functools.partial(prepare_kernel, harm, bodies, reals),
            in_specs=[VMEM] * 5,
            out_shape=(dense,) * 4,
            compiler_params=params(),
            cost_estimate=cost(10**9, 4 << 20),
            name="prepare",
        )(imped, mine, other, flat_excite, flat)

        res, total = pl.pallas_call(
            functools.partial(couple_kernel, harm, bodies, reals, flips),
            in_specs=[VMEM] * (2 + len(pieces)),
            out_shape=(dense, jax.ShapeDtypeStruct((8, 128), F32)),
            scratch_shapes=[pltpu.VMEM((4, everyone, group), BF16)],
            compiler_params=params(),
            cost_estimate=cost(10**9, 4 << 20),
            name="couple",
        )(imped, *pieces, rest)

        steps = 8
        rows = total_rows // steps
        new = pl.pallas_call(
            functools.partial(finish_kernel, harm, bodies, reals),
            grid=(steps,),
            in_specs=[VMEM] * 4,
            out_specs=pl.BlockSpec((2, rows, reals), lambda i: (0, i, 0)),
            out_shape=jax.ShapeDtypeStruct((2, total_rows, reals), F32),
            compiler_params=params(),
            cost_estimate=cost(0, 6 << 20),
            name="finish",
        )(res, factor_p, factor_q, vel_dense)

        got = flipped(total, 1)
        total = total + got
        got = flipped(total, 2)
        flip = 1
        while flip < body_count:
            total = total + got
            got = lax.ppermute(total, "body", [(i, i ^ flip) for i in range(body_count)])
            flip *= 2
        rms = pl.pallas_call(
            functools.partial(rms_kernel, 1.0 / (2.0 * H * everyone * reals)),
            in_specs=[VMEM] * 2,
            out_specs=SMEM,
            out_shape=jax.ShapeDtypeStruct((1,), F32),
            name="rms",
        )(total, got)
        return new.reshape(vel.shape), rms

    return local


def solution(mesh):
    in_specs = (
        P(None, "harm", "body", "sea"),
        P(None, "harm", "body", None),
        P(None, "harm", "body", "sea"),
        P("body"),
        P("body"),
    )
    out_specs = (P(None, "harm", "body", "sea"), P("sea"))
    return jax.shard_map(make_local(mesh), mesh=mesh, in_specs=in_specs, out_specs=out_specs, check_vma=False)
```

time: 68.3 us -> 66.9 us (0.980)
  Pallas kernels: 19.2 us -> 15.4 us
  waiting for transfers between devices: 28.4 us -> 30.5 us
  starting transfers between devices: 15.7 us -> 17.7 us
  between operations: 2.64 us -> 0.8 us
    ppermute x1, waiting for transfers between devices: 0.01 us -> 10.9 us  [gather_line(): outer = lax.ppermute(cross, axis, [(1, 0), (2, 3)])]
    ppermute x1, waiting for transfers between devices: 4.98 us -> 0.01 us  [gather_line(): cross = lax.ppermute(x, axis, [(1, 2), (2, 1), (0, 3), (3, 0)])]
    pallas_call x1, Pallas kernels: 12.1 us -> 7.16 us  [local(): pl.pallas_call(functools.partial(time_kernel, harm, bodies, reals), grid=...]
    ppermute x1, waiting for transfers between devices: 9.65 us -> 6.41 us  [gather_line(): near = lax.ppermute(x, axis, [(0, 1), (1, 0), (2, 3), (3, 2)])]
    ppermute x5 -> x6, starting transfers between devices: 3.68 us -> 5.24 us  [flipped(): return lax.ppermute(x, 'harm', [(i, i ^ flip) for i in range(4)])]
    pallas_call x4 -> x5, Pallas kernels: 6.86 us -> 8.05 us  [the longest x1 3.68 us: local(): pl.pallas_call(functools.partial(finish_kernel, harm, bodies, reals), gri...]
    unnamed x16 -> x20, local copies, waits for them, and re-layouts: 1.62 us -> 2.22 us
    ppermute x5 -> x6, waiting for transfers between devices: 12.2 us -> 11.6 us  [flipped(): return lax.ppermute(x, 'harm', [(i, i ^ flip) for i in range(4)])]
  transfers between devices with their start and end apart: 11 -> 12, of which waited for: 6 -> 7; matrix products, arithmetic and copies ran while one was open for 0% -> 0% of each run, Pallas kernels for 24% -> 18%
where the time goes in v1:
time: 66.9 us; the launch traced here: 66.7 us
  waiting for transfers between devices  30.5 us (46%)
  starting transfers between devices  17.7 us (26%)
  Pallas kernels  15.4 us (23%)
  local copies, waits for them, and re-layouts  2.22 us (3%)
  between operations  0.8 us (1%)
    ppermute x6, waiting for transfers between devices, flipped(): return lax.ppermute(x, 'harm', [(i, i ^ flip) for i in range(4)])  11.6 us
    ppermute x1, waiting for transfers between devices, gather_line(): outer = lax.ppermute(cross, axis, [(1, 0), (2, 3)])  10.9 us
    pallas_call x1, Pallas kernels, local(): pl.pallas_call(functools.partial(time_kernel, harm, bodies, reals), grid=...  7.16 us
    ppermute x2, starting transfers between devices, local(): lax.ppermute(total, 'body', [(i, i ^ flip) for i in range(body_count)])  6.73 us
    ppermute x1, waiting for transfers between devices, gather_line(): near = lax.ppermute(x, axis, [(0, 1), (1, 0), (2, 3), (3, 2)])  6.41 us
    ppermute x6, starting transfers between devices, flipped(): return lax.ppermute(x, 'harm', [(i, i ^ flip) for i in range(4)])  5.24 us
    ppermute x1, starting transfers between devices, gather_line(): cross = lax.ppermute(x, axis, [(1, 2), (2, 1), (0, 3), (3, 0)])  3.81 us
    pallas_call x1, Pallas kernels, local(): pl.pallas_call(functools.partial(finish_kernel, harm, bodies, reals), gri...  3.68 us
  transfers between devices with their start and end apart: 12, of which 7 were waited for; matrix products, arithmetic and copies ran while one was open for 0% of the time, Pallas kernels for 18%

profile of v1, /device:TPU:0, one launch (start us, length us, event | category | flops | bytes accessed | tf_op | source)
XLA Modules:
  0.0 66.7 jit_solution(10023988772691572345)
XLA Ops:
  0.6 0.0 copy-start
  0.6 1.6 %copy-done = f32[2,32,64,64]{3,2,1,0:T(8,128)S(1)} copy-done((f32[2,32,64,64]{3,2,1,0:T(8,128)S(1)}, f32[2,32,64,64]{3,2,1,0:T(8,128)}, u32[]{:S(2)}) %copy-start) | copy-done | bytes 1048600
  2.2 0.0 copy-start.4
  2.2 0.0 copy-start.5
  2.2 0.0 copy-start.6
  2.2 0.2 pack_couple.1.low_ref.refs_0_
  2.4 1.3 %pack_time.1 = (f32[64,2048]{1,0:T(8,128)S(1)}, f32[64,2048]{1,0:T(8,128)S(1)}, bf16[64,2048]{1,0:T(8,128)(2,1)S(1)}, bf16[64,2048]{1,0:T(8,128)(2,1)S(1)}) custom-call(f32[4096,64]{1,0:T(8,128)S(1)} %bitcast.4, bf16[2048,128]{1,0:T(8,128)(2,1)S(1)} %pack_couple.1.low_ref.refs_0_), custom_call_target="tpu_custom_call" | custom-call | bytes 4194304 | tf_op jit(solution)/shard_map/pack_time/pallas_call | solution.py:246
  3.7 0.5 collective-permute-start.4
  4.2 2.6 %collective-permute-start.5 = (bf16[64,2048]{1,0:T(8,128)(2,1)S(1)}, bf16[64,2048]{1,0:T(8,128)(2,1)S(1)}, u32[]{:S(2)}, u32[]{:S(2)}) collective-permute-start(bf16[64,2048]{1,0:T(8,128)(2,1)S(1)} %get-tuple-element.16), channel_id=1, source_target_pairs={{0,2},{1,3},{2,0},{3,1},{4,6},{5,7},{6,4},{7,5},{8,10},{9,11},{10,... | collective-permute-start | bytes 786440 | tf_op jit(solution)/shard_map/ppermute | solution.py:256
  6.8 0.1 collective-permute-start.6
  6.9 3.8 %collective-permute-start.1 = (bf16[2048,128]{1,0:T(8,128)(2,1)S(1)}, bf16[2048,128]{1,0:T(8,128)(2,1)S(1)}, u32[]{:S(2)}, u32[]{:S(2)}) collective-permute-start(bf16[2048,128]{1,0:T(8,128)(2,1)S(1)} %pack_couple.1.low_ref.refs_0_), channel_id=1, source_target_pairs={{4,8},{8,4},{0,12},{12,0},{5,9},{9,5},{1,13},{13,1},{6,10},{10,6},... | collective-permute-start | bytes 1572872 | tf_op jit(solution)/shard_map/ppermute | solution.py:202
  10.7 0.0 collective-permute-start
  10.7 3.3 %collective-permute-done.5.far_ref = bf16[64,2048]{1,0:T(8,128)(2,1)S(1)} collective-permute-done((bf16[64,2048]{1,0:T(8,128)(2,1)S(1)}, bf16[64,2048]{1,0:T(8,128)(2,1)S(1)}, u32[]{:S(2)}, u32[]{:S(2)}) %collective-permute-start.5) | collective-permute-done | bytes 262176 | tf_op jit(solution)/shard_map/ppermute | solution.py:256
  14.0 5.1 %collective-permute-done.6.far_core_ref = bf16[64,2048]{1,0:T(8,128)(2,1)S(1)} collective-permute-done((bf16[64,2048]{1,0:T(8,128)(2,1)S(1)}, bf16[64,2048]{1,0:T(8,128)(2,1)S(1)}, u32[]{:S(2)}, u32[]{:S(2)}) %collective-permute-start.6) | collective-permute-done | bytes 262176 | tf_op jit(solution)/shard_map/ppermute | solution.py:256
  19.1 0.0 collective-permute-done.4.core_ref
  19.1 0.0 copy-done.4
  19.1 0.0 copy-done.5
  19.1 0.0 copy-done.6
  19.1 0.0 copy-done.7
  19.1 0.0 copy-start.1
  19.1 0.0 copy-start.2
  19.1 0.0 copy-start.3
  19.1 7.2 %time_kernel.1 = (f32[1056,128]{1,0:T(8,128)S(1)}, f32[1056,128]{1,0:T(8,128)S(1)}) custom-call(f32[64]{0:T(128)S(1)} %copy-done.4, f32[64]{0:T(128)S(1)} %copy-done.5, f32[64,2048]{1,0:T(8,128)S(1)} %get-tuple-element.14.own_ref, f32[64,2048]{1,0:T(8,128)S(1)} %collective-permute-done.4.core_ref, bf16[64,2048]{1,0:T(8,128)(2,1)S(1)} %collective-permute-done.5.far_ref, ...), custom_call_target="tpu_custom_call" | custom-call | flops 5000000000 | bytes 4194304 | tf_op jit(solution)/shard_map/time_kernel/pallas_call | solution.py:267
  26.3 0.5 collective-permute-start.7
  26.8 0.0 collective-permute-done.1.refs_2_
  26.8 1.3 %collective-permute-start.2 = (bf16[2048,128]{1,0:T(8,128)(2,1)S(1)}, bf16[2048,128]{1,0:T(8,128)(2,1)S(1)}, u32[]{:S(2)}, u32[]{:S(2)}) collective-permute-start(bf16[2048,128]{1,0:T(8,128)(2,1)S(1)} %collective-permute-done.1.refs_2_), channel_id=1, source_target_pairs={{4,0},{8,12},{5,1},{9,13},{6,2},{10,14},{7,3},{11,15},{20,16},{24,... | collective-permute-start | bytes 1572872 | tf_op jit(solution)/shard_map/ppermute | solution.py:203
  28.1 6.4 %collective-permute-done.refs_1_ = bf16[2048,128]{1,0:T(8,128)(2,1)S(1)} collective-permute-done((bf16[2048,128]{1,0:T(8,128)(2,1)S(1)}, bf16[2048,128]{1,0:T(8,128)(2,1)S(1)}, u32[]{:S(2)}, u32[]{:S(2)}) %collective-permute-start) | collective-permute-done | bytes 524320 | tf_op jit(solution)/shard_map/ppermute | solution.py:201
  34.5 0.7 %collective-permute-start.3 = (bf16[2048,128]{1,0:T(8,128)(2,1)S(1)}, bf16[2048,128]{1,0:T(8,128)(2,1)S(1)}, u32[]{:S(2)}, u32[]{:S(2)}) collective-permute-start(bf16[2048,128]{1,0:T(8,128)(2,1)S(1)} %collective-permute-done.refs_1_), channel_id=1, source_target_pairs={{4,8},{8,4},{5,9},{9,5},{6,10},{10,6},{7,11},{11,7},{20,24},{24,20... | collective-permute-start | bytes 1572872 | tf_op jit(solution)/shard_map/ppermute | solution.py:204
  35.2 0.0 collective-permute-done.7.other_ref
  35.2 0.0 copy-done.1
  35.2 0.0 copy-done.2
  35.2 0.0 copy-done.3
  35.2 0.9 %prepare.1 = (f32[2048,128]{1,0:T(8,128)S(1)}, f32[2048,128]{1,0:T(8,128)S(1)}, f32[2048,128]{1,0:T(8,128)S(1)}, f32[2048,128]{1,0:T(8,128)S(1)}) custom-call(bf16[2,32,64,256]{3,2,1,0:T(8,128)(2,1)S(1)} %copy-done.2, f32[1056,128]{1,0:T(8,128)S(1)} %get-tuple-element.18.mine_ref, f32[1056,128]{1,0:T(8,128)S(1)} %collective-permute-done.7.other_ref, ...), custom_call_target="tpu_custom_call" | custom-call | flops 1000000000 | bytes 4194304 | tf_op jit(solution)/shard_map/prepare/pallas_call | solution.py:280
  36.1 10.9 %collective-permute-done.2.refs_3_ = bf16[2048,128]{1,0:T(8,128)(2,1)S(1)} collective-permute-done((bf16[2048,128]{1,0:T(8,128)(2,1)S(1)}, bf16[2048,128]{1,0:T(8,128)(2,1)S(1)}, u32[]{:S(2)}, u32[]{:S(2)}) %collective-permute-start.2) | collective-permute-done | bytes 524320 | tf_op jit(solution)/shard_map/ppermute | solution.py:203
  47.0 0.0 collective-permute-done.3.refs_4_
  47.0 1.0 %couple.1 = (f32[2048,128]{1,0:T(8,128)S(1)}, f32[8,128]{1,0:T(8,128)S(1)}) custom-call(bf16[2,32,64,256]{3,2,1,0:T(8,128)(2,1)S(1)} %copy-done.2, bf16[2048,128]{1,0:T(8,128)(2,1)S(1)} %pack_couple.1.low_ref.refs_0_, bf16[2048,128]{1,0:T(8,128)(2,1)S(1)} %collective-permute-done.refs_1_, bf16[2048,128]{1,0:T(8,128)(2,1)S(1)} %collective-permute-done.1.refs_2_, ...), custom_call_target="tpu_custom_call" | custom-call | flops 1000000000 | bytes 4194304 | tf_op jit(solution)/shard_map/couple/pallas_call | solution.py:289
  48.0 0.1 collective-permute-start.8
  48.1 1.2 %collective-permute-done.8 = f32[8,128]{1,0:T(8,128)S(1)} collective-permute-done((f32[8,128]{1,0:T(8,128)S(1)}, f32[8,128]{1,0:T(8,128)S(1)}, u32[]{:S(2)}, u32[]{:S(2)}) %collective-permute-start.8) | collective-permute-done | bytes 4128 | tf_op jit(solution)/shard_map/ppermute | solution.py:256
  49.2 1.5 %collective-permute-start.9 = (f32[8,128]{1,0:T(8,128)S(1)}, f32[8,128]{1,0:T(8,128)S(1)}, u32[]{:S(2)}, u32[]{:S(2)}) collective-permute-start(f32[8,128]{1,0:T(8,128)S(1)} %add.9), channel_id=1, source_target_pairs={{0,2},{1,3},{2,0},{3,1},{4,6},{5,7},{6,4},{7,5},{8,10},{9,11},{10,... | collective-permute-start | bytes 12296 | tf_op jit(solution)/shard_map/ppermute | solution.py:256
  50.8 2.1 %collective-permute-done.9 = f32[8,128]{1,0:T(8,128)S(1)} collective-permute-done((f32[8,128]{1,0:T(8,128)S(1)}, f32[8,128]{1,0:T(8,128)S(1)}, u32[]{:S(2)}, u32[]{:S(2)}) %collective-permute-start.9) | collective-permute-done | bytes 4128 | tf_op jit(solution)/shard_map/ppermute | solution.py:256
  52.9 4.4 %collective-permute-start.10 = (f32[8,128]{1,0:T(8,128)S(1)}, f32[8,128]{1,0:T(8,128)S(1)}, u32[]{:S(2)}, u32[]{:S(2)}) collective-permute-start(f32[8,128]{1,0:T(8,128)S(1)} %add.10), channel_id=1, source_target_pairs={{0,4},{4,0},{8,12},{12,8},{1,5},{5,1},{9,13},{13,9},{2,6},{6,2},{1... | collective-permute-start | bytes 12296 | tf_op jit(solution)/shard_map/ppermute | solution.py:318
  57.3 1.6 %collective-permute-done.10 = f32[8,128]{1,0:T(8,128)S(1)} collective-permute-done((f32[8,128]{1,0:T(8,128)S(1)}, f32[8,128]{1,0:T(8,128)S(1)}, u32[]{:S(2)}, u32[]{:S(2)}) %collective-permute-start.10) | collective-permute-done | bytes 4128 | tf_op jit(solution)/shard_map/ppermute | solution.py:318
  58.9 2.3 %collective-permute-start.11 = (f32[8,128]{1,0:T(8,128)S(1)}, f32[8,128]{1,0:T(8,128)S(1)}, u32[]{:S(2)}, u32[]{:S(2)}) collective-permute-start(f32[8,128]{1,0:T(8,128)S(1)} %add.11.one_ref), channel_id=1, source_target_pairs={{0,8},{4,12},{8,0},{12,4},{1,9},{5,13},{9,1},{13,5},{2,10},{6,14},... | collective-permute-start | bytes 12296 | tf_op jit(solution)/shard_map/ppermute | solution.py:318
  61.2 3.7 %finish.1 = f32[2,2048,64]{2,1,0:T(8,128)} custom-call(f32[2048,128]{1,0:T(8,128)S(1)} %get-tuple-element.21.res_ref, f32[2048,128]{1,0:T(8,128)S(1)} %get-tuple-element.22.p_ref, f32[2048,128]{1,0:T(8,128)S(1)} %get-tuple-element.23.q_ref, f32[2048,128]{1,0:T(8,128)S(1)} %get-tuple-element.24.vel_ref), custom_call_target="tpu_custom_call" | custom-call | bytes 6291456 | tf_op jit(solution)/shard_map/finish/pallas_call | solution.py:301
  64.8 0.0 copy-done.8
  64.8 0.0 collective-permute-done.11.two_ref
  64.9 0.6 copy-done.9
  65.4 1.2 %rms.1 = f32[1]{0:T(128)} custom-call(f32[8,128]{1,0:T(8,128)} %copy-done.8, f32[8,128]{1,0:T(8,128)} %copy-done.9), custom_call_target="tpu_custom_call" | custom-call | tf_op jit(solution)/shard_map/rms/pallas_call | solution.py:320
  (6 shorter events, 0.0 us)
Async XLA Ops:
  0.6 1.6 %copy-start = (f32[2,32,64,64]{3,2,1,0:T(8,128)S(1)}, f32[2,32,64,64]{3,2,1,0:T(8,128)}, u32[]{:S(2)}) copy-start(f32[2,32,64,64]{3,2,1,0:T(8,128)} %param.7) | copy-start | bytes 3145732
  2.2 16.9 %copy-start.4 = (f32[64]{0:T(128)S(1)}, f32[64]{0:T(128)}, u32[]{:S(2)}) copy-start(f32[64]{0:T(128)} %quad_ref.1) | copy-start | bytes 772
  2.2 16.9 %copy-start.5 = (f32[64]{0:T(128)S(1)}, f32[64]{0:T(128)}, u32[]{:S(2)}) copy-start(f32[64]{0:T(128)} %coul_ref.1) | copy-start | bytes 772
  2.2 16.9 %copy-start.6 = (bf16[1024,256]{1,0:T(8,128)(2,1)S(1)}, bf16[1024,256]{1,0:T(8,128)(2,1)}, u32[]{:S(2)}) copy-start(bf16[1024,256]{1,0:T(8,128)(2,1)} %constant.4.clone.fwd_ref) | copy-start | bytes 1572868
  2.2 16.9 %copy-start.7 = (bf16[512,512]{1,0:T(8,128)(2,1)S(1)}, bf16[512,512]{1,0:T(8,128)(2,1)}, u32[]{:S(2)}) copy-start(bf16[512,512]{1,0:T(8,128)(2,1)} %constant.5.clone.inv_ref) | copy-start | bytes 1572868
  3.7 15.4 %collective-permute-start.4 = (f32[64,2048]{1,0:T(8,128)S(1)}, f32[64,2048]{1,0:T(8,128)S(1)}, u32[]{:S(2)}, u32[]{:S(2)}) collective-permute-start(f32[64,2048]{1,0:T(8,128)S(1)} %get-tuple-element.15), channel_id=1, source_target_pairs={{0,1},{1,0},{2,3},{3,2},{4,5},{5,4},{6,7},{7,6},{8,9},{9,8},{10,11... | collective-permute-start | bytes 1572872 | tf_op jit(solution)/shard_map/ppermute | solution.py:256
  4.2 9.8 %collective-permute-start.5 = (bf16[64,2048]{1,0:T(8,128)(2,1)S(1)}, bf16[64,2048]{1,0:T(8,128)(2,1)S(1)}, u32[]{:S(2)}, u32[]{:S(2)}) collective-permute-start(bf16[64,2048]{1,0:T(8,128)(2,1)S(1)} %get-tuple-element.16), channel_id=1, source_target_pairs={{0,2},{1,3},{2,0},{3,1},{4,6},{5,7},{6,4},{7,5},{8,10},{9,11},{10,... | collective-permute-start | bytes 786440 | tf_op jit(solution)/shard_map/ppermute | solution.py:256
  6.8 12.3 %collective-permute-start.6 = (bf16[64,2048]{1,0:T(8,128)(2,1)S(1)}, bf16[64,2048]{1,0:T(8,128)(2,1)S(1)}, u32[]{:S(2)}, u32[]{:S(2)}) collective-permute-start(bf16[64,2048]{1,0:T(8,128)(2,1)S(1)} %get-tuple-element.17), channel_id=1, source_target_pairs={{0,3},{1,2},{2,1},{3,0},{4,7},{5,6},{6,5},{7,4},{8,11},{9,10},{10,... | collective-permute-start | bytes 786440 | tf_op jit(solution)/shard_map/ppermute | solution.py:256
  6.9 19.9 %collective-permute-start.1 = (bf16[2048,128]{1,0:T(8,128)(2,1)S(1)}, bf16[2048,128]{1,0:T(8,128)(2,1)S(1)}, u32[]{:S(2)}, u32[]{:S(2)}) collective-permute-start(bf16[2048,128]{1,0:T(8,128)(2,1)S(1)} %pack_couple.1.low_ref.refs_0_), channel_id=1, source_target_pairs={{4,8},{8,4},{0,12},{12,0},{5,9},{9,5},{1,13},{13,1},{6,10},{10,6},... | collective-permute-start | bytes 1572872 | tf_op jit(solution)/shard_map/ppermute | solution.py:202
  10.7 23.8 %collective-permute-start = (bf16[2048,128]{1,0:T(8,128)(2,1)S(1)}, bf16[2048,128]{1,0:T(8,128)(2,1)S(1)}, u32[]{:S(2)}, u32[]{:S(2)}) collective-permute-start(bf16[2048,128]{1,0:T(8,128)(2,1)S(1)} %pack_couple.1.low_ref.refs_0_), channel_id=1, source_target_pairs={{0,4},{4,0},{8,12},{12,8},{1,5},{5,1},{9,13},{13,9},{2,6},{6,2},{1... | collective-permute-start | bytes 1572872 | tf_op jit(solution)/shard_map/ppermute | solution.py:201
  19.1 16.1 %copy-start.1 = (f32[2,32,64,64]{3,2,1,0:T(8,128)S(1)}, f32[2,32,64,64]{3,2,1,0:T(8,128)}, u32[]{:S(2)}) copy-start(f32[2,32,64,64]{3,2,1,0:T(8,128)} %param.7) | copy-start | bytes 3145732
  19.1 16.1 %copy-start.2 = (bf16[2,32,64,256]{3,2,1,0:T(8,128)(2,1)S(1)}, bf16[2,32,64,256]{3,2,1,0:T(8,128)(2,1)}, u32[]{:S(2)}) copy-start(bf16[2,32,64,256]{3,2,1,0:T(8,128)(2,1)} %imped_ref.3) | copy-start | bytes 6291460
  19.1 16.1 %copy-start.3 = (f32[2,32,64,64]{3,2,1,0:T(8,128)S(1)}, f32[2,32,64,64]{3,2,1,0:T(8,128)}, u32[]{:S(2)}) copy-start(f32[2,32,64,64]{3,2,1,0:T(8,128)} %param.9) | copy-start | bytes 3145732
  26.3 8.9 %collective-permute-start.7 = (f32[1056,128]{1,0:T(8,128)S(1)}, f32[1056,128]{1,0:T(8,128)S(1)}, u32[]{:S(2)}, u32[]{:S(2)}) collective-permute-start(f32[1056,128]{1,0:T(8,128)S(1)} %get-tuple-element.19), channel_id=1, source_target_pairs={{0,1},{1,0},{2,3},{3,2},{4,5},{5,4},{6,7},{7,6},{8,9},{9,8},{10,11... | collective-permute-start | bytes 1622024 | tf_op jit(solution)/shard_map/ppermute | solution.py:256
  26.8 20.2 %collective-permute-start.2 = (bf16[2048,128]{1,0:T(8,128)(2,1)S(1)}, bf16[2048,128]{1,0:T(8,128)(2,1)S(1)}, u32[]{:S(2)}, u32[]{:S(2)}) collective-permute-start(bf16[2048,128]{1,0:T(8,128)(2,1)S(1)} %collective-permute-done.1.refs_2_), channel_id=1, source_target_pairs={{4,0},{8,12},{5,1},{9,13},{6,2},{10,14},{7,3},{11,15},{20,16},{24,... | collective-permute-start | bytes 1572872 | tf_op jit(solution)/shard_map/ppermute | solution.py:203
  34.5 12.5 %collective-permute-start.3 = (bf16[2048,128]{1,0:T(8,128)(2,1)S(1)}, bf16[2048,128]{1,0:T(8,128)(2,1)S(1)}, u32[]{:S(2)}, u32[]{:S(2)}) collective-permute-start(bf16[2048,128]{1,0:T(8,128)(2,1)S(1)} %collective-permute-done.refs_1_), channel_id=1, source_target_pairs={{4,8},{8,4},{5,9},{9,5},{6,10},{10,6},{7,11},{11,7},{20,24},{24,20... | collective-permute-start | bytes 1572872 | tf_op jit(solution)/shard_map/ppermute | solution.py:204
  48.0 1.2 %collective-permute-start.8 = (f32[8,128]{1,0:T(8,128)S(1)}, f32[8,128]{1,0:T(8,128)S(1)}, u32[]{:S(2)}, u32[]{:S(2)}) collective-permute-start(f32[8,128]{1,0:T(8,128)S(1)} %get-tuple-element.25), channel_id=1, source_target_pairs={{0,1},{1,0},{2,3},{3,2},{4,5},{5,4},{6,7},{7,6},{8,9},{9,8},{10,11... | collective-permute-start | bytes 12296 | tf_op jit(solution)/shard_map/ppermute | solution.py:256
  49.2 3.6 %collective-permute-start.9 = (f32[8,128]{1,0:T(8,128)S(1)}, f32[8,128]{1,0:T(8,128)S(1)}, u32[]{:S(2)}, u32[]{:S(2)}) collective-permute-start(f32[8,128]{1,0:T(8,128)S(1)} %add.9), channel_id=1, source_target_pairs={{0,2},{1,3},{2,0},{3,1},{4,6},{5,7},{6,4},{7,5},{8,10},{9,11},{10,... | collective-permute-start | bytes 12296 | tf_op jit(solution)/shard_map/ppermute | solution.py:256
  52.9 6.0 %collective-permute-start.10 = (f32[8,128]{1,0:T(8,128)S(1)}, f32[8,128]{1,0:T(8,128)S(1)}, u32[]{:S(2)}, u32[]{:S(2)}) collective-permute-start(f32[8,128]{1,0:T(8,128)S(1)} %add.10), channel_id=1, source_target_pairs={{0,4},{4,0},{8,12},{12,8},{1,5},{5,1},{9,13},{13,9},{2,6},{6,2},{1... | collective-permute-start | bytes 12296 | tf_op jit(solution)/shard_map/ppermute | solution.py:318
  58.9 6.0 %copy-start.8 = (f32[8,128]{1,0:T(8,128)}, f32[8,128]{1,0:T(8,128)S(1)}, u32[]{:S(2)}) copy-start(f32[8,128]{1,0:T(8,128)S(1)} %add.11.one_ref) | copy-start | bytes 12292
  58.9 6.0 %collective-permute-start.11 = (f32[8,128]{1,0:T(8,128)S(1)}, f32[8,128]{1,0:T(8,128)S(1)}, u32[]{:S(2)}, u32[]{:S(2)}) collective-permute-start(f32[8,128]{1,0:T(8,128)S(1)} %add.11.one_ref), channel_id=1, source_target_pairs={{0,8},{4,12},{8,0},{12,4},{1,9},{5,13},{9,1},{13,5},{2,10},{6,14},... | collective-permute-start | bytes 12296 | tf_op jit(solution)/shard_map/ppermute | solution.py:318
  64.9 0.6 copy-start.9

commit v2 on v1

v2 whole, which is shorter than its diff:
```python
import functools
import math

import ml_dtypes
import numpy as np
import jax
import jax.numpy as jnp
from jax import lax
from jax.experimental import pallas as pl
from jax.experimental.pallas import tpu as pltpu
from jax.sharding import PartitionSpec as P

H = 128
NT = 512
DELTA = 0.1
F32 = jnp.float32
BF16 = jnp.bfloat16
VMEM = pl.BlockSpec(memory_space=pltpu.VMEM)
SMEM = pl.BlockSpec(memory_space=pltpu.SMEM)


def split(x):
    high = x.astype(BF16)
    return high, (x - high.astype(F32)).astype(BF16)


def wave_constants(groups):
    k = np.arange(1, H + 1)
    phase = np.arange(NT)[None, :] * k[:, None] % NT
    angle = phase * (2.0 * math.pi / NT)
    waves = np.stack([np.cos(angle), -np.sin(angle)]).reshape(2, groups, H // groups, NT)
    table = (np.swapaxes(waves, 0, 1).reshape(2 * H, NT) / math.sqrt(H)).astype(np.float32)
    high = table.astype(ml_dtypes.bfloat16)
    low = (table - high.astype(np.float32)).astype(ml_dtypes.bfloat16)
    return np.concatenate([high.T, low.T], axis=1), np.concatenate([high, low, high], axis=1)


def pack_couple(harm, bodies, reals, vel_ref, out_ref):
    for h in range(harm):
        rows = pl.ds(h * bodies, bodies)
        re = vel_ref[rows, :]
        im = vel_ref[pl.ds((harm + h) * bodies, bodies), :]
        out_ref[rows, :] = jnp.concatenate([re, im], axis=1).astype(BF16)


def pack_time(harm, bodies, reals, vel_ref, own_ref, send_ref):
    core = lax.axis_index("harm") % 2
    half = bodies // 2
    pair = bodies // 4
    for which, out_ref in ((core, own_ref), (1 - core, send_ref)):
        for j in range(pair):
            one = vel_ref[pl.ds(which * half + j, 2 * harm, stride=bodies), :]
            two = vel_ref[pl.ds(which * half + pair + j, 2 * harm, stride=bodies), :]
            out_ref[:, pl.ds(j * 2 * reals, 2 * reals)] = jnp.concatenate([one, two], axis=1).astype(BF16)


def time_kernel(harm, bodies, reals, quad_ref, coul_ref, own_ref, core_ref, far_ref, far_core_ref, fwd_ref, inv_ref,
                mine_ref, other_ref, held_ref, force_ref):
    step = pl.program_id(0)
    me = lax.axis_index("harm")
    core = me % 2
    size = 2 * harm
    width = own_ref.shape[1]
    group = 2 * reals
    pair = bodies // 4
    base = core * (bodies // 2) + step * (width // group)
    small = DELTA * DELTA

    for flip, ref in enumerate((own_ref, core_ref, far_ref, far_core_ref)):
        value = ref[...]
        first = pl.multiple_of((me ^ flip) * size, size)
        held_ref[pl.ds(first, size), :] = value
        held_ref[pl.ds(first + 2 * H, size), :] = value

    lane = lax.broadcasted_iota(jnp.int32, (1, group), 1)
    quads, couls = [], []
    for g in range(width // group):
        quads.append(jnp.where(lane < reals, quad_ref[base + g], quad_ref[base + g + pair]))
        couls.append(jnp.where(lane < reals, coul_ref[base + g], coul_ref[base + g + pair]))
    quad = jnp.concatenate(quads, axis=1)
    coul = jnp.concatenate(couls, axis=1)

    signal = jnp.dot(fwd_ref[...], held_ref[...], preferred_element_type=F32)
    square = signal * signal + small
    inverse = lax.rsqrt(square)
    root = square * inverse
    high, low = split(signal * (quad * root + coul * inverse))
    force_ref[:NT] = high
    force_ref[NT:2 * NT] = high
    force_ref[2 * NT:] = low
    roots = jnp.sum(root, axis=0, keepdims=True)
    inverses = jnp.sum(inverse, axis=0, keepdims=True)
    cubes = jnp.sum(inverse * inverse * inverse, axis=0, keepdims=True)
    mean = (quad * (2.0 * roots - small * inverses) + coul * (small * cubes)) * (1.0 / NT)

    first = pl.multiple_of((me // 2) * 2 * size, 2 * size)
    back = jnp.dot(inv_ref[pl.ds(first, 2 * size), :], force_ref[...], preferred_element_type=F32) * (2.0 * H / NT)
    lower = core == 0
    mine_ref[:size] = jnp.where(lower, back[:size], back[size:])
    other_ref[:size] = jnp.where(lower, back[size:], back[:size])
    slope = jnp.broadcast_to(mean, (8, width))
    mine_ref[size:] = slope
    other_ref[size:] = slope


def prepare_kernel(harm, bodies, reals, imped_ref, mine_ref, other_ref, excite_ref, velocity_ref,
                   rest_ref, p_ref, q_ref, vel_ref, slope_ref):
    everyone = imped_ref.shape[3]
    group = 2 * reals
    half = bodies // 2
    pair = bodies // 4
    core = lax.axis_index("harm") % 2
    for which, ref in ((core, mine_ref), (1 - core, other_ref)):
        for j in range(pair):
            cols = slice(j * group, (j + 1) * group)
            re = ref[:harm, cols]
            im = ref[harm:2 * harm, cols]
            slope = ref[2 * harm:2 * harm + 1, cols]
            one = which * half + j
            two = one + pair
            rest_ref[pl.ds(one, harm, stride=bodies), :] = jnp.concatenate([re[:, :reals], im[:, :reals]], axis=1)
            rest_ref[pl.ds(two, harm, stride=bodies), :] = jnp.concatenate([re[:, reals:], im[:, reals:]], axis=1)
            slope_ref[pl.ds(one, 1), :] = jnp.concatenate([slope[:, :reals], slope[:, :reals]], axis=1)
            slope_ref[pl.ds(two, 1), :] = jnp.concatenate([slope[:, reals:], slope[:, reals:]], axis=1)

    first = lax.axis_index("body") * bodies
    row = lax.broadcasted_iota(jnp.int32, (bodies, everyone), 0)
    col = lax.broadcasted_iota(jnp.int32, (bodies, everyone), 1)
    mine = col == row + first
    ones = jnp.ones((everyone, group), BF16)
    sign = jnp.where(lax.broadcasted_iota(jnp.int32, (bodies, group), 1) < reals, 1.0, -1.0)
    slope = slope_ref[...]
    for h in range(harm):
        rows = pl.ds(h * bodies, bodies)
        rows_im = pl.ds((harm + h) * bodies, bodies)
        real = jnp.where(mine, imped_ref[0, h], jnp.zeros((), BF16))
        imag = jnp.where(mine, imped_ref[1, h], jnp.zeros((), BF16))
        den = jnp.dot(jnp.concatenate([real, imag], axis=0), ones, preferred_element_type=F32)
        den_re = den[:bodies] + slope
        den_im = den[bodies:]
        inverse = 1.0 / (den_re * den_re + den_im * den_im)
        p_ref[rows, :] = den_re * inverse
        q_ref[rows, :] = den_im * inverse * sign
        vel = jnp.concatenate([velocity_ref[rows, :], velocity_ref[rows_im, :]], axis=1)
        vel_ref[rows, :] = vel
        excite = jnp.concatenate([excite_ref[rows, :], excite_ref[rows_im, :]], axis=1)
        rest_ref[rows, :] = rest_ref[rows, :] - excite + slope * (vel - vel.astype(BF16).astype(F32))


def couple_kernel(harm, bodies, reals, flips, imped_ref, *refs):
    pieces, (rest_ref, res_ref, total_ref, held_ref) = refs[:-4], refs[-4:]
    me = lax.axis_index("body")
    sign = jnp.where(lax.broadcasted_iota(jnp.int32, (bodies, 2 * reals), 1) < reals, -1.0, 1.0)
    total = jnp.zeros((8, 2 * reals), F32)
    ends = jnp.logical_or(me == 0, me == 3)
    for h in range(harm):
        rows = pl.ds(h * bodies, bodies)
        if flips is None:
            vels = pieces[0][:, h].reshape(-1, 2 * reals)
        else:
            slot = h % 4
            for flip, ref in zip(flips, pieces[:-2]):
                held_ref[slot, pl.ds(pl.multiple_of((me ^ flip) * bodies, bodies), bodies), :] = ref[rows, :]
            held_ref[slot, pl.ds(pl.multiple_of((me ^ 2) * bodies, bodies), bodies), :] = jnp.where(
                ends, pieces[-1][rows, :], pieces[-2][rows, :])
            vels = held_ref[slot]
        both = imped_ref[:, h].reshape(2 * bodies, imped_ref.shape[3])
        out = jnp.dot(both, vels, preferred_element_type=F32)
        res = out[:bodies] + sign * pltpu.roll(out[bodies:], reals, 1) + rest_ref[rows, :]
        res_ref[rows, :] = res
        total = total + jnp.sum((res * res).reshape(bodies // 8, 8, 2 * reals), axis=0)
    total_ref[...] = jnp.broadcast_to(jnp.sum(total), total_ref.shape)


def finish_kernel(harm, bodies, reals, res_ref, p_ref, q_ref, vel_ref, out_ref):
    rows = out_ref.shape[1]
    at = pl.ds(pl.multiple_of(pl.program_id(0) * rows, rows), rows)
    res = res_ref[at, :]
    new = vel_ref[at, :] - (res * p_ref[at, :] + pltpu.roll(res, reals, 1) * q_ref[at, :])
    out_ref[0] = new[:, :reals]
    out_ref[1] = new[:, reals:]


def rms_kernel(scale, one_ref, two_ref, out_ref):
    mean = (one_ref[...] + two_ref[...]) * scale
    out_ref[0] = jnp.sqrt(mean)[0, 0]


def gather_line(x, axis):
    near = lax.ppermute(x, axis, [(0, 1), (1, 0), (2, 3), (3, 2)])
    cross = lax.ppermute(x, axis, [(1, 2), (2, 1), (0, 3), (3, 0)])
    inner = lax.ppermute(near, axis, [(1, 2), (2, 1)])
    outer = lax.ppermute(cross, axis, [(1, 0), (2, 3)])
    return x, near, cross, inner, outer


def params(mib=24):
    return pltpu.CompilerParams(vmem_limit_bytes=mib << 20)


def cost(flops, moved):
    return pl.CostEstimate(flops=flops, bytes_accessed=moved, transcendentals=0)


def make_local(mesh):
    body_count = mesh.shape["body"]

    def local(vel, imped, excite, quad_coef, coul_coef):
        _, harm, bodies, reals = vel.shape
        everyone = imped.shape[3]
        group = 2 * reals
        total_rows = harm * bodies
        forward, inverse = wave_constants(H // harm)
        flat = vel.reshape(2 * total_rows, reals)
        flat_excite = excite.reshape(2 * total_rows, reals)
        dense = jax.ShapeDtypeStruct((total_rows, group), F32)

        def flipped(x, flip):
            return lax.ppermute(x, "harm", [(i, i ^ flip) for i in range(4)])

        low = pl.pallas_call(
            functools.partial(pack_couple, harm, bodies, reals),
            out_shape=jax.ShapeDtypeStruct((total_rows, group), BF16),
            compiler_params=params(),
            cost_estimate=cost(0, 1 << 10),
            name="pack_couple",
        )(flat)
        if body_count == 4:
            pieces = gather_line(low, "body")
            flips = (0, 1, 3)
        else:
            pieces = (lax.all_gather(low, "body").reshape(body_count, harm, bodies, group),)
            flips = None

        columns = bodies * reals // 2
        own, send = pl.pallas_call(
            functools.partial(pack_time, harm, bodies, reals),
            in_specs=[VMEM],
            out_shape=(jax.ShapeDtypeStruct((2 * harm, columns), BF16),) * 2,
            compiler_params=params(),
            cost_estimate=cost(0, 1 << 10),
            name="pack_time",
        )(flat)
        far = flipped(own, 2)
        far_core = flipped(send, 3)
        core = flipped(send, 1)

        width = 8 * group
        tile = pl.BlockSpec((2 * harm, width), lambda i: (0, i))
        half_spec = pl.BlockSpec((2 * harm + 8, width), lambda i: (0, i))
        half_shape = jax.ShapeDtypeStruct((2 * harm + 8, columns), F32)
        mine, other = pl.pallas_call(
            functools.partial(time_kernel, harm, bodies, reals),
            grid=(columns // width,),
            in_specs=[SMEM, SMEM, tile, tile, tile, tile, VMEM, VMEM],
            out_specs=[half_spec, half_spec],
            out_shape=(half_shape, half_shape),
            scratch_shapes=[pltpu.VMEM((4 * H, width), BF16), pltpu.VMEM((3 * NT, width), BF16)],
            compiler_params=params(),
            cost_estimate=cost(0, 1 << 10),
            name="time_kernel",
        )(quad_coef, coul_coef, own, core, far, far_core, jnp.asarray(forward), jnp.asarray(inverse))
        other = flipped(other, 1)

        rest, factor_p, factor_q, vel_dense = pl.pallas_call(
            functools.partial(prepare_kernel, harm, bodies, reals),
            in_specs=[VMEM] * 5,
            out_shape=(dense,) * 4,
            scratch_shapes=[pltpu.VMEM((bodies, group), F32)],
            compiler_params=params(),
            cost_estimate=cost(0, 1 << 10),
            name="prepare",
        )(imped, mine, other, flat_excite, flat)

        res, total = pl.pallas_call(
            functools.partial(couple_kernel, harm, bodies, reals, flips),
            in_specs=[VMEM] * (2 + len(pieces)),
            out_shape=(dense, jax.ShapeDtypeStruct((8, 128), F32)),
            scratch_shapes=[pltpu.VMEM((4, everyone, group), BF16)],
            compiler_params=params(),
            cost_estimate=cost(0, 1 << 10),
            name="couple",
        )(imped, *pieces, rest)

        steps = 2
        rows = total_rows // steps
        new = pl.pallas_call(
            functools.partial(finish_kernel, harm, bodies, reals),
            grid=(steps,),
            in_specs=[VMEM] * 4,
            out_specs=pl.BlockSpec((2, rows, reals), lambda i: (0, i, 0)),
            out_shape=jax.ShapeDtypeStruct((2, total_rows, reals), F32),
            compiler_params=params(),
            cost_estimate=cost(0, 1 << 10),
            name="finish",
        )(res, factor_p, factor_q, vel_dense)

        got = flipped(total, 1)
        total = total + got
        got = flipped(total, 2)
        flip = 1
        while flip < body_count:
            total = total + got
            got = lax.ppermute(total, "body", [(i, i ^ flip) for i in range(body_count)])
            flip *= 2
        rms = pl.pallas_call(
            functools.partial(rms_kernel, 1.0 / (2.0 * H * everyone * reals)),
            in_specs=[VMEM] * 2,
            out_specs=SMEM,
            out_shape=jax.ShapeDtypeStruct((1,), F32),
            compiler_params=params(),
            name="rms",
        )(total, got)
        return new.reshape(vel.shape), rms

    return local


def solution(mesh):
    in_specs = (
        P(None, "harm", "body", "sea"),
        P(None, "harm", "body", None),
        P(None, "harm", "body", "sea"),
        P("body"),
        P("body"),
    )
    out_specs = (P(None, "harm", "body", "sea"), P("sea"))
    return jax.shard_map(make_local(mesh), mesh=mesh, in_specs=in_specs, out_specs=out_specs, check_vma=False)
```

time: 66.9 us -> 60.9 us (0.910)
  starting transfers between devices: 17.7 us -> 12.4 us
  Pallas kernels: 15.4 us -> 11 us
  waiting for transfers between devices: 30.5 us -> 33.8 us
    ppermute x1, waiting for transfers between devices: 6.41 us -> 0.01 us  [gather_line(): near = lax.ppermute(x, axis, [(0, 1), (1, 0), (2, 3), (3, 2)])]
    ppermute x2, starting transfers between devices: 6.73 us -> 0.7 us  [local(): lax.ppermute(total, 'body', [(i, i ^ flip) for i in range(body_count)])]
    ppermute x2, waiting for transfers between devices: 1.59 us -> 5.76 us  [local(): lax.ppermute(total, 'body', [(i, i ^ flip) for i in range(body_count)])]
    ppermute x6, waiting for transfers between devices: 11.6 us -> 15.3 us  [flipped(): return lax.ppermute(x, 'harm', [(i, i ^ flip) for i in range(4)])]
    ppermute x1, starting transfers between devices: 0.01 us -> 3.09 us  [gather_line(): near = lax.ppermute(x, axis, [(0, 1), (1, 0), (2, 3), (3, 2)])]
    pallas_call x1, Pallas kernels: 7.16 us -> 4.75 us  [local(): pl.pallas_call(functools.partial(time_kernel, harm, bodies, reals), grid=...]
    pallas_call x1, Pallas kernels: 3.68 us -> 1.66 us  [local(): pl.pallas_call(functools.partial(finish_kernel, harm, bodies, reals), gri...]
    ppermute x1, starting transfers between devices: 3.81 us -> 2.47 us  [gather_line(): cross = lax.ppermute(x, axis, [(1, 2), (2, 1), (0, 3), (3, 0)])]
  transfers between devices with their start and end apart: 12 -> 12, of which waited for: 7 -> 8; matrix products, arithmetic and copies ran while one was open for 0% -> 0% of each run, Pallas kernels for 18% -> 15%
where the time goes in v2:
time: 60.9 us; the launch traced here: 60.7 us
  waiting for transfers between devices  33.8 us (56%)
  starting transfers between devices  12.4 us (20%)
  Pallas kernels  11 us (18%)
  local copies, waits for them, and re-layouts  2.66 us (4%)
  between operations  0.8 us (1%)
    ppermute x6, waiting for transfers between devices, flipped(): return lax.ppermute(x, 'harm', [(i, i ^ flip) for i in range(4)])  15.3 us
    ppermute x1, waiting for transfers between devices, gather_line(): outer = lax.ppermute(cross, axis, [(1, 0), (2, 3)])  12.1 us
    ppermute x2, waiting for transfers between devices, local(): lax.ppermute(total, 'body', [(i, i ^ flip) for i in range(body_count)])  5.76 us
    pallas_call x1, Pallas kernels, local(): pl.pallas_call(functools.partial(time_kernel, harm, bodies, reals), grid=...  4.75 us
    ppermute x6, starting transfers between devices, flipped(): return lax.ppermute(x, 'harm', [(i, i ^ flip) for i in range(4)])  4.16 us
    ppermute x1, starting transfers between devices, gather_line(): near = lax.ppermute(x, axis, [(0, 1), (1, 0), (2, 3), (3, 2)])  3.09 us
    unnamed x16, local copies, waits for them, and re-layouts  2.66 us
    ppermute x1, starting transfers between devices, gather_line(): cross = lax.ppermute(x, axis, [(1, 2), (2, 1), (0, 3), (3, 0)])  2.47 us
  transfers between devices with their start and end apart: 12, of which 8 were waited for; matrix products, arithmetic and copies ran while one was open for 0% of the time, Pallas kernels for 15%

profile of v2, /device:TPU:0, one launch (start us, length us, event | category | flops | bytes accessed | tf_op | source)
XLA Modules:
  0.0 60.7 jit_solution(4129511142849019664)
XLA Ops:
  0.6 0.0 copy-start.6
  0.6 0.0 copy-start.7
  0.7 0.0 copy-start
  0.7 1.6 %copy-done = f32[2,32,64,64]{3,2,1,0:T(8,128)S(1)} copy-done((f32[2,32,64,64]{3,2,1,0:T(8,128)S(1)}, f32[2,32,64,64]{3,2,1,0:T(8,128)}, u32[]{:S(2)}) %copy-start) | copy-done | bytes 1048600
  2.3 0.0 copy-start.4
  2.3 0.0 copy-start.3
  2.3 0.2 pack_couple.1.refs_0_
  2.5 0.0 copy-start.1
  2.5 0.0 copy-start.2
  2.5 3.1 %collective-permute-start = (bf16[2048,128]{1,0:T(8,128)(2,1)S(1)}, bf16[2048,128]{1,0:T(8,128)(2,1)S(1)}, u32[]{:S(2)}, u32[]{:S(2)}) collective-permute-start(bf16[2048,128]{1,0:T(8,128)(2,1)S(1)} %pack_couple.1.refs_0_), channel_id=1, source_target_pairs={{0,4},{4,0},{8,12},{12,8},{1,5},{5,1},{9,13},{13,9},{2,6},{6,2},{1... | collective-permute-start | bytes 1572872 | tf_op jit(solution)/shard_map/ppermute | solution.py:190
  5.6 2.5 %collective-permute-start.1 = (bf16[2048,128]{1,0:T(8,128)(2,1)S(1)}, bf16[2048,128]{1,0:T(8,128)(2,1)S(1)}, u32[]{:S(2)}, u32[]{:S(2)}) collective-permute-start(bf16[2048,128]{1,0:T(8,128)(2,1)S(1)} %pack_couple.1.refs_0_), channel_id=1, source_target_pairs={{4,8},{8,4},{0,12},{12,0},{5,9},{9,5},{1,13},{13,1},{6,10},{10,6},... | collective-permute-start | bytes 1572872 | tf_op jit(solution)/shard_map/ppermute | solution.py:191
  8.1 1.2 %pack_time.1 = (bf16[64,2048]{1,0:T(8,128)(2,1)S(1)}, bf16[64,2048]{1,0:T(8,128)(2,1)S(1)}) custom-call(f32[4096,64]{1,0:T(8,128)S(1)} %bitcast.4), custom_call_target="tpu_custom_call" | custom-call | bytes 1024 | tf_op jit(solution)/shard_map/pack_time/pallas_call | solution.py:236
  9.2 0.1 collective-permute-start.4
  9.3 1.6 %collective-permute-start.5 = (bf16[64,2048]{1,0:T(8,128)(2,1)S(1)}, bf16[64,2048]{1,0:T(8,128)(2,1)S(1)}, u32[]{:S(2)}, u32[]{:S(2)}) collective-permute-start(bf16[64,2048]{1,0:T(8,128)(2,1)S(1)} %get-tuple-element.12.own_ref), channel_id=1, source_target_pairs={{0,2},{1,3},{2,0},{3,1},{4,6},{5,7},{6,4},{7,5},{8,10},{9,11},{10,... | collective-permute-start | bytes 786440 | tf_op jit(solution)/shard_map/ppermute | solution.py:219
  10.9 0.3 collective-permute-start.6
  11.2 0.0 collective-permute-done.4.core_ref
  11.2 7.3 %collective-permute-done.5.far_ref = bf16[64,2048]{1,0:T(8,128)(2,1)S(1)} collective-permute-done((bf16[64,2048]{1,0:T(8,128)(2,1)S(1)}, bf16[64,2048]{1,0:T(8,128)(2,1)S(1)}, u32[]{:S(2)}, u32[]{:S(2)}) %collective-permute-start.5) | collective-permute-done | bytes 262176 | tf_op jit(solution)/shard_map/ppermute | solution.py:219
  18.5 4.7 %collective-permute-done.6.far_core_ref = bf16[64,2048]{1,0:T(8,128)(2,1)S(1)} collective-permute-done((bf16[64,2048]{1,0:T(8,128)(2,1)S(1)}, bf16[64,2048]{1,0:T(8,128)(2,1)S(1)}, u32[]{:S(2)}, u32[]{:S(2)}) %collective-permute-start.6) | collective-permute-done | bytes 262176 | tf_op jit(solution)/shard_map/ppermute | solution.py:219
  23.2 0.0 copy-done.6
  23.2 0.0 copy-done.7
  23.2 0.0 copy-done.4
  23.2 0.0 copy-start.5
  23.2 1.0 %copy-done.5 = bf16[512,512]{1,0:T(8,128)(2,1)S(1)} copy-done((bf16[512,512]{1,0:T(8,128)(2,1)S(1)}, bf16[512,512]{1,0:T(8,128)(2,1)}, u32[]{:S(2)}) %copy-start.5) | copy-done | bytes 524312
  24.3 4.8 %time_kernel.1 = (f32[72,2048]{1,0:T(8,128)S(1)}, f32[72,2048]{1,0:T(8,128)S(1)}) custom-call(f32[64]{0:T(128)S(1)} %copy-done.6, f32[64]{0:T(128)S(1)} %copy-done.7, bf16[64,2048]{1,0:T(8,128)(2,1)S(1)} %get-tuple-element.12.own_ref, bf16[64,2048]{1,0:T(8,128)(2,1)S(1)} %collective-permute-done.4.core_ref, ...), custom_call_target="tpu_custom_call" | custom-call | bytes 1024 | tf_op jit(solution)/shard_map/time_kernel/pallas_call | solution.py:252
  29.0 0.6 %collective-permute-start.7 = (f32[72,2048]{1,0:T(8,128)S(1)}, f32[72,2048]{1,0:T(8,128)S(1)}, u32[]{:S(2)}, u32[]{:S(2)}) collective-permute-start(f32[72,2048]{1,0:T(8,128)S(1)} %get-tuple-element.15), channel_id=1, source_target_pairs={{0,1},{1,0},{2,3},{3,2},{4,5},{5,4},{6,7},{7,6},{8,9},{9,8},{10,11... | collective-permute-start | bytes 1769480 | tf_op jit(solution)/shard_map/ppermute | solution.py:219
  29.7 0.0 collective-permute-done.refs_1_
  29.7 0.7 %collective-permute-start.2 = (bf16[2048,128]{1,0:T(8,128)(2,1)S(1)}, bf16[2048,128]{1,0:T(8,128)(2,1)S(1)}, u32[]{:S(2)}, u32[]{:S(2)}) collective-permute-start(bf16[2048,128]{1,0:T(8,128)(2,1)S(1)} %collective-permute-done.refs_1_), channel_id=1, source_target_pairs={{4,8},{8,4},{5,9},{9,5},{6,10},{10,6},{7,11},{11,7},{20,24},{24,20... | collective-permute-start | bytes 1572872 | tf_op jit(solution)/shard_map/ppermute | solution.py:192
  30.3 0.7 %collective-permute-done.1.refs_2_ = bf16[2048,128]{1,0:T(8,128)(2,1)S(1)} collective-permute-done((bf16[2048,128]{1,0:T(8,128)(2,1)S(1)}, bf16[2048,128]{1,0:T(8,128)(2,1)S(1)}, u32[]{:S(2)}, u32[]{:S(2)}) %collective-permute-start.1) | collective-permute-done | bytes 524320 | tf_op jit(solution)/shard_map/ppermute | solution.py:191
  31.0 1.3 %collective-permute-start.3 = (bf16[2048,128]{1,0:T(8,128)(2,1)S(1)}, bf16[2048,128]{1,0:T(8,128)(2,1)S(1)}, u32[]{:S(2)}, u32[]{:S(2)}) collective-permute-start(bf16[2048,128]{1,0:T(8,128)(2,1)S(1)} %collective-permute-done.1.refs_2_), channel_id=1, source_target_pairs={{4,0},{8,12},{5,1},{9,13},{6,2},{10,14},{7,3},{11,15},{20,16},{24,... | collective-permute-start | bytes 1572872 | tf_op jit(solution)/shard_map/ppermute | solution.py:193
  32.3 0.0 collective-permute-done.7.other_ref
  32.3 0.0 copy-done.3
  32.3 0.0 copy-done.1
  32.4 0.0 copy-done.2
  32.4 1.6 %prepare.1 = (f32[2048,128]{1,0:T(8,128)S(1)}, f32[2048,128]{1,0:T(8,128)S(1)}, f32[2048,128]{1,0:T(8,128)S(1)}, f32[2048,128]{1,0:T(8,128)S(1)}) custom-call(bf16[2,32,64,256]{3,2,1,0:T(8,128)(2,1)S(1)} %copy-done.2, f32[72,2048]{1,0:T(8,128)S(1)} %get-tuple-element.14.mine_ref, f32[72,2048]{1,0:T(8,128)S(1)} %collective-permute-done.7.other_ref, ...), custom_call_target="tpu_custom_call" | custom-call | bytes 1024 | tf_op jit(solution)/shard_map/prepare/pallas_call | solution.py:265
  34.0 0.0 collective-permute-done.2.refs_3_
  34.0 12.1 %collective-permute-done.3.refs_4_ = bf16[2048,128]{1,0:T(8,128)(2,1)S(1)} collective-permute-done((bf16[2048,128]{1,0:T(8,128)(2,1)S(1)}, bf16[2048,128]{1,0:T(8,128)(2,1)S(1)}, u32[]{:S(2)}, u32[]{:S(2)}) %collective-permute-start.3) | collective-permute-done | bytes 524320 | tf_op jit(solution)/shard_map/ppermute | solution.py:193
  46.1 1.0 %couple.1 = (f32[2048,128]{1,0:T(8,128)S(1)}, f32[8,128]{1,0:T(8,128)S(1)}) custom-call(bf16[2,32,64,256]{3,2,1,0:T(8,128)(2,1)S(1)} %copy-done.2, bf16[2048,128]{1,0:T(8,128)(2,1)S(1)} %pack_couple.1.refs_0_, bf16[2048,128]{1,0:T(8,128)(2,1)S(1)} %collective-permute-done.refs_1_, bf16[2048,128]{1,0:T(8,128)(2,1)S(1)} %collective-permute-done.1.refs_2_, ...), custom_call_target="tpu_custom_call" | custom-call | bytes 1024 | tf_op jit(solution)/shard_map/couple/pallas_call | solution.py:275
  47.1 0.1 collective-permute-start.8
  47.2 1.2 %collective-permute-done.8 = f32[8,128]{1,0:T(8,128)S(1)} collective-permute-done((f32[8,128]{1,0:T(8,128)S(1)}, f32[8,128]{1,0:T(8,128)S(1)}, u32[]{:S(2)}, u32[]{:S(2)}) %collective-permute-start.8) | collective-permute-done | bytes 4128 | tf_op jit(solution)/shard_map/ppermute | solution.py:219
  48.4 1.5 %collective-permute-start.9 = (f32[8,128]{1,0:T(8,128)S(1)}, f32[8,128]{1,0:T(8,128)S(1)}, u32[]{:S(2)}, u32[]{:S(2)}) collective-permute-start(f32[8,128]{1,0:T(8,128)S(1)} %add.9), channel_id=1, source_target_pairs={{0,2},{1,3},{2,0},{3,1},{4,6},{5,7},{6,4},{7,5},{8,10},{9,11},{10,... | collective-permute-start | bytes 12296 | tf_op jit(solution)/shard_map/ppermute | solution.py:219
  49.9 2.1 %collective-permute-done.9 = f32[8,128]{1,0:T(8,128)S(1)} collective-permute-done((f32[8,128]{1,0:T(8,128)S(1)}, f32[8,128]{1,0:T(8,128)S(1)}, u32[]{:S(2)}, u32[]{:S(2)}) %collective-permute-start.9) | collective-permute-done | bytes 4128 | tf_op jit(solution)/shard_map/ppermute | solution.py:219
  52.0 0.0 collective-permute-start.10
  52.0 3.6 %collective-permute-done.10 = f32[8,128]{1,0:T(8,128)S(1)} collective-permute-done((f32[8,128]{1,0:T(8,128)S(1)}, f32[8,128]{1,0:T(8,128)S(1)}, u32[]{:S(2)}, u32[]{:S(2)}) %collective-permute-start.10) | collective-permute-done | bytes 4128 | tf_op jit(solution)/shard_map/ppermute | solution.py:304
  55.6 0.7 %collective-permute-start.11 = (f32[8,128]{1,0:T(8,128)S(1)}, f32[8,128]{1,0:T(8,128)S(1)}, u32[]{:S(2)}, u32[]{:S(2)}) collective-permute-start(f32[8,128]{1,0:T(8,128)S(1)} %add.11.one_ref), channel_id=1, source_target_pairs={{0,8},{4,12},{8,0},{12,4},{1,9},{5,13},{9,1},{13,5},{2,10},{6,14},... | collective-permute-start | bytes 12296 | tf_op jit(solution)/shard_map/ppermute | solution.py:304
  56.3 1.7 %finish.1 = f32[2,2048,64]{2,1,0:T(8,128)} custom-call(f32[2048,128]{1,0:T(8,128)S(1)} %get-tuple-element.17.res_ref, f32[2048,128]{1,0:T(8,128)S(1)} %get-tuple-element.18.p_ref, f32[2048,128]{1,0:T(8,128)S(1)} %get-tuple-element.19.q_ref, f32[2048,128]{1,0:T(8,128)S(1)} %get-tuple-element.20.vel_ref), custom_call_target="tpu_custom_call" | custom-call | bytes 1024 | tf_op jit(solution)/shard_map/finish/pallas_call | solution.py:287
  58.0 2.2 %collective-permute-done.11.two_ref = f32[8,128]{1,0:T(8,128)S(1)} collective-permute-done((f32[8,128]{1,0:T(8,128)S(1)}, f32[8,128]{1,0:T(8,128)S(1)}, u32[]{:S(2)}, u32[]{:S(2)}) %collective-permute-start.11) | collective-permute-done | bytes 4128 | tf_op jit(solution)/shard_map/ppermute | solution.py:304
  60.1 0.6 rms.1
  (3 shorter events, 0.0 us)
Async XLA Ops:
  0.6 22.6 %copy-start.6 = (f32[64]{0:T(128)S(1)}, f32[64]{0:T(128)}, u32[]{:S(2)}) copy-start(f32[64]{0:T(128)} %quad_ref.1) | copy-start | bytes 772
  0.6 22.6 %copy-start.7 = (f32[64]{0:T(128)S(1)}, f32[64]{0:T(128)}, u32[]{:S(2)}) copy-start(f32[64]{0:T(128)} %coul_ref.1) | copy-start | bytes 772
  0.7 1.6 %copy-start = (f32[2,32,64,64]{3,2,1,0:T(8,128)S(1)}, f32[2,32,64,64]{3,2,1,0:T(8,128)}, u32[]{:S(2)}) copy-start(f32[2,32,64,64]{3,2,1,0:T(8,128)} %param.7) | copy-start | bytes 3145732
  2.3 21.0 %copy-start.4 = (bf16[256,1536]{1,0:T(8,128)(2,1)S(1)}, bf16[256,1536]{1,0:T(8,128)(2,1)}, u32[]{:S(2)}) copy-start(bf16[256,1536]{1,0:T(8,128)(2,1)} %constant.5.clone.inv_ref) | copy-start | bytes 2359300
  2.3 30.1 %copy-start.3 = (f32[2,32,64,64]{3,2,1,0:T(8,128)S(1)}, f32[2,32,64,64]{3,2,1,0:T(8,128)}, u32[]{:S(2)}) copy-start(f32[2,32,64,64]{3,2,1,0:T(8,128)} %param.9) | copy-start | bytes 3145732
  2.5 29.9 %copy-start.1 = (f32[2,32,64,64]{3,2,1,0:T(8,128)S(1)}, f32[2,32,64,64]{3,2,1,0:T(8,128)}, u32[]{:S(2)}) copy-start(f32[2,32,64,64]{3,2,1,0:T(8,128)} %param.7) | copy-start | bytes 3145732
  2.5 29.9 %copy-start.2 = (bf16[2,32,64,256]{3,2,1,0:T(8,128)(2,1)S(1)}, bf16[2,32,64,256]{3,2,1,0:T(8,128)(2,1)}, u32[]{:S(2)}) copy-start(bf16[2,32,64,256]{3,2,1,0:T(8,128)(2,1)} %imped_ref.3) | copy-start | bytes 6291460
  2.5 27.2 %collective-permute-start = (bf16[2048,128]{1,0:T(8,128)(2,1)S(1)}, bf16[2048,128]{1,0:T(8,128)(2,1)S(1)}, u32[]{:S(2)}, u32[]{:S(2)}) collective-permute-start(bf16[2048,128]{1,0:T(8,128)(2,1)S(1)} %pack_couple.1.refs_0_), channel_id=1, source_target_pairs={{0,4},{4,0},{8,12},{12,8},{1,5},{5,1},{9,13},{13,9},{2,6},{6,2},{1... | collective-permute-start | bytes 1572872 | tf_op jit(solution)/shard_map/ppermute | solution.py:190
  5.6 25.5 %collective-permute-start.1 = (bf16[2048,128]{1,0:T(8,128)(2,1)S(1)}, bf16[2048,128]{1,0:T(8,128)(2,1)S(1)}, u32[]{:S(2)}, u32[]{:S(2)}) collective-permute-start(bf16[2048,128]{1,0:T(8,128)(2,1)S(1)} %pack_couple.1.refs_0_), channel_id=1, source_target_pairs={{4,8},{8,4},{0,12},{12,0},{5,9},{9,5},{1,13},{13,1},{6,10},{10,6},... | collective-permute-start | bytes 1572872 | tf_op jit(solution)/shard_map/ppermute | solution.py:191
  9.2 1.9 %collective-permute-start.4 = (bf16[64,2048]{1,0:T(8,128)(2,1)S(1)}, bf16[64,2048]{1,0:T(8,128)(2,1)S(1)}, u32[]{:S(2)}, u32[]{:S(2)}) collective-permute-start(bf16[64,2048]{1,0:T(8,128)(2,1)S(1)} %get-tuple-element.13), channel_id=1, source_target_pairs={{0,1},{1,0},{2,3},{3,2},{4,5},{5,4},{6,7},{7,6},{8,9},{9,8},{10,11... | collective-permute-start | bytes 786440 | tf_op jit(solution)/shard_map/ppermute | solution.py:219
  9.3 9.2 %collective-permute-start.5 = (bf16[64,2048]{1,0:T(8,128)(2,1)S(1)}, bf16[64,2048]{1,0:T(8,128)(2,1)S(1)}, u32[]{:S(2)}, u32[]{:S(2)}) collective-permute-start(bf16[64,2048]{1,0:T(8,128)(2,1)S(1)} %get-tuple-element.12.own_ref), channel_id=1, source_target_pairs={{0,2},{1,3},{2,0},{3,1},{4,6},{5,7},{6,4},{7,5},{8,10},{9,11},{10,... | collective-permute-start | bytes 786440 | tf_op jit(solution)/shard_map/ppermute | solution.py:219
  10.9 12.3 %collective-permute-start.6 = (bf16[64,2048]{1,0:T(8,128)(2,1)S(1)}, bf16[64,2048]{1,0:T(8,128)(2,1)S(1)}, u32[]{:S(2)}, u32[]{:S(2)}) collective-permute-start(bf16[64,2048]{1,0:T(8,128)(2,1)S(1)} %get-tuple-element.13), channel_id=1, source_target_pairs={{0,3},{1,2},{2,1},{3,0},{4,7},{5,6},{6,5},{7,4},{8,11},{9,10},{10,... | collective-permute-start | bytes 786440 | tf_op jit(solution)/shard_map/ppermute | solution.py:219
  23.2 1.0 %copy-start.5 = (bf16[512,512]{1,0:T(8,128)(2,1)S(1)}, bf16[512,512]{1,0:T(8,128)(2,1)}, u32[]{:S(2)}) copy-start(bf16[512,512]{1,0:T(8,128)(2,1)} %constant.4.clone.fwd_ref) | copy-start | bytes 1572868
  29.0 3.3 %collective-permute-start.7 = (f32[72,2048]{1,0:T(8,128)S(1)}, f32[72,2048]{1,0:T(8,128)S(1)}, u32[]{:S(2)}, u32[]{:S(2)}) collective-permute-start(f32[72,2048]{1,0:T(8,128)S(1)} %get-tuple-element.15), channel_id=1, source_target_pairs={{0,1},{1,0},{2,3},{3,2},{4,5},{5,4},{6,7},{7,6},{8,9},{9,8},{10,11... | collective-permute-start | bytes 1769480 | tf_op jit(solution)/shard_map/ppermute | solution.py:219
  29.7 4.3 %collective-permute-start.2 = (bf16[2048,128]{1,0:T(8,128)(2,1)S(1)}, bf16[2048,128]{1,0:T(8,128)(2,1)S(1)}, u32[]{:S(2)}, u32[]{:S(2)}) collective-permute-start(bf16[2048,128]{1,0:T(8,128)(2,1)S(1)} %collective-permute-done.refs_1_), channel_id=1, source_target_pairs={{4,8},{8,4},{5,9},{9,5},{6,10},{10,6},{7,11},{11,7},{20,24},{24,20... | collective-permute-start | bytes 1572872 | tf_op jit(solution)/shard_map/ppermute | solution.py:192
  31.0 15.1 %collective-permute-start.3 = (bf16[2048,128]{1,0:T(8,128)(2,1)S(1)}, bf16[2048,128]{1,0:T(8,128)(2,1)S(1)}, u32[]{:S(2)}, u32[]{:S(2)}) collective-permute-start(bf16[2048,128]{1,0:T(8,128)(2,1)S(1)} %collective-permute-done.1.refs_2_), channel_id=1, source_target_pairs={{4,0},{8,12},{5,1},{9,13},{6,2},{10,14},{7,3},{11,15},{20,16},{24,... | collective-permute-start | bytes 1572872 | tf_op jit(solution)/shard_map/ppermute | solution.py:193
  47.1 1.2 %collective-permute-start.8 = (f32[8,128]{1,0:T(8,128)S(1)}, f32[8,128]{1,0:T(8,128)S(1)}, u32[]{:S(2)}, u32[]{:S(2)}) collective-permute-start(f32[8,128]{1,0:T(8,128)S(1)} %get-tuple-element.21), channel_id=1, source_target_pairs={{0,1},{1,0},{2,3},{3,2},{4,5},{5,4},{6,7},{7,6},{8,9},{9,8},{10,11... | collective-permute-start | bytes 12296 | tf_op jit(solution)/shard_map/ppermute | solution.py:219
  48.4 3.6 %collective-permute-start.9 = (f32[8,128]{1,0:T(8,128)S(1)}, f32[8,128]{1,0:T(8,128)S(1)}, u32[]{:S(2)}, u32[]{:S(2)}) collective-permute-start(f32[8,128]{1,0:T(8,128)S(1)} %add.9), channel_id=1, source_target_pairs={{0,2},{1,3},{2,0},{3,1},{4,6},{5,7},{6,4},{7,5},{8,10},{9,11},{10,... | collective-permute-start | bytes 12296 | tf_op jit(solution)/shard_map/ppermute | solution.py:219
  52.0 3.6 %collective-permute-start.10 = (f32[8,128]{1,0:T(8,128)S(1)}, f32[8,128]{1,0:T(8,128)S(1)}, u32[]{:S(2)}, u32[]{:S(2)}) collective-permute-start(f32[8,128]{1,0:T(8,128)S(1)} %add.10), channel_id=1, source_target_pairs={{0,4},{4,0},{8,12},{12,8},{1,5},{5,1},{9,13},{13,9},{2,6},{6,2},{1... | collective-permute-start | bytes 12296 | tf_op jit(solution)/shard_map/ppermute | solution.py:304
  55.6 4.5 %collective-permute-start.11 = (f32[8,128]{1,0:T(8,128)S(1)}, f32[8,128]{1,0:T(8,128)S(1)}, u32[]{:S(2)}, u32[]{:S(2)}) collective-permute-start(f32[8,128]{1,0:T(8,128)S(1)} %add.11.one_ref), channel_id=1, source_target_pairs={{0,8},{4,12},{8,0},{12,4},{1,9},{5,13},{9,1},{13,5},{2,10},{6,14},... | collective-permute-start | bytes 12296 | tf_op jit(solution)/shard_map/ppermute | solution.py:304

commit v3 on v2

--- a/solution.py
+++ b/solution.py
@@ -43,7 +43,7 @@
         out_ref[rows, :] = jnp.concatenate([re, im], axis=1).astype(BF16)
 
 
-def pack_time(harm, bodies, reals, vel_ref, own_ref, send_ref):
+def pack_time(harm, bodies, reals, vel_ref, own_ref, send_ref, again_ref):
     core = lax.axis_index("harm") % 2
     half = bodies // 2
     pair = bodies // 4
@@ -52,10 +52,11 @@
             one = vel_ref[pl.ds(which * half + j, 2 * harm, stride=bodies), :]
             two = vel_ref[pl.ds(which * half + pair + j, 2 * harm, stride=bodies), :]
             out_ref[:, pl.ds(j * 2 * reals, 2 * reals)] = jnp.concatenate([one, two], axis=1).astype(BF16)
+    pack_couple(harm, bodies, reals, vel_ref, again_ref)
 
 
 def time_kernel(harm, bodies, reals, quad_ref, coul_ref, own_ref, core_ref, far_ref, far_core_ref, fwd_ref, inv_ref,
-                mine_ref, other_ref, held_ref, force_ref):
+                mine_ref, other_ref, other_im_ref, held_ref, force_ref):
     step = pl.program_id(0)
     me = lax.axis_index("harm")
     core = me % 2
@@ -97,25 +98,28 @@
     back = jnp.dot(inv_ref[pl.ds(first, 2 * size), :], force_ref[...], preferred_element_type=F32) * (2.0 * H / NT)
     lower = core == 0
     mine_ref[:size] = jnp.where(lower, back[:size], back[size:])
-    other_ref[:size] = jnp.where(lower, back[size:], back[:size])
+    other = jnp.where(lower, back[size:], back[:size])
     slope = jnp.broadcast_to(mean, (8, width))
     mine_ref[size:] = slope
-    other_ref[size:] = slope
-
-
-def prepare_kernel(harm, bodies, reals, imped_ref, mine_ref, other_ref, excite_ref, velocity_ref,
+    other_ref[...] = other[:harm]
+    other_im_ref[:harm] = other[harm:]
+    other_im_ref[harm:] = slope
+
+
+def prepare_kernel(harm, bodies, reals, imped_ref, mine_ref, other_re_ref, other_im_ref, excite_ref, velocity_ref,
                    rest_ref, p_ref, q_ref, vel_ref, slope_ref):
     everyone = imped_ref.shape[3]
     group = 2 * reals
     half = bodies // 2
     pair = bodies // 4
     core = lax.axis_index("harm") % 2
-    for which, ref in ((core, mine_ref), (1 - core, other_ref)):
+    mine_re_ref, mine_im_ref = mine_ref.at[:harm], mine_ref.at[harm:]
+    for which, re_ref, im_ref in ((core, mine_re_ref, mine_im_ref), (1 - core, other_re_ref, other_im_ref)):
         for j in range(pair):
             cols = slice(j * group, (j + 1) * group)
-            re = ref[:harm, cols]
-            im = ref[harm:2 * harm, cols]
-            slope = ref[2 * harm:2 * harm + 1, cols]
+            re = re_ref[:, cols]
+            im = im_ref[:harm, cols]
+            slope = im_ref[harm:harm + 1, cols]
             one = which * half + j
             two = one + pair
             rest_ref[pl.ds(one, harm, stride=bodies), :] = jnp.concatenate([re[:, :reals], im[:, :reals]], axis=1)
@@ -147,7 +151,7 @@
         rest_ref[rows, :] = rest_ref[rows, :] - excite + slope * (vel - vel.astype(BF16).astype(F32))
 
 
-def couple_kernel(harm, bodies, reals, flips, imped_ref, *refs):
+def couple_kernel(harm, bodies, reals, line, imped_ref, *refs):
     pieces, (rest_ref, res_ref, total_ref, held_ref) = refs[:-4], refs[-4:]
     me = lax.axis_index("body")
     sign = jnp.where(lax.broadcasted_iota(jnp.int32, (bodies, 2 * reals), 1) < reals, -1.0, 1.0)
@@ -155,14 +159,14 @@
     ends = jnp.logical_or(me == 0, me == 3)
     for h in range(harm):
         rows = pl.ds(h * bodies, bodies)
-        if flips is None:
+        if not line:
             vels = pieces[0][:, h].reshape(-1, 2 * reals)
         else:
             slot = h % 4
-            for flip, ref in zip(flips, pieces[:-2]):
-                held_ref[slot, pl.ds(pl.multiple_of((me ^ flip) * bodies, bodies), bodies), :] = ref[rows, :]
-            held_ref[slot, pl.ds(pl.multiple_of((me ^ 2) * bodies, bodies), bodies), :] = jnp.where(
-                ends, pieces[-1][rows, :], pieces[-2][rows, :])
+            held = [ref[rows, :] for ref in pieces]
+            for flip, value in ((0, held[0]), (1, held[1]), (3, jnp.where(ends, held[3], held[2])),
+                                (2, jnp.where(ends, held[4], held[5]))):
+                held_ref[slot, pl.ds(pl.multiple_of((me ^ flip) * bodies, bodies), bodies), :] = value
             vels = held_ref[slot]
         both = imped_ref[:, h].reshape(2 * bodies, imped_ref.shape[3])
         out = jnp.dot(both, vels, preferred_element_type=F32)
@@ -186,12 +190,13 @@
     out_ref[0] = jnp.sqrt(mean)[0, 0]
 
 
-def gather_line(x, axis):
+def gather_line(x, again, axis):
     near = lax.ppermute(x, axis, [(0, 1), (1, 0), (2, 3), (3, 2)])
-    cross = lax.ppermute(x, axis, [(1, 2), (2, 1), (0, 3), (3, 0)])
+    cross = lax.ppermute(x, axis, [(1, 2), (2, 1)])
+    across = lax.ppermute(again, axis, [(0, 3), (3, 0)])
+    outer = lax.ppermute(cross, axis, [(1, 0), (2, 3)])
     inner = lax.ppermute(near, axis, [(1, 2), (2, 1)])
-    outer = lax.ppermute(cross, axis, [(1, 0), (2, 3)])
-    return x, near, cross, inner, outer
+    return x, near, cross, across, outer, inner
 
 
 def params(mib=24):
@@ -225,55 +230,55 @@
             cost_estimate=cost(0, 1 << 10),
             name="pack_couple",
         )(flat)
+        columns = bodies * reals // 2
+        own, send, again = pl.pallas_call(
+            functools.partial(pack_time, harm, bodies, reals),
+            in_specs=[VMEM],
+            out_shape=(
+                *[jax.ShapeDtypeStruct((2 * harm, columns), BF16)] * 2,
+                jax.ShapeDtypeStruct((total_rows, group), BF16),
+            ),
+            compiler_params=params(),
+            cost_estimate=cost(0, 1 << 10),
+            name="pack_time",
+        )(flat)
         if body_count == 4:
-            pieces = gather_line(low, "body")
-            flips = (0, 1, 3)
+            pieces = gather_line(low, again, "body")
         else:
             pieces = (lax.all_gather(low, "body").reshape(body_count, harm, bodies, group),)
-            flips = None
-
-        columns = bodies * reals // 2
-        own, send = pl.pallas_call(
-            functools.partial(pack_time, harm, bodies, reals),
-            in_specs=[VMEM],
-            out_shape=(jax.ShapeDtypeStruct((2 * harm, columns), BF16),) * 2,
-            compiler_params=params(),
-            cost_estimate=cost(0, 1 << 10),
-            name="pack_time",
-        )(flat)
+
         far = flipped(own, 2)
         far_core = flipped(send, 3)
         core = flipped(send, 1)
 
         width = 8 * group
         tile = pl.BlockSpec((2 * harm, width), lambda i: (0, i))
-        half_spec = pl.BlockSpec((2 * harm + 8, width), lambda i: (0, i))
-        half_shape = jax.ShapeDtypeStruct((2 * harm + 8, columns), F32)
-        mine, other = pl.pallas_call(
+        heights = (2 * harm + 8, harm, harm + 8)
+        mine, *other = pl.pallas_call(
             functools.partial(time_kernel, harm, bodies, reals),
             grid=(columns // width,),
             in_specs=[SMEM, SMEM, tile, tile, tile, tile, VMEM, VMEM],
-            out_specs=[half_spec, half_spec],
-            out_shape=(half_shape, half_shape),
+            out_specs=[pl.BlockSpec((height, width), lambda i: (0, i)) for height in heights],
+            out_shape=tuple(jax.ShapeDtypeStruct((height, columns), F32) for height in heights),
             scratch_shapes=[pltpu.VMEM((4 * H, width), BF16), pltpu.VMEM((3 * NT, width), BF16)],
             compiler_params=params(),
             cost_estimate=cost(0, 1 << 10),
             name="time_kernel",
         )(quad_coef, coul_coef, own, core, far, far_core, jnp.asarray(forward), jnp.asarray(inverse))
-        other = flipped(other, 1)
+        other = [flipped(part, 1) for part in other]
 
         rest, factor_p, factor_q, vel_dense = pl.pallas_call(
             functools.partial(prepare_kernel, harm, bodies, reals),
-            in_specs=[VMEM] * 5,
+            in_specs=[VMEM] * 6,
             out_shape=(dense,) * 4,
             scratch_shapes=[pltpu.VMEM((bodies, group), F32)],
             compiler_params=params(),
             cost_estimate=cost(0, 1 << 10),
             name="prepare",
-        )(imped, mine, other, flat_excite, flat)
+        )(imped, mine, *other, flat_excite, flat)
 
         res, total = pl.pallas_call(
-            functools.partial(couple_kernel, harm, bodies, reals, flips),
+            functools.partial(couple_kernel, harm, bodies, reals, body_count == 4),
             in_specs=[VMEM] * (2 + len(pieces)),
             out_shape=(dense, jax.ShapeDtypeStruct((8, 128), F32)),
             scratch_shapes=[pltpu.VMEM((4, everyone, group), BF16)],

time: 60.9 us -> 59.2 us (0.972)
  waiting for transfers between devices: 33.8 us -> 25 us
  starting transfers between devices: 12.4 us -> 19.1 us
    ppermute x6 -> x7, waiting for transfers between devices: 15.3 us -> 7.06 us  [flipped(): return lax.ppermute(x, 'harm', [(i, i ^ flip) for i in range(4)])]
    ppermute x1, waiting for transfers between devices: 0.01 us -> 4.5 us  [gather_line(): near = lax.ppermute(x, axis, [(0, 1), (1, 0), (2, 3), (3, 2)])]
    ppermute x1, starting transfers between devices: 3.09 us -> 6.01 us  [gather_line(): near = lax.ppermute(x, axis, [(0, 1), (1, 0), (2, 3), (3, 2)])]
    ppermute x1, waiting for transfers between devices: 12.1 us -> 9.84 us  [gather_line(): outer = lax.ppermute(cross, axis, [(1, 0), (2, 3)])]
    ppermute x2, starting transfers between devices: 0.7 us -> 2.83 us  [local(): lax.ppermute(total, 'body', [(i, i ^ flip) for i in range(body_count)])]
    ppermute x2, waiting for transfers between devices: 5.76 us -> 3.62 us  [local(): lax.ppermute(total, 'body', [(i, i ^ flip) for i in range(body_count)])]
    ppermute x1 -> x2, starting transfers between devices: 2.47 us -> 4.07 us  [the longest x1 3.25 us: gather_line(): across = lax.ppermute(again, axis, [(0, 3), (3, 0)])]
    ppermute x1 -> x2, waiting for transfers between devices: 0.69 us -> 0.01 us  [the longest x1 0.01 us: gather_line(): cross = lax.ppermute(x, axis, [(1, 2), (2, 1)])]
  transfers between devices with their start and end apart: 12 -> 14, of which waited for: 8 -> 8; matrix products, arithmetic and copies ran while one was open for 0% -> 0% of each run, Pallas kernels for 15% -> 16%
where the time goes in v3:
time: 59.2 us; the launch traced here: 58.9 us
  waiting for transfers between devices  25 us (42%)
  starting transfers between devices  19.1 us (32%)
  Pallas kernels  11.3 us (19%)
  local copies, waits for them, and re-layouts  2.66 us (4%)
  between operations  0.81 us (1%)
    ppermute x1, waiting for transfers between devices, gather_line(): outer = lax.ppermute(cross, axis, [(1, 0), (2, 3)])  9.84 us
    ppermute x7, waiting for transfers between devices, flipped(): return lax.ppermute(x, 'harm', [(i, i ^ flip) for i in range(4)])  7.06 us
    ppermute x1, starting transfers between devices, gather_line(): near = lax.ppermute(x, axis, [(0, 1), (1, 0), (2, 3), (3, 2)])  6.01 us
    pallas_call x1, Pallas kernels, local(): pl.pallas_call(functools.partial(time_kernel, harm, bodies, reals), grid=...  4.77 us
    ppermute x1, waiting for transfers between devices, gather_line(): near = lax.ppermute(x, axis, [(0, 1), (1, 0), (2, 3), (3, 2)])  4.5 us
    ppermute x7, starting transfers between devices, flipped(): return lax.ppermute(x, 'harm', [(i, i ^ flip) for i in range(4)])  4.23 us
    ppermute x2, waiting for transfers between devices, local(): lax.ppermute(total, 'body', [(i, i ^ flip) for i in range(body_count)])  3.62 us
    ppermute x1, starting transfers between devices, gather_line(): across = lax.ppermute(again, axis, [(0, 3), (3, 0)])  3.25 us
  transfers between devices with their start and end apart: 14, of which 8 were waited for; matrix products, arithmetic and copies ran while one was open for 0% of the time, Pallas kernels for 16%

profile of v3, /device:TPU:0, one launch (start us, length us, event | category | flops | bytes accessed | tf_op | source)
XLA Modules:
  0.0 58.9 jit_solution(14591879961173901727)
XLA Ops:
  0.6 0.0 copy-start.6
  0.6 0.0 copy-start.7
  0.7 0.0 copy-start
  0.7 1.6 %copy-done = f32[2,32,64,64]{3,2,1,0:T(8,128)S(1)} copy-done((f32[2,32,64,64]{3,2,1,0:T(8,128)S(1)}, f32[2,32,64,64]{3,2,1,0:T(8,128)}, u32[]{:S(2)}) %copy-start) | copy-done | bytes 1048600
  2.3 0.2 pack_couple.1.refs_0_
  2.5 0.0 copy-start.1
  2.5 0.0 copy-start.2
  2.5 0.8 %collective-permute-start.1 = (bf16[2048,128]{1,0:T(8,128)(2,1)S(1)}, bf16[2048,128]{1,0:T(8,128)(2,1)S(1)}, u32[]{:S(2)}, u32[]{:S(2)}) collective-permute-start(bf16[2048,128]{1,0:T(8,128)(2,1)S(1)} %pack_couple.1.refs_0_), channel_id=1, source_target_pairs={{4,8},{8,4},{5,9},{9,5},{6,10},{10,6},{7,11},{11,7},{20,24},{24,20... | collective-permute-start | bytes 1572872 | tf_op jit(solution)/shard_map/ppermute | solution.py:195
  3.3 6.0 %collective-permute-start = (bf16[2048,128]{1,0:T(8,128)(2,1)S(1)}, bf16[2048,128]{1,0:T(8,128)(2,1)S(1)}, u32[]{:S(2)}, u32[]{:S(2)}) collective-permute-start(bf16[2048,128]{1,0:T(8,128)(2,1)S(1)} %pack_couple.1.refs_0_), channel_id=1, source_target_pairs={{0,4},{4,0},{8,12},{12,8},{1,5},{5,1},{9,13},{13,9},{2,6},{6,2},{1... | collective-permute-start | bytes 1572872 | tf_op jit(solution)/shard_map/ppermute | solution.py:194
  9.3 1.3 %pack_time.1 = (bf16[64,2048]{1,0:T(8,128)(2,1)S(1)}, bf16[64,2048]{1,0:T(8,128)(2,1)S(1)}, bf16[2048,128]{1,0:T(8,128)(2,1)S(1)}) custom-call(f32[4096,64]{1,0:T(8,128)S(1)} %bitcast.4), custom_call_target="tpu_custom_call" | custom-call | bytes 1024 | tf_op jit(solution)/shard_map/pack_time/pallas_call | solution.py:234
  10.7 0.1 collective-permute-start.5
  10.8 1.6 %collective-permute-start.6 = (bf16[64,2048]{1,0:T(8,128)(2,1)S(1)}, bf16[64,2048]{1,0:T(8,128)(2,1)S(1)}, u32[]{:S(2)}, u32[]{:S(2)}) collective-permute-start(bf16[64,2048]{1,0:T(8,128)(2,1)S(1)} %get-tuple-element.15.own_ref), channel_id=1, source_target_pairs={{0,2},{1,3},{2,0},{3,1},{4,6},{5,7},{6,4},{7,5},{8,10},{9,11},{10,... | collective-permute-start | bytes 786440 | tf_op jit(solution)/shard_map/ppermute | solution.py:224
  12.4 0.3 collective-permute-start.7
  12.6 0.0 collective-permute-done.5.core_ref
  12.6 3.2 %collective-permute-start.2 = (bf16[2048,128]{1,0:T(8,128)(2,1)S(1)}, bf16[2048,128]{1,0:T(8,128)(2,1)S(1)}, u32[]{:S(2)}, u32[]{:S(2)}) collective-permute-start(bf16[2048,128]{1,0:T(8,128)(2,1)S(1)} %get-tuple-element.14), channel_id=1, source_target_pairs={{0,12},{12,0},{1,13},{13,1},{2,14},{14,2},{3,15},{15,3},{16,28},{2... | collective-permute-start | bytes 1572872 | tf_op jit(solution)/shard_map/ppermute | solution.py:196
  15.9 0.0 collective-permute-done.1.refs_2_
  15.9 1.3 %collective-permute-start.3 = (bf16[2048,128]{1,0:T(8,128)(2,1)S(1)}, bf16[2048,128]{1,0:T(8,128)(2,1)S(1)}, u32[]{:S(2)}, u32[]{:S(2)}) collective-permute-start(bf16[2048,128]{1,0:T(8,128)(2,1)S(1)} %collective-permute-done.1.refs_2_), channel_id=1, source_target_pairs={{4,0},{8,12},{5,1},{9,13},{6,2},{10,14},{7,3},{11,15},{20,16},{24,... | collective-permute-start | bytes 1572872 | tf_op jit(solution)/shard_map/ppermute | solution.py:197
  17.2 4.5 %collective-permute-done.refs_1_ = bf16[2048,128]{1,0:T(8,128)(2,1)S(1)} collective-permute-done((bf16[2048,128]{1,0:T(8,128)(2,1)S(1)}, bf16[2048,128]{1,0:T(8,128)(2,1)S(1)}, u32[]{:S(2)}, u32[]{:S(2)}) %collective-permute-start) | collective-permute-done | bytes 524320 | tf_op jit(solution)/shard_map/ppermute | solution.py:194
  21.7 0.7 %collective-permute-start.4 = (bf16[2048,128]{1,0:T(8,128)(2,1)S(1)}, bf16[2048,128]{1,0:T(8,128)(2,1)S(1)}, u32[]{:S(2)}, u32[]{:S(2)}) collective-permute-start(bf16[2048,128]{1,0:T(8,128)(2,1)S(1)} %collective-permute-done.refs_1_), channel_id=1, source_target_pairs={{4,8},{8,4},{5,9},{9,5},{6,10},{10,6},{7,11},{11,7},{20,24},{24,20... | collective-permute-start | bytes 1572872 | tf_op jit(solution)/shard_map/ppermute | solution.py:198
  22.4 0.0 collective-permute-done.6.far_ref
  22.4 2.3 %collective-permute-done.7.far_core_ref = bf16[64,2048]{1,0:T(8,128)(2,1)S(1)} collective-permute-done((bf16[64,2048]{1,0:T(8,128)(2,1)S(1)}, bf16[64,2048]{1,0:T(8,128)(2,1)S(1)}, u32[]{:S(2)}, u32[]{:S(2)}) %collective-permute-start.7) | collective-permute-done | bytes 262176 | tf_op jit(solution)/shard_map/ppermute | solution.py:224
  24.7 0.0 copy-done.6
  24.7 0.0 copy-done.7
  24.7 0.0 copy-done.4
  24.7 0.0 copy-start.5
  24.7 1.0 %copy-done.5 = bf16[512,512]{1,0:T(8,128)(2,1)S(1)} copy-done((bf16[512,512]{1,0:T(8,128)(2,1)S(1)}, bf16[512,512]{1,0:T(8,128)(2,1)}, u32[]{:S(2)}) %copy-start.5) | copy-done | bytes 524312
  25.7 4.8 %time_kernel.1 = (f32[72,2048]{1,0:T(8,128)S(1)}, f32[32,2048]{1,0:T(8,128)S(1)}, f32[40,2048]{1,0:T(8,128)S(1)}) custom-call(f32[64]{0:T(128)S(1)} %copy-done.6, f32[64]{0:T(128)S(1)} %copy-done.7, bf16[64,2048]{1,0:T(8,128)(2,1)S(1)} %get-tuple-element.15.own_ref, bf16[64,2048]{1,0:T(8,128)(2,1)S(1)} %collective-permute-done.5.core_ref, ...), custom_call_target="tpu_custom_call" | custom-call | bytes 1024 | tf_op jit(solution)/shard_map/time_kernel/pallas_call | solution.py:257
  30.5 0.6 %collective-permute-start.9 = (f32[40,2048]{1,0:T(8,128)S(1)}, f32[40,2048]{1,0:T(8,128)S(1)}, u32[]{:S(2)}, u32[]{:S(2)}) collective-permute-start(f32[40,2048]{1,0:T(8,128)S(1)} %get-tuple-element.19), channel_id=1, source_target_pairs={{0,1},{1,0},{2,3},{3,2},{4,5},{5,4},{6,7},{7,6},{8,9},{9,8},{10,11... | collective-permute-start | bytes 983048 | tf_op jit(solution)/shard_map/ppermute | solution.py:224
  31.1 0.1 collective-permute-start.8
  31.2 1.6 %collective-permute-done.8.other_re_ref = f32[32,2048]{1,0:T(8,128)S(1)} collective-permute-done((f32[32,2048]{1,0:T(8,128)S(1)}, f32[32,2048]{1,0:T(8,128)S(1)}, u32[]{:S(2)}, u32[]{:S(2)}) %collective-permute-start.8) | collective-permute-done | bytes 262176 | tf_op jit(solution)/shard_map/ppermute | solution.py:224
  32.8 0.0 collective-permute-done.9.other_im_ref
  32.8 0.0 copy-done.3
  32.8 0.0 copy-done.1
  32.8 1.6 %prepare.1 = (f32[2048,128]{1,0:T(8,128)S(1)}, f32[2048,128]{1,0:T(8,128)S(1)}, f32[2048,128]{1,0:T(8,128)S(1)}, f32[2048,128]{1,0:T(8,128)S(1)}) custom-call(bf16[2,32,64,256]{3,2,1,0:T(8,128)(2,1)S(1)} %copy-done.2, f32[72,2048]{1,0:T(8,128)S(1)} %get-tuple-element.17.mine_ref, f32[32,2048]{1,0:T(8,128)S(1)} %collective-permute-done.8.other_re_ref, ...), custom_call_target="tpu_custom_call" | custom-call | bytes 1024 | tf_op jit(solution)/shard_map/prepare/pallas_call | solution.py:270
  34.4 0.0 collective-permute-done.2.refs_3_
  34.4 9.8 %collective-permute-done.3.refs_4_ = bf16[2048,128]{1,0:T(8,128)(2,1)S(1)} collective-permute-done((bf16[2048,128]{1,0:T(8,128)(2,1)S(1)}, bf16[2048,128]{1,0:T(8,128)(2,1)S(1)}, u32[]{:S(2)}, u32[]{:S(2)}) %collective-permute-start.3) | collective-permute-done | bytes 524320 | tf_op jit(solution)/shard_map/ppermute | solution.py:197
  44.2 0.0 collective-permute-done.4.refs_5_
  44.2 1.2 %couple.1 = (f32[2048,128]{1,0:T(8,128)S(1)}, f32[8,128]{1,0:T(8,128)S(1)}) custom-call(bf16[2,32,64,256]{3,2,1,0:T(8,128)(2,1)S(1)} %copy-done.2, bf16[2048,128]{1,0:T(8,128)(2,1)S(1)} %pack_couple.1.refs_0_, bf16[2048,128]{1,0:T(8,128)(2,1)S(1)} %collective-permute-done.refs_1_, bf16[2048,128]{1,0:T(8,128)(2,1)S(1)} %collective-permute-done.1.refs_2_, ...), custom_call_target="tpu_custom_call" | custom-call | bytes 1024 | tf_op jit(solution)/shard_map/couple/pallas_call | solution.py:280
  45.4 0.1 collective-permute-start.10
  45.5 1.2 %collective-permute-done.10 = f32[8,128]{1,0:T(8,128)S(1)} collective-permute-done((f32[8,128]{1,0:T(8,128)S(1)}, f32[8,128]{1,0:T(8,128)S(1)}, u32[]{:S(2)}, u32[]{:S(2)}) %collective-permute-start.10) | collective-permute-done | bytes 4128 | tf_op jit(solution)/shard_map/ppermute | solution.py:224
  46.6 1.5 %collective-permute-start.11 = (f32[8,128]{1,0:T(8,128)S(1)}, f32[8,128]{1,0:T(8,128)S(1)}, u32[]{:S(2)}, u32[]{:S(2)}) collective-permute-start(f32[8,128]{1,0:T(8,128)S(1)} %add.9), channel_id=1, source_target_pairs={{0,2},{1,3},{2,0},{3,1},{4,6},{5,7},{6,4},{7,5},{8,10},{9,11},{10,... | collective-permute-start | bytes 12296 | tf_op jit(solution)/shard_map/ppermute | solution.py:224
  48.2 2.1 %collective-permute-done.11 = f32[8,128]{1,0:T(8,128)S(1)} collective-permute-done((f32[8,128]{1,0:T(8,128)S(1)}, f32[8,128]{1,0:T(8,128)S(1)}, u32[]{:S(2)}, u32[]{:S(2)}) %collective-permute-start.11) | collective-permute-done | bytes 4128 | tf_op jit(solution)/shard_map/ppermute | solution.py:224
  50.3 0.9 %collective-permute-start.12 = (f32[8,128]{1,0:T(8,128)S(1)}, f32[8,128]{1,0:T(8,128)S(1)}, u32[]{:S(2)}, u32[]{:S(2)}) collective-permute-start(f32[8,128]{1,0:T(8,128)S(1)} %add.10), channel_id=1, source_target_pairs={{0,4},{4,0},{8,12},{12,8},{1,5},{5,1},{9,13},{13,9},{2,6},{6,2},{1... | collective-permute-start | bytes 12296 | tf_op jit(solution)/shard_map/ppermute | solution.py:309
  51.2 2.7 %collective-permute-done.12 = f32[8,128]{1,0:T(8,128)S(1)} collective-permute-done((f32[8,128]{1,0:T(8,128)S(1)}, f32[8,128]{1,0:T(8,128)S(1)}, u32[]{:S(2)}, u32[]{:S(2)}) %collective-permute-start.12) | collective-permute-done | bytes 4128 | tf_op jit(solution)/shard_map/ppermute | solution.py:309
  53.9 1.9 %collective-permute-start.13 = (f32[8,128]{1,0:T(8,128)S(1)}, f32[8,128]{1,0:T(8,128)S(1)}, u32[]{:S(2)}, u32[]{:S(2)}) collective-permute-start(f32[8,128]{1,0:T(8,128)S(1)} %add.11.one_ref), channel_id=1, source_target_pairs={{0,8},{4,12},{8,0},{12,4},{1,9},{5,13},{9,1},{13,5},{2,10},{6,14},... | collective-permute-start | bytes 12296 | tf_op jit(solution)/shard_map/ppermute | solution.py:309
  55.7 1.7 %finish.1 = f32[2,2048,64]{2,1,0:T(8,128)} custom-call(f32[2048,128]{1,0:T(8,128)S(1)} %get-tuple-element.21.res_ref, f32[2048,128]{1,0:T(8,128)S(1)} %get-tuple-element.22.p_ref, f32[2048,128]{1,0:T(8,128)S(1)} %get-tuple-element.23.q_ref, f32[2048,128]{1,0:T(8,128)S(1)} %get-tuple-element.24.vel_ref), custom_call_target="tpu_custom_call" | custom-call | bytes 1024 | tf_op jit(solution)/shard_map/finish/pallas_call | solution.py:292
  57.4 1.0 %collective-permute-done.13.two_ref = f32[8,128]{1,0:T(8,128)S(1)} collective-permute-done((f32[8,128]{1,0:T(8,128)S(1)}, f32[8,128]{1,0:T(8,128)S(1)}, u32[]{:S(2)}, u32[]{:S(2)}) %collective-permute-start.13) | collective-permute-done | bytes 4128 | tf_op jit(solution)/shard_map/ppermute | solution.py:309
  58.4 0.6 rms.1
  (6 shorter events, 0.0 us)
Async XLA Ops:
  0.6 24.0 %copy-start.6 = (f32[64]{0:T(128)S(1)}, f32[64]{0:T(128)}, u32[]{:S(2)}) copy-start(f32[64]{0:T(128)} %quad_ref.1) | copy-start | bytes 772
  0.6 24.0 %copy-start.7 = (f32[64]{0:T(128)S(1)}, f32[64]{0:T(128)}, u32[]{:S(2)}) copy-start(f32[64]{0:T(128)} %coul_ref.1) | copy-start | bytes 772
  0.7 1.6 %copy-start = (f32[2,32,64,64]{3,2,1,0:T(8,128)S(1)}, f32[2,32,64,64]{3,2,1,0:T(8,128)}, u32[]{:S(2)}) copy-start(f32[2,32,64,64]{3,2,1,0:T(8,128)} %param.7) | copy-start | bytes 3145732
  2.3 22.4 %copy-start.4 = (bf16[256,1536]{1,0:T(8,128)(2,1)S(1)}, bf16[256,1536]{1,0:T(8,128)(2,1)}, u32[]{:S(2)}) copy-start(bf16[256,1536]{1,0:T(8,128)(2,1)} %constant.5.clone.inv_ref) | copy-start | bytes 2359300
  2.3 30.5 %copy-start.3 = (f32[2,32,64,64]{3,2,1,0:T(8,128)S(1)}, f32[2,32,64,64]{3,2,1,0:T(8,128)}, u32[]{:S(2)}) copy-start(f32[2,32,64,64]{3,2,1,0:T(8,128)} %param.9) | copy-start | bytes 3145732
  2.5 30.3 %copy-start.1 = (f32[2,32,64,64]{3,2,1,0:T(8,128)S(1)}, f32[2,32,64,64]{3,2,1,0:T(8,128)}, u32[]{:S(2)}) copy-start(f32[2,32,64,64]{3,2,1,0:T(8,128)} %param.7) | copy-start | bytes 3145732
  2.5 30.3 %copy-start.2 = (bf16[2,32,64,256]{3,2,1,0:T(8,128)(2,1)S(1)}, bf16[2,32,64,256]{3,2,1,0:T(8,128)(2,1)}, u32[]{:S(2)}) copy-start(bf16[2,32,64,256]{3,2,1,0:T(8,128)(2,1)} %imped_ref.3) | copy-start | bytes 6291460
  2.5 13.4 %collective-permute-start.1 = (bf16[2048,128]{1,0:T(8,128)(2,1)S(1)}, bf16[2048,128]{1,0:T(8,128)(2,1)S(1)}, u32[]{:S(2)}, u32[]{:S(2)}) collective-permute-start(bf16[2048,128]{1,0:T(8,128)(2,1)S(1)} %pack_couple.1.refs_0_), channel_id=1, source_target_pairs={{4,8},{8,4},{5,9},{9,5},{6,10},{10,6},{7,11},{11,7},{20,24},{24,20... | collective-permute-start | bytes 1572872 | tf_op jit(solution)/shard_map/ppermute | solution.py:195
  3.3 18.4 %collective-permute-start = (bf16[2048,128]{1,0:T(8,128)(2,1)S(1)}, bf16[2048,128]{1,0:T(8,128)(2,1)S(1)}, u32[]{:S(2)}, u32[]{:S(2)}) collective-permute-start(bf16[2048,128]{1,0:T(8,128)(2,1)S(1)} %pack_couple.1.refs_0_), channel_id=1, source_target_pairs={{0,4},{4,0},{8,12},{12,8},{1,5},{5,1},{9,13},{13,9},{2,6},{6,2},{1... | collective-permute-start | bytes 1572872 | tf_op jit(solution)/shard_map/ppermute | solution.py:194
  10.7 1.9 %collective-permute-start.5 = (bf16[64,2048]{1,0:T(8,128)(2,1)S(1)}, bf16[64,2048]{1,0:T(8,128)(2,1)S(1)}, u32[]{:S(2)}, u32[]{:S(2)}) collective-permute-start(bf16[64,2048]{1,0:T(8,128)(2,1)S(1)} %get-tuple-element.16), channel_id=1, source_target_pairs={{0,1},{1,0},{2,3},{3,2},{4,5},{5,4},{6,7},{7,6},{8,9},{9,8},{10,11... | collective-permute-start | bytes 786440 | tf_op jit(solution)/shard_map/ppermute | solution.py:224
  10.8 11.6 %collective-permute-start.6 = (bf16[64,2048]{1,0:T(8,128)(2,1)S(1)}, bf16[64,2048]{1,0:T(8,128)(2,1)S(1)}, u32[]{:S(2)}, u32[]{:S(2)}) collective-permute-start(bf16[64,2048]{1,0:T(8,128)(2,1)S(1)} %get-tuple-element.15.own_ref), channel_id=1, source_target_pairs={{0,2},{1,3},{2,0},{3,1},{4,6},{5,7},{6,4},{7,5},{8,10},{9,11},{10,... | collective-permute-start | bytes 786440 | tf_op jit(solution)/shard_map/ppermute | solution.py:224
  12.4 12.3 %collective-permute-start.7 = (bf16[64,2048]{1,0:T(8,128)(2,1)S(1)}, bf16[64,2048]{1,0:T(8,128)(2,1)S(1)}, u32[]{:S(2)}, u32[]{:S(2)}) collective-permute-start(bf16[64,2048]{1,0:T(8,128)(2,1)S(1)} %get-tuple-element.16), channel_id=1, source_target_pairs={{0,3},{1,2},{2,1},{3,0},{4,7},{5,6},{6,5},{7,4},{8,11},{9,10},{10,... | collective-permute-start | bytes 786440 | tf_op jit(solution)/shard_map/ppermute | solution.py:224
  12.6 21.8 %collective-permute-start.2 = (bf16[2048,128]{1,0:T(8,128)(2,1)S(1)}, bf16[2048,128]{1,0:T(8,128)(2,1)S(1)}, u32[]{:S(2)}, u32[]{:S(2)}) collective-permute-start(bf16[2048,128]{1,0:T(8,128)(2,1)S(1)} %get-tuple-element.14), channel_id=1, source_target_pairs={{0,12},{12,0},{1,13},{13,1},{2,14},{14,2},{3,15},{15,3},{16,28},{2... | collective-permute-start | bytes 1572872 | tf_op jit(solution)/shard_map/ppermute | solution.py:196
  15.9 28.3 %collective-permute-start.3 = (bf16[2048,128]{1,0:T(8,128)(2,1)S(1)}, bf16[2048,128]{1,0:T(8,128)(2,1)S(1)}, u32[]{:S(2)}, u32[]{:S(2)}) collective-permute-start(bf16[2048,128]{1,0:T(8,128)(2,1)S(1)} %collective-permute-done.1.refs_2_), channel_id=1, source_target_pairs={{4,0},{8,12},{5,1},{9,13},{6,2},{10,14},{7,3},{11,15},{20,16},{24,... | collective-permute-start | bytes 1572872 | tf_op jit(solution)/shard_map/ppermute | solution.py:197
  21.7 22.5 %collective-permute-start.4 = (bf16[2048,128]{1,0:T(8,128)(2,1)S(1)}, bf16[2048,128]{1,0:T(8,128)(2,1)S(1)}, u32[]{:S(2)}, u32[]{:S(2)}) collective-permute-start(bf16[2048,128]{1,0:T(8,128)(2,1)S(1)} %collective-permute-done.refs_1_), channel_id=1, source_target_pairs={{4,8},{8,4},{5,9},{9,5},{6,10},{10,6},{7,11},{11,7},{20,24},{24,20... | collective-permute-start | bytes 1572872 | tf_op jit(solution)/shard_map/ppermute | solution.py:198
  24.7 1.0 %copy-start.5 = (bf16[512,512]{1,0:T(8,128)(2,1)S(1)}, bf16[512,512]{1,0:T(8,128)(2,1)}, u32[]{:S(2)}) copy-start(bf16[512,512]{1,0:T(8,128)(2,1)} %constant.4.clone.fwd_ref) | copy-start | bytes 1572868
  30.5 2.3 %collective-permute-start.9 = (f32[40,2048]{1,0:T(8,128)S(1)}, f32[40,2048]{1,0:T(8,128)S(1)}, u32[]{:S(2)}, u32[]{:S(2)}) collective-permute-start(f32[40,2048]{1,0:T(8,128)S(1)} %get-tuple-element.19), channel_id=1, source_target_pairs={{0,1},{1,0},{2,3},{3,2},{4,5},{5,4},{6,7},{7,6},{8,9},{9,8},{10,11... | collective-permute-start | bytes 983048 | tf_op jit(solution)/shard_map/ppermute | solution.py:224
  31.1 1.6 %collective-permute-start.8 = (f32[32,2048]{1,0:T(8,128)S(1)}, f32[32,2048]{1,0:T(8,128)S(1)}, u32[]{:S(2)}, u32[]{:S(2)}) collective-permute-start(f32[32,2048]{1,0:T(8,128)S(1)} %get-tuple-element.18), channel_id=1, source_target_pairs={{0,1},{1,0},{2,3},{3,2},{4,5},{5,4},{6,7},{7,6},{8,9},{9,8},{10,11... | collective-permute-start | bytes 786440 | tf_op jit(solution)/shard_map/ppermute | solution.py:224
  45.4 1.2 %collective-permute-start.10 = (f32[8,128]{1,0:T(8,128)S(1)}, f32[8,128]{1,0:T(8,128)S(1)}, u32[]{:S(2)}, u32[]{:S(2)}) collective-permute-start(f32[8,128]{1,0:T(8,128)S(1)} %get-tuple-element.25), channel_id=1, source_target_pairs={{0,1},{1,0},{2,3},{3,2},{4,5},{5,4},{6,7},{7,6},{8,9},{9,8},{10,11... | collective-permute-start | bytes 12296 | tf_op jit(solution)/shard_map/ppermute | solution.py:224
  46.6 3.6 %collective-permute-start.11 = (f32[8,128]{1,0:T(8,128)S(1)}, f32[8,128]{1,0:T(8,128)S(1)}, u32[]{:S(2)}, u32[]{:S(2)}) collective-permute-start(f32[8,128]{1,0:T(8,128)S(1)} %add.9), channel_id=1, source_target_pairs={{0,2},{1,3},{2,0},{3,1},{4,6},{5,7},{6,4},{7,5},{8,10},{9,11},{10,... | collective-permute-start | bytes 12296 | tf_op jit(solution)/shard_map/ppermute | solution.py:224
  50.3 3.6 %collective-permute-start.12 = (f32[8,128]{1,0:T(8,128)S(1)}, f32[8,128]{1,0:T(8,128)S(1)}, u32[]{:S(2)}, u32[]{:S(2)}) collective-permute-start(f32[8,128]{1,0:T(8,128)S(1)} %add.10), channel_id=1, source_target_pairs={{0,4},{4,0},{8,12},{12,8},{1,5},{5,1},{9,13},{13,9},{2,6},{6,2},{1... | collective-permute-start | bytes 12296 | tf_op jit(solution)/shard_map/ppermute | solution.py:309
  53.9 4.5 %collective-permute-start.13 = (f32[8,128]{1,0:T(8,128)S(1)}, f32[8,128]{1,0:T(8,128)S(1)}, u32[]{:S(2)}, u32[]{:S(2)}) collective-permute-start(f32[8,128]{1,0:T(8,128)S(1)} %add.11.one_ref), channel_id=1, source_target_pairs={{0,8},{4,12},{8,0},{12,4},{1,9},{5,13},{9,1},{13,5},{2,10},{6,14},... | collective-permute-start | bytes 12296 | tf_op jit(solution)/shard_map/ppermute | solution.py:309

commit v4 on v3

--- a/solution.py
+++ b/solution.py
@@ -300,13 +300,13 @@
             name="finish",
         )(res, factor_p, factor_q, vel_dense)
 
-        got = flipped(total, 1)
-        total = total + got
-        got = flipped(total, 2)
+        total = total + flipped(total, 1)
+        got = flipped(total, 3)
         flip = 1
         while flip < body_count:
             total = total + got
-            got = lax.ppermute(total, "body", [(i, i ^ flip) for i in range(body_count)])
+            pairs = [(4 * i + j, 4 * (i ^ flip) + (j ^ 1)) for i in range(body_count) for j in range(4)]
+            got = lax.ppermute(total, ("body", "harm"), pairs)
             flip *= 2
         rms = pl.pallas_call(
             functools.partial(rms_kernel, 1.0 / (2.0 * H * everyone * reals)),

time: 59.2 us -> 57.5 us (0.971)
  waiting for transfers between devices: 25 us -> 24 us
  starting transfers between devices: 19.1 us -> 18.4 us
    ppermute x2, waiting for transfers between devices: 3.62 us -> 2.93 us  [local(): got = lax.ppermute(total, ('body', 'harm'), pairs)]
where the time goes in v4:
time: 57.5 us; the launch traced here: 57.2 us
  waiting for transfers between devices  24 us (42%)
  starting transfers between devices  18.4 us (32%)
  Pallas kernels  11.3 us (20%)
  local copies, waits for them, and re-layouts  2.66 us (5%)
  between operations  0.81 us (1%)
    ppermute x1, waiting for transfers between devices, gather_line(): outer = lax.ppermute(cross, axis, [(1, 0), (2, 3)])  9.84 us
    ppermute x7, waiting for transfers between devices, flipped(): return lax.ppermute(x, 'harm', [(i, i ^ flip) for i in range(4)])  6.71 us
    ppermute x1, starting transfers between devices, gather_line(): near = lax.ppermute(x, axis, [(0, 1), (1, 0), (2, 3), (3, 2)])  6.01 us
    pallas_call x1, Pallas kernels, local(): pl.pallas_call(functools.partial(time_kernel, harm, bodies, reals), grid=...  4.77 us
    ppermute x1, waiting for transfers between devices, gather_line(): near = lax.ppermute(x, axis, [(0, 1), (1, 0), (2, 3), (3, 2)])  4.5 us
    ppermute x7, starting transfers between devices, flipped(): return lax.ppermute(x, 'harm', [(i, i ^ flip) for i in range(4)])  4 us
    ppermute x1, starting transfers between devices, gather_line(): across = lax.ppermute(again, axis, [(0, 3), (3, 0)])  3.25 us
    ppermute x2, waiting for transfers between devices, local(): got = lax.ppermute(total, ('body', 'harm'), pairs)  2.93 us
  transfers between devices with their start and end apart: 14, of which 8 were waited for; matrix products, arithmetic and copies ran while one was open for 0% of the time, Pallas kernels for 16%

profile of v4, /device:TPU:0, one launch (start us, length us, event | category | flops | bytes accessed | tf_op | source)
XLA Modules:
  0.0 57.2 jit_solution(6287519024789345421)
XLA Ops:
  0.6 0.0 copy-start.6
  0.6 0.0 copy-start.7
  0.7 0.0 copy-start
  0.7 1.6 %copy-done = f32[2,32,64,64]{3,2,1,0:T(8,128)S(1)} copy-done((f32[2,32,64,64]{3,2,1,0:T(8,128)S(1)}, f32[2,32,64,64]{3,2,1,0:T(8,128)}, u32[]{:S(2)}) %copy-start) | copy-done | bytes 1048600
  2.3 0.2 pack_couple.1.refs_0_
  2.5 0.0 copy-start.1
  2.5 0.0 copy-start.2
  2.5 0.8 %collective-permute-start.1 = (bf16[2048,128]{1,0:T(8,128)(2,1)S(1)}, bf16[2048,128]{1,0:T(8,128)(2,1)S(1)}, u32[]{:S(2)}, u32[]{:S(2)}) collective-permute-start(bf16[2048,128]{1,0:T(8,128)(2,1)S(1)} %pack_couple.1.refs_0_), channel_id=1, source_target_pairs={{4,8},{8,4},{5,9},{9,5},{6,10},{10,6},{7,11},{11,7},{20,24},{24,20... | collective-permute-start | bytes 1572872 | tf_op jit(solution)/shard_map/ppermute | solution.py:195
  3.3 6.0 %collective-permute-start = (bf16[2048,128]{1,0:T(8,128)(2,1)S(1)}, bf16[2048,128]{1,0:T(8,128)(2,1)S(1)}, u32[]{:S(2)}, u32[]{:S(2)}) collective-permute-start(bf16[2048,128]{1,0:T(8,128)(2,1)S(1)} %pack_couple.1.refs_0_), channel_id=1, source_target_pairs={{0,4},{4,0},{8,12},{12,8},{1,5},{5,1},{9,13},{13,9},{2,6},{6,2},{1... | collective-permute-start | bytes 1572872 | tf_op jit(solution)/shard_map/ppermute | solution.py:194
  9.3 1.3 %pack_time.1 = (bf16[64,2048]{1,0:T(8,128)(2,1)S(1)}, bf16[64,2048]{1,0:T(8,128)(2,1)S(1)}, bf16[2048,128]{1,0:T(8,128)(2,1)S(1)}) custom-call(f32[4096,64]{1,0:T(8,128)S(1)} %bitcast.4), custom_call_target="tpu_custom_call" | custom-call | bytes 1024 | tf_op jit(solution)/shard_map/pack_time/pallas_call | solution.py:234
  10.7 0.1 collective-permute-start.5
  10.8 1.6 %collective-permute-start.6 = (bf16[64,2048]{1,0:T(8,128)(2,1)S(1)}, bf16[64,2048]{1,0:T(8,128)(2,1)S(1)}, u32[]{:S(2)}, u32[]{:S(2)}) collective-permute-start(bf16[64,2048]{1,0:T(8,128)(2,1)S(1)} %get-tuple-element.15.own_ref), channel_id=1, source_target_pairs={{0,2},{1,3},{2,0},{3,1},{4,6},{5,7},{6,4},{7,5},{8,10},{9,11},{10,... | collective-permute-start | bytes 786440 | tf_op jit(solution)/shard_map/ppermute | solution.py:224
  12.4 0.3 collective-permute-start.7
  12.6 0.0 collective-permute-done.5.core_ref
  12.6 3.2 %collective-permute-start.2 = (bf16[2048,128]{1,0:T(8,128)(2,1)S(1)}, bf16[2048,128]{1,0:T(8,128)(2,1)S(1)}, u32[]{:S(2)}, u32[]{:S(2)}) collective-permute-start(bf16[2048,128]{1,0:T(8,128)(2,1)S(1)} %get-tuple-element.14), channel_id=1, source_target_pairs={{0,12},{12,0},{1,13},{13,1},{2,14},{14,2},{3,15},{15,3},{16,28},{2... | collective-permute-start | bytes 1572872 | tf_op jit(solution)/shard_map/ppermute | solution.py:196
  15.9 0.0 collective-permute-done.1.refs_2_
  15.9 1.3 %collective-permute-start.3 = (bf16[2048,128]{1,0:T(8,128)(2,1)S(1)}, bf16[2048,128]{1,0:T(8,128)(2,1)S(1)}, u32[]{:S(2)}, u32[]{:S(2)}) collective-permute-start(bf16[2048,128]{1,0:T(8,128)(2,1)S(1)} %collective-permute-done.1.refs_2_), channel_id=1, source_target_pairs={{4,0},{8,12},{5,1},{9,13},{6,2},{10,14},{7,3},{11,15},{20,16},{24,... | collective-permute-start | bytes 1572872 | tf_op jit(solution)/shard_map/ppermute | solution.py:197
  17.2 4.5 %collective-permute-done.refs_1_ = bf16[2048,128]{1,0:T(8,128)(2,1)S(1)} collective-permute-done((bf16[2048,128]{1,0:T(8,128)(2,1)S(1)}, bf16[2048,128]{1,0:T(8,128)(2,1)S(1)}, u32[]{:S(2)}, u32[]{:S(2)}) %collective-permute-start) | collective-permute-done | bytes 524320 | tf_op jit(solution)/shard_map/ppermute | solution.py:194
  21.7 0.7 %collective-permute-start.4 = (bf16[2048,128]{1,0:T(8,128)(2,1)S(1)}, bf16[2048,128]{1,0:T(8,128)(2,1)S(1)}, u32[]{:S(2)}, u32[]{:S(2)}) collective-permute-start(bf16[2048,128]{1,0:T(8,128)(2,1)S(1)} %collective-permute-done.refs_1_), channel_id=1, source_target_pairs={{4,8},{8,4},{5,9},{9,5},{6,10},{10,6},{7,11},{11,7},{20,24},{24,20... | collective-permute-start | bytes 1572872 | tf_op jit(solution)/shard_map/ppermute | solution.py:198
  22.4 0.0 collective-permute-done.6.far_ref
  22.4 2.3 %collective-permute-done.7.far_core_ref = bf16[64,2048]{1,0:T(8,128)(2,1)S(1)} collective-permute-done((bf16[64,2048]{1,0:T(8,128)(2,1)S(1)}, bf16[64,2048]{1,0:T(8,128)(2,1)S(1)}, u32[]{:S(2)}, u32[]{:S(2)}) %collective-permute-start.7) | collective-permute-done | bytes 262176 | tf_op jit(solution)/shard_map/ppermute | solution.py:224
  24.7 0.0 copy-done.6
  24.7 0.0 copy-done.7
  24.7 0.0 copy-done.4
  24.7 0.0 copy-start.5
  24.7 1.0 %copy-done.5 = bf16[512,512]{1,0:T(8,128)(2,1)S(1)} copy-done((bf16[512,512]{1,0:T(8,128)(2,1)S(1)}, bf16[512,512]{1,0:T(8,128)(2,1)}, u32[]{:S(2)}) %copy-start.5) | copy-done | bytes 524312
  25.7 4.8 %time_kernel.1 = (f32[72,2048]{1,0:T(8,128)S(1)}, f32[32,2048]{1,0:T(8,128)S(1)}, f32[40,2048]{1,0:T(8,128)S(1)}) custom-call(f32[64]{0:T(128)S(1)} %copy-done.6, f32[64]{0:T(128)S(1)} %copy-done.7, bf16[64,2048]{1,0:T(8,128)(2,1)S(1)} %get-tuple-element.15.own_ref, bf16[64,2048]{1,0:T(8,128)(2,1)S(1)} %collective-permute-done.5.core_ref, ...), custom_call_target="tpu_custom_call" | custom-call | bytes 1024 | tf_op jit(solution)/shard_map/time_kernel/pallas_call | solution.py:257
  30.5 0.6 %collective-permute-start.9 = (f32[40,2048]{1,0:T(8,128)S(1)}, f32[40,2048]{1,0:T(8,128)S(1)}, u32[]{:S(2)}, u32[]{:S(2)}) collective-permute-start(f32[40,2048]{1,0:T(8,128)S(1)} %get-tuple-element.19), channel_id=1, source_target_pairs={{0,1},{1,0},{2,3},{3,2},{4,5},{5,4},{6,7},{7,6},{8,9},{9,8},{10,11... | collective-permute-start | bytes 983048 | tf_op jit(solution)/shard_map/ppermute | solution.py:224
  31.1 0.1 collective-permute-start.8
  31.2 1.6 %collective-permute-done.8.other_re_ref = f32[32,2048]{1,0:T(8,128)S(1)} collective-permute-done((f32[32,2048]{1,0:T(8,128)S(1)}, f32[32,2048]{1,0:T(8,128)S(1)}, u32[]{:S(2)}, u32[]{:S(2)}) %collective-permute-start.8) | collective-permute-done | bytes 262176 | tf_op jit(solution)/shard_map/ppermute | solution.py:224
  32.8 0.0 collective-permute-done.9.other_im_ref
  32.8 0.0 copy-done.3
  32.8 0.0 copy-done.1
  32.8 1.6 %prepare.1 = (f32[2048,128]{1,0:T(8,128)S(1)}, f32[2048,128]{1,0:T(8,128)S(1)}, f32[2048,128]{1,0:T(8,128)S(1)}, f32[2048,128]{1,0:T(8,128)S(1)}) custom-call(bf16[2,32,64,256]{3,2,1,0:T(8,128)(2,1)S(1)} %copy-done.2, f32[72,2048]{1,0:T(8,128)S(1)} %get-tuple-element.17.mine_ref, f32[32,2048]{1,0:T(8,128)S(1)} %collective-permute-done.8.other_re_ref, ...), custom_call_target="tpu_custom_call" | custom-call | bytes 1024 | tf_op jit(solution)/shard_map/prepare/pallas_call | solution.py:270
  34.4 0.0 collective-permute-done.2.refs_3_
  34.4 9.8 %collective-permute-done.3.refs_4_ = bf16[2048,128]{1,0:T(8,128)(2,1)S(1)} collective-permute-done((bf16[2048,128]{1,0:T(8,128)(2,1)S(1)}, bf16[2048,128]{1,0:T(8,128)(2,1)S(1)}, u32[]{:S(2)}, u32[]{:S(2)}) %collective-permute-start.3) | collective-permute-done | bytes 524320 | tf_op jit(solution)/shard_map/ppermute | solution.py:197
  44.2 0.0 collective-permute-done.4.refs_5_
  44.2 1.2 %couple.1 = (f32[2048,128]{1,0:T(8,128)S(1)}, f32[8,128]{1,0:T(8,128)S(1)}) custom-call(bf16[2,32,64,256]{3,2,1,0:T(8,128)(2,1)S(1)} %copy-done.2, bf16[2048,128]{1,0:T(8,128)(2,1)S(1)} %pack_couple.1.refs_0_, bf16[2048,128]{1,0:T(8,128)(2,1)S(1)} %collective-permute-done.refs_1_, bf16[2048,128]{1,0:T(8,128)(2,1)S(1)} %collective-permute-done.1.refs_2_, ...), custom_call_target="tpu_custom_call" | custom-call | bytes 1024 | tf_op jit(solution)/shard_map/couple/pallas_call | solution.py:280
  45.4 0.1 collective-permute-start.10
  45.5 1.2 %collective-permute-done.10 = f32[8,128]{1,0:T(8,128)S(1)} collective-permute-done((f32[8,128]{1,0:T(8,128)S(1)}, f32[8,128]{1,0:T(8,128)S(1)}, u32[]{:S(2)}, u32[]{:S(2)}) %collective-permute-start.10) | collective-permute-done | bytes 4128 | tf_op jit(solution)/shard_map/ppermute | solution.py:224
  46.6 1.3 %collective-permute-start.11 = (f32[8,128]{1,0:T(8,128)S(1)}, f32[8,128]{1,0:T(8,128)S(1)}, u32[]{:S(2)}, u32[]{:S(2)}) collective-permute-start(f32[8,128]{1,0:T(8,128)S(1)} %add.9), channel_id=1, source_target_pairs={{0,3},{1,2},{2,1},{3,0},{4,7},{5,6},{6,5},{7,4},{8,11},{9,10},{10,... | collective-permute-start | bytes 12296 | tf_op jit(solution)/shard_map/ppermute | solution.py:224
  47.9 1.8 %collective-permute-done.11 = f32[8,128]{1,0:T(8,128)S(1)} collective-permute-done((f32[8,128]{1,0:T(8,128)S(1)}, f32[8,128]{1,0:T(8,128)S(1)}, u32[]{:S(2)}, u32[]{:S(2)}) %collective-permute-start.11) | collective-permute-done | bytes 4128 | tf_op jit(solution)/shard_map/ppermute | solution.py:224
  49.7 0.7 %collective-permute-start.12 = (f32[8,128]{1,0:T(8,128)S(1)}, f32[8,128]{1,0:T(8,128)S(1)}, u32[]{:S(2)}, u32[]{:S(2)}) collective-permute-start(f32[8,128]{1,0:T(8,128)S(1)} %add.10), channel_id=1, source_target_pairs={{0,5},{1,4},{2,7},{3,6},{4,1},{5,0},{6,3},{7,2},{8,13},{9,12},{10,... | collective-permute-start | bytes 12296 | tf_op jit(solution)/shard_map/ppermute | solution.py:309
  50.4 2.3 %collective-permute-done.12 = f32[8,128]{1,0:T(8,128)S(1)} collective-permute-done((f32[8,128]{1,0:T(8,128)S(1)}, f32[8,128]{1,0:T(8,128)S(1)}, u32[]{:S(2)}, u32[]{:S(2)}) %collective-permute-start.12) | collective-permute-done | bytes 4128 | tf_op jit(solution)/shard_map/ppermute | solution.py:309
  52.7 1.7 %collective-permute-start.13 = (f32[8,128]{1,0:T(8,128)S(1)}, f32[8,128]{1,0:T(8,128)S(1)}, u32[]{:S(2)}, u32[]{:S(2)}) collective-permute-start(f32[8,128]{1,0:T(8,128)S(1)} %add.11.one_ref), channel_id=1, source_target_pairs={{0,9},{1,8},{2,11},{3,10},{4,13},{5,12},{6,15},{7,14},{8,1},{9,0},... | collective-permute-start | bytes 12296 | tf_op jit(solution)/shard_map/ppermute | solution.py:309
  54.4 1.7 %finish.1 = f32[2,2048,64]{2,1,0:T(8,128)} custom-call(f32[2048,128]{1,0:T(8,128)S(1)} %get-tuple-element.21.res_ref, f32[2048,128]{1,0:T(8,128)S(1)} %get-tuple-element.22.p_ref, f32[2048,128]{1,0:T(8,128)S(1)} %get-tuple-element.23.q_ref, f32[2048,128]{1,0:T(8,128)S(1)} %get-tuple-element.24.vel_ref), custom_call_target="tpu_custom_call" | custom-call | bytes 1024 | tf_op jit(solution)/shard_map/finish/pallas_call | solution.py:292
  56.0 0.6 %collective-permute-done.13.two_ref = f32[8,128]{1,0:T(8,128)S(1)} collective-permute-done((f32[8,128]{1,0:T(8,128)S(1)}, f32[8,128]{1,0:T(8,128)S(1)}, u32[]{:S(2)}, u32[]{:S(2)}) %collective-permute-start.13) | collective-permute-done | bytes 4128 | tf_op jit(solution)/shard_map/ppermute | solution.py:309
  56.6 0.6 rms.1
  (6 shorter events, 0.0 us)
Async XLA Ops:
  0.6 24.0 %copy-start.6 = (f32[64]{0:T(128)S(1)}, f32[64]{0:T(128)}, u32[]{:S(2)}) copy-start(f32[64]{0:T(128)} %quad_ref.1) | copy-start | bytes 772
  0.6 24.0 %copy-start.7 = (f32[64]{0:T(128)S(1)}, f32[64]{0:T(128)}, u32[]{:S(2)}) copy-start(f32[64]{0:T(128)} %coul_ref.1) | copy-start | bytes 772
  0.7 1.6 %copy-start = (f32[2,32,64,64]{3,2,1,0:T(8,128)S(1)}, f32[2,32,64,64]{3,2,1,0:T(8,128)}, u32[]{:S(2)}) copy-start(f32[2,32,64,64]{3,2,1,0:T(8,128)} %param.7) | copy-start | bytes 3145732
  2.3 22.4 %copy-start.4 = (bf16[256,1536]{1,0:T(8,128)(2,1)S(1)}, bf16[256,1536]{1,0:T(8,128)(2,1)}, u32[]{:S(2)}) copy-start(bf16[256,1536]{1,0:T(8,128)(2,1)} %constant.5.clone.inv_ref) | copy-start | bytes 2359300
  2.3 30.5 %copy-start.3 = (f32[2,32,64,64]{3,2,1,0:T(8,128)S(1)}, f32[2,32,64,64]{3,2,1,0:T(8,128)}, u32[]{:S(2)}) copy-start(f32[2,32,64,64]{3,2,1,0:T(8,128)} %param.9) | copy-start | bytes 3145732
  2.5 30.3 %copy-start.1 = (f32[2,32,64,64]{3,2,1,0:T(8,128)S(1)}, f32[2,32,64,64]{3,2,1,0:T(8,128)}, u32[]{:S(2)}) copy-start(f32[2,32,64,64]{3,2,1,0:T(8,128)} %param.7) | copy-start | bytes 3145732
  2.5 30.3 %copy-start.2 = (bf16[2,32,64,256]{3,2,1,0:T(8,128)(2,1)S(1)}, bf16[2,32,64,256]{3,2,1,0:T(8,128)(2,1)}, u32[]{:S(2)}) copy-start(bf16[2,32,64,256]{3,2,1,0:T(8,128)(2,1)} %imped_ref.3) | copy-start | bytes 6291460
  2.5 13.4 %collective-permute-start.1 = (bf16[2048,128]{1,0:T(8,128)(2,1)S(1)}, bf16[2048,128]{1,0:T(8,128)(2,1)S(1)}, u32[]{:S(2)}, u32[]{:S(2)}) collective-permute-start(bf16[2048,128]{1,0:T(8,128)(2,1)S(1)} %pack_couple.1.refs_0_), channel_id=1, source_target_pairs={{4,8},{8,4},{5,9},{9,5},{6,10},{10,6},{7,11},{11,7},{20,24},{24,20... | collective-permute-start | bytes 1572872 | tf_op jit(solution)/shard_map/ppermute | solution.py:195
  3.3 18.4 %collective-permute-start = (bf16[2048,128]{1,0:T(8,128)(2,1)S(1)}, bf16[2048,128]{1,0:T(8,128)(2,1)S(1)}, u32[]{:S(2)}, u32[]{:S(2)}) collective-permute-start(bf16[2048,128]{1,0:T(8,128)(2,1)S(1)} %pack_couple.1.refs_0_), channel_id=1, source_target_pairs={{0,4},{4,0},{8,12},{12,8},{1,5},{5,1},{9,13},{13,9},{2,6},{6,2},{1... | collective-permute-start | bytes 1572872 | tf_op jit(solution)/shard_map/ppermute | solution.py:194
  10.7 1.9 %collective-permute-start.5 = (bf16[64,2048]{1,0:T(8,128)(2,1)S(1)}, bf16[64,2048]{1,0:T(8,128)(2,1)S(1)}, u32[]{:S(2)}, u32[]{:S(2)}) collective-permute-start(bf16[64,2048]{1,0:T(8,128)(2,1)S(1)} %get-tuple-element.16), channel_id=1, source_target_pairs={{0,1},{1,0},{2,3},{3,2},{4,5},{5,4},{6,7},{7,6},{8,9},{9,8},{10,11... | collective-permute-start | bytes 786440 | tf_op jit(solution)/shard_map/ppermute | solution.py:224
  10.8 11.6 %collective-permute-start.6 = (bf16[64,2048]{1,0:T(8,128)(2,1)S(1)}, bf16[64,2048]{1,0:T(8,128)(2,1)S(1)}, u32[]{:S(2)}, u32[]{:S(2)}) collective-permute-start(bf16[64,2048]{1,0:T(8,128)(2,1)S(1)} %get-tuple-element.15.own_ref), channel_id=1, source_target_pairs={{0,2},{1,3},{2,0},{3,1},{4,6},{5,7},{6,4},{7,5},{8,10},{9,11},{10,... | collective-permute-start | bytes 786440 | tf_op jit(solution)/shard_map/ppermute | solution.py:224
  12.4 12.3 %collective-permute-start.7 = (bf16[64,2048]{1,0:T(8,128)(2,1)S(1)}, bf16[64,2048]{1,0:T(8,128)(2,1)S(1)}, u32[]{:S(2)}, u32[]{:S(2)}) collective-permute-start(bf16[64,2048]{1,0:T(8,128)(2,1)S(1)} %get-tuple-element.16), channel_id=1, source_target_pairs={{0,3},{1,2},{2,1},{3,0},{4,7},{5,6},{6,5},{7,4},{8,11},{9,10},{10,... | collective-permute-start | bytes 786440 | tf_op jit(solution)/shard_map/ppermute | solution.py:224
  12.6 21.8 %collective-permute-start.2 = (bf16[2048,128]{1,0:T(8,128)(2,1)S(1)}, bf16[2048,128]{1,0:T(8,128)(2,1)S(1)}, u32[]{:S(2)}, u32[]{:S(2)}) collective-permute-start(bf16[2048,128]{1,0:T(8,128)(2,1)S(1)} %get-tuple-element.14), channel_id=1, source_target_pairs={{0,12},{12,0},{1,13},{13,1},{2,14},{14,2},{3,15},{15,3},{16,28},{2... | collective-permute-start | bytes 1572872 | tf_op jit(solution)/shard_map/ppermute | solution.py:196
  15.9 28.3 %collective-permute-start.3 = (bf16[2048,128]{1,0:T(8,128)(2,1)S(1)}, bf16[2048,128]{1,0:T(8,128)(2,1)S(1)}, u32[]{:S(2)}, u32[]{:S(2)}) collective-permute-start(bf16[2048,128]{1,0:T(8,128)(2,1)S(1)} %collective-permute-done.1.refs_2_), channel_id=1, source_target_pairs={{4,0},{8,12},{5,1},{9,13},{6,2},{10,14},{7,3},{11,15},{20,16},{24,... | collective-permute-start | bytes 1572872 | tf_op jit(solution)/shard_map/ppermute | solution.py:197
  21.7 22.5 %collective-permute-start.4 = (bf16[2048,128]{1,0:T(8,128)(2,1)S(1)}, bf16[2048,128]{1,0:T(8,128)(2,1)S(1)}, u32[]{:S(2)}, u32[]{:S(2)}) collective-permute-start(bf16[2048,128]{1,0:T(8,128)(2,1)S(1)} %collective-permute-done.refs_1_), channel_id=1, source_target_pairs={{4,8},{8,4},{5,9},{9,5},{6,10},{10,6},{7,11},{11,7},{20,24},{24,20... | collective-permute-start | bytes 1572872 | tf_op jit(solution)/shard_map/ppermute | solution.py:198
  24.7 1.0 %copy-start.5 = (bf16[512,512]{1,0:T(8,128)(2,1)S(1)}, bf16[512,512]{1,0:T(8,128)(2,1)}, u32[]{:S(2)}) copy-start(bf16[512,512]{1,0:T(8,128)(2,1)} %constant.4.clone.fwd_ref) | copy-start | bytes 1572868
  30.5 2.3 %collective-permute-start.9 = (f32[40,2048]{1,0:T(8,128)S(1)}, f32[40,2048]{1,0:T(8,128)S(1)}, u32[]{:S(2)}, u32[]{:S(2)}) collective-permute-start(f32[40,2048]{1,0:T(8,128)S(1)} %get-tuple-element.19), channel_id=1, source_target_pairs={{0,1},{1,0},{2,3},{3,2},{4,5},{5,4},{6,7},{7,6},{8,9},{9,8},{10,11... | collective-permute-start | bytes 983048 | tf_op jit(solution)/shard_map/ppermute | solution.py:224
  31.1 1.6 %collective-permute-start.8 = (f32[32,2048]{1,0:T(8,128)S(1)}, f32[32,2048]{1,0:T(8,128)S(1)}, u32[]{:S(2)}, u32[]{:S(2)}) collective-permute-start(f32[32,2048]{1,0:T(8,128)S(1)} %get-tuple-element.18), channel_id=1, source_target_pairs={{0,1},{1,0},{2,3},{3,2},{4,5},{5,4},{6,7},{7,6},{8,9},{9,8},{10,11... | collective-permute-start | bytes 786440 | tf_op jit(solution)/shard_map/ppermute | solution.py:224
  45.4 1.2 %collective-permute-start.10 = (f32[8,128]{1,0:T(8,128)S(1)}, f32[8,128]{1,0:T(8,128)S(1)}, u32[]{:S(2)}, u32[]{:S(2)}) collective-permute-start(f32[8,128]{1,0:T(8,128)S(1)} %get-tuple-element.25), channel_id=1, source_target_pairs={{0,1},{1,0},{2,3},{3,2},{4,5},{5,4},{6,7},{7,6},{8,9},{9,8},{10,11... | collective-permute-start | bytes 12296 | tf_op jit(solution)/shard_map/ppermute | solution.py:224
  46.6 3.0 %collective-permute-start.11 = (f32[8,128]{1,0:T(8,128)S(1)}, f32[8,128]{1,0:T(8,128)S(1)}, u32[]{:S(2)}, u32[]{:S(2)}) collective-permute-start(f32[8,128]{1,0:T(8,128)S(1)} %add.9), channel_id=1, source_target_pairs={{0,3},{1,2},{2,1},{3,0},{4,7},{5,6},{6,5},{7,4},{8,11},{9,10},{10,... | collective-permute-start | bytes 12296 | tf_op jit(solution)/shard_map/ppermute | solution.py:224
  49.7 3.0 %collective-permute-start.12 = (f32[8,128]{1,0:T(8,128)S(1)}, f32[8,128]{1,0:T(8,128)S(1)}, u32[]{:S(2)}, u32[]{:S(2)}) collective-permute-start(f32[8,128]{1,0:T(8,128)S(1)} %add.10), channel_id=1, source_target_pairs={{0,5},{1,4},{2,7},{3,6},{4,1},{5,0},{6,3},{7,2},{8,13},{9,12},{10,... | collective-permute-start | bytes 12296 | tf_op jit(solution)/shard_map/ppermute | solution.py:309
  52.7 3.9 %collective-permute-start.13 = (f32[8,128]{1,0:T(8,128)S(1)}, f32[8,128]{1,0:T(8,128)S(1)}, u32[]{:S(2)}, u32[]{:S(2)}) collective-permute-start(f32[8,128]{1,0:T(8,128)S(1)} %add.11.one_ref), channel_id=1, source_target_pairs={{0,9},{1,8},{2,11},{3,10},{4,13},{5,12},{6,15},{7,14},{8,1},{9,0},... | collective-permute-start | bytes 12296 | tf_op jit(solution)/shard_map/ppermute | solution.py:309

commit v5 on v4

--- a/solution.py
+++ b/solution.py
@@ -185,8 +185,9 @@
     out_ref[1] = new[:, reals:]
 
 
-def rms_kernel(scale, one_ref, two_ref, out_ref):
-    mean = (one_ref[...] + two_ref[...]) * scale
+def rms_kernel(scale, *refs):
+    *parts, out_ref = refs
+    mean = sum(part[...] for part in parts) * scale
     out_ref[0] = jnp.sqrt(mean)[0, 0]
 
 
@@ -301,21 +302,23 @@
         )(res, factor_p, factor_q, vel_dense)
 
         total = total + flipped(total, 1)
-        got = flipped(total, 3)
-        flip = 1
-        while flip < body_count:
-            total = total + got
+        total = total + flipped(total, 3)
+
+        def crossed(flip):
             pairs = [(4 * i + j, 4 * (i ^ flip) + (j ^ 1)) for i in range(body_count) for j in range(4)]
-            got = lax.ppermute(total, ("body", "harm"), pairs)
-            flip *= 2
+            return lax.ppermute(total, ("body", "harm"), pairs)
+
+        for bit in range(2, body_count.bit_length() - 1):
+            total = total + crossed(1 << bit)
+        got = [crossed(flip) for flip in (3, 2, 1)]
         rms = pl.pallas_call(
             functools.partial(rms_kernel, 1.0 / (2.0 * H * everyone * reals)),
-            in_specs=[VMEM] * 2,
+            in_specs=[VMEM] * (1 + len(got)),
             out_specs=SMEM,
             out_shape=jax.ShapeDtypeStruct((1,), F32),
             compiler_params=params(),
             name="rms",
-        )(total, got)
+        )(total, *got)
         return new.reshape(vel.shape), rms
 
     return local

time: 57.5 us -> 56.4 us (0.981)
  waiting for transfers between devices: 24 us -> 21.4 us
  starting transfers between devices: 18.4 us -> 19.9 us
    ppermute x2 -> x3, waiting for transfers between devices: 2.93 us -> 0.35 us  [crossed(): return lax.ppermute(total, ('body', 'harm'), pairs)]
    ppermute x2 -> x3, starting transfers between devices: 2.38 us -> 3.88 us  [crossed(): return lax.ppermute(total, ('body', 'harm'), pairs)]
  transfers between devices with their start and end apart: 14 -> 15, of which waited for: 8 -> 7; matrix products, arithmetic and copies ran while one was open for 0% -> 0% of each run, Pallas kernels for 16% -> 17%
where the time goes in v5:
time: 56.4 us; the launch traced here: 56.1 us
  waiting for transfers between devices  21.4 us (38%)
  starting transfers between devices  19.9 us (35%)
  Pallas kernels  11.3 us (20%)
  local copies, waits for them, and re-layouts  2.66 us (5%)
  between operations  0.81 us (1%)
    ppermute x1, waiting for transfers between devices, gather_line(): outer = lax.ppermute(cross, axis, [(1, 0), (2, 3)])  9.84 us
    ppermute x7, waiting for transfers between devices, flipped(): return lax.ppermute(x, 'harm', [(i, i ^ flip) for i in range(4)])  6.71 us
    ppermute x1, starting transfers between devices, gather_line(): near = lax.ppermute(x, axis, [(0, 1), (1, 0), (2, 3), (3, 2)])  6.01 us
    pallas_call x1, Pallas kernels, local(): pl.pallas_call(functools.partial(time_kernel, harm, bodies, reals), grid=...  4.77 us
    ppermute x1, waiting for transfers between devices, gather_line(): near = lax.ppermute(x, axis, [(0, 1), (1, 0), (2, 3), (3, 2)])  4.5 us
    ppermute x7, starting transfers between devices, flipped(): return lax.ppermute(x, 'harm', [(i, i ^ flip) for i in range(4)])  4 us
    ppermute x3, starting transfers between devices, crossed(): return lax.ppermute(total, ('body', 'harm'), pairs)  3.88 us
    ppermute x1, starting transfers between devices, gather_line(): across = lax.ppermute(again, axis, [(0, 3), (3, 0)])  3.25 us
  transfers between devices with their start and end apart: 15, of which 7 were waited for; matrix products, arithmetic and copies ran while one was open for 0% of the time, Pallas kernels for 17%

profile of v5, /device:TPU:0, one launch (start us, length us, event | category | flops | bytes accessed | tf_op | source)
XLA Modules:
  0.0 56.1 jit_solution(4800269141105223963)
XLA Ops:
  0.6 0.0 copy-start.6
  0.6 0.0 copy-start.7
  0.7 0.0 copy-start
  0.7 1.6 %copy-done = f32[2,32,64,64]{3,2,1,0:T(8,128)S(1)} copy-done((f32[2,32,64,64]{3,2,1,0:T(8,128)S(1)}, f32[2,32,64,64]{3,2,1,0:T(8,128)}, u32[]{:S(2)}) %copy-start) | copy-done | bytes 1048600
  2.3 0.2 pack_couple.1.refs_0_
  2.5 0.0 copy-start.1
  2.5 0.0 copy-start.2
  2.5 0.8 %collective-permute-start.1 = (bf16[2048,128]{1,0:T(8,128)(2,1)S(1)}, bf16[2048,128]{1,0:T(8,128)(2,1)S(1)}, u32[]{:S(2)}, u32[]{:S(2)}) collective-permute-start(bf16[2048,128]{1,0:T(8,128)(2,1)S(1)} %pack_couple.1.refs_0_), channel_id=1, source_target_pairs={{4,8},{8,4},{5,9},{9,5},{6,10},{10,6},{7,11},{11,7},{20,24},{24,20... | collective-permute-start | bytes 1572872 | tf_op jit(solution)/shard_map/ppermute | solution.py:196
  3.3 6.0 %collective-permute-start = (bf16[2048,128]{1,0:T(8,128)(2,1)S(1)}, bf16[2048,128]{1,0:T(8,128)(2,1)S(1)}, u32[]{:S(2)}, u32[]{:S(2)}) collective-permute-start(bf16[2048,128]{1,0:T(8,128)(2,1)S(1)} %pack_couple.1.refs_0_), channel_id=1, source_target_pairs={{0,4},{4,0},{8,12},{12,8},{1,5},{5,1},{9,13},{13,9},{2,6},{6,2},{1... | collective-permute-start | bytes 1572872 | tf_op jit(solution)/shard_map/ppermute | solution.py:195
  9.3 1.3 %pack_time.1 = (bf16[64,2048]{1,0:T(8,128)(2,1)S(1)}, bf16[64,2048]{1,0:T(8,128)(2,1)S(1)}, bf16[2048,128]{1,0:T(8,128)(2,1)S(1)}) custom-call(f32[4096,64]{1,0:T(8,128)S(1)} %bitcast.4), custom_call_target="tpu_custom_call" | custom-call | bytes 1024 | tf_op jit(solution)/shard_map/pack_time/pallas_call | solution.py:235
  10.7 0.1 collective-permute-start.5
  10.8 1.6 %collective-permute-start.6 = (bf16[64,2048]{1,0:T(8,128)(2,1)S(1)}, bf16[64,2048]{1,0:T(8,128)(2,1)S(1)}, u32[]{:S(2)}, u32[]{:S(2)}) collective-permute-start(bf16[64,2048]{1,0:T(8,128)(2,1)S(1)} %get-tuple-element.15.own_ref), channel_id=1, source_target_pairs={{0,2},{1,3},{2,0},{3,1},{4,6},{5,7},{6,4},{7,5},{8,10},{9,11},{10,... | collective-permute-start | bytes 786440 | tf_op jit(solution)/shard_map/ppermute | solution.py:225
  12.4 0.3 collective-permute-start.7
  12.6 0.0 collective-permute-done.5.core_ref
  12.6 3.2 %collective-permute-start.2 = (bf16[2048,128]{1,0:T(8,128)(2,1)S(1)}, bf16[2048,128]{1,0:T(8,128)(2,1)S(1)}, u32[]{:S(2)}, u32[]{:S(2)}) collective-permute-start(bf16[2048,128]{1,0:T(8,128)(2,1)S(1)} %get-tuple-element.14), channel_id=1, source_target_pairs={{0,12},{12,0},{1,13},{13,1},{2,14},{14,2},{3,15},{15,3},{16,28},{2... | collective-permute-start | bytes 1572872 | tf_op jit(solution)/shard_map/ppermute | solution.py:197
  15.9 0.0 collective-permute-done.1.refs_2_
  15.9 1.3 %collective-permute-start.3 = (bf16[2048,128]{1,0:T(8,128)(2,1)S(1)}, bf16[2048,128]{1,0:T(8,128)(2,1)S(1)}, u32[]{:S(2)}, u32[]{:S(2)}) collective-permute-start(bf16[2048,128]{1,0:T(8,128)(2,1)S(1)} %collective-permute-done.1.refs_2_), channel_id=1, source_target_pairs={{4,0},{8,12},{5,1},{9,13},{6,2},{10,14},{7,3},{11,15},{20,16},{24,... | collective-permute-start | bytes 1572872 | tf_op jit(solution)/shard_map/ppermute | solution.py:198
  17.2 4.5 %collective-permute-done.refs_1_ = bf16[2048,128]{1,0:T(8,128)(2,1)S(1)} collective-permute-done((bf16[2048,128]{1,0:T(8,128)(2,1)S(1)}, bf16[2048,128]{1,0:T(8,128)(2,1)S(1)}, u32[]{:S(2)}, u32[]{:S(2)}) %collective-permute-start) | collective-permute-done | bytes 524320 | tf_op jit(solution)/shard_map/ppermute | solution.py:195
  21.7 0.7 %collective-permute-start.4 = (bf16[2048,128]{1,0:T(8,128)(2,1)S(1)}, bf16[2048,128]{1,0:T(8,128)(2,1)S(1)}, u32[]{:S(2)}, u32[]{:S(2)}) collective-permute-start(bf16[2048,128]{1,0:T(8,128)(2,1)S(1)} %collective-permute-done.refs_1_), channel_id=1, source_target_pairs={{4,8},{8,4},{5,9},{9,5},{6,10},{10,6},{7,11},{11,7},{20,24},{24,20... | collective-permute-start | bytes 1572872 | tf_op jit(solution)/shard_map/ppermute | solution.py:199
  22.4 0.0 collective-permute-done.6.far_ref
  22.4 2.3 %collective-permute-done.7.far_core_ref = bf16[64,2048]{1,0:T(8,128)(2,1)S(1)} collective-permute-done((bf16[64,2048]{1,0:T(8,128)(2,1)S(1)}, bf16[64,2048]{1,0:T(8,128)(2,1)S(1)}, u32[]{:S(2)}, u32[]{:S(2)}) %collective-permute-start.7) | collective-permute-done | bytes 262176 | tf_op jit(solution)/shard_map/ppermute | solution.py:225
  24.7 0.0 copy-done.6
  24.7 0.0 copy-done.7
  24.7 0.0 copy-start.5
  24.7 1.0 %copy-done.5 = bf16[512,512]{1,0:T(8,128)(2,1)S(1)} copy-done((bf16[512,512]{1,0:T(8,128)(2,1)S(1)}, bf16[512,512]{1,0:T(8,128)(2,1)}, u32[]{:S(2)}) %copy-start.5) | copy-done | bytes 524312
  25.7 4.8 %time_kernel.1 = (f32[72,2048]{1,0:T(8,128)S(1)}, f32[32,2048]{1,0:T(8,128)S(1)}, f32[40,2048]{1,0:T(8,128)S(1)}) custom-call(f32[64]{0:T(128)S(1)} %copy-done.6, f32[64]{0:T(128)S(1)} %copy-done.7, bf16[64,2048]{1,0:T(8,128)(2,1)S(1)} %get-tuple-element.15.own_ref, bf16[64,2048]{1,0:T(8,128)(2,1)S(1)} %collective-permute-done.5.core_ref, ...), custom_call_target="tpu_custom_call" | custom-call | bytes 1024 | tf_op jit(solution)/shard_map/time_kernel/pallas_call | solution.py:258
  30.5 0.6 %collective-permute-start.9 = (f32[40,2048]{1,0:T(8,128)S(1)}, f32[40,2048]{1,0:T(8,128)S(1)}, u32[]{:S(2)}, u32[]{:S(2)}) collective-permute-start(f32[40,2048]{1,0:T(8,128)S(1)} %get-tuple-element.19), channel_id=1, source_target_pairs={{0,1},{1,0},{2,3},{3,2},{4,5},{5,4},{6,7},{7,6},{8,9},{9,8},{10,11... | collective-permute-start | bytes 983048 | tf_op jit(solution)/shard_map/ppermute | solution.py:225
  31.1 0.1 collective-permute-start.8
  31.2 1.6 %collective-permute-done.8.other_re_ref = f32[32,2048]{1,0:T(8,128)S(1)} collective-permute-done((f32[32,2048]{1,0:T(8,128)S(1)}, f32[32,2048]{1,0:T(8,128)S(1)}, u32[]{:S(2)}, u32[]{:S(2)}) %collective-permute-start.8) | collective-permute-done | bytes 262176 | tf_op jit(solution)/shard_map/ppermute | solution.py:225
  32.8 0.0 collective-permute-done.9.other_im_ref
  32.8 0.0 copy-done.2
  32.8 1.6 %prepare.1 = (f32[2048,128]{1,0:T(8,128)S(1)}, f32[2048,128]{1,0:T(8,128)S(1)}, f32[2048,128]{1,0:T(8,128)S(1)}, f32[2048,128]{1,0:T(8,128)S(1)}) custom-call(bf16[2,32,64,256]{3,2,1,0:T(8,128)(2,1)S(1)} %copy-done.2, f32[72,2048]{1,0:T(8,128)S(1)} %get-tuple-element.17.mine_ref, f32[32,2048]{1,0:T(8,128)S(1)} %collective-permute-done.8.other_re_ref, ...), custom_call_target="tpu_custom_call" | custom-call | bytes 1024 | tf_op jit(solution)/shard_map/prepare/pallas_call | solution.py:271
  34.4 0.0 collective-permute-done.2.refs_3_
  34.4 9.8 %collective-permute-done.3.refs_4_ = bf16[2048,128]{1,0:T(8,128)(2,1)S(1)} collective-permute-done((bf16[2048,128]{1,0:T(8,128)(2,1)S(1)}, bf16[2048,128]{1,0:T(8,128)(2,1)S(1)}, u32[]{:S(2)}, u32[]{:S(2)}) %collective-permute-start.3) | collective-permute-done | bytes 524320 | tf_op jit(solution)/shard_map/ppermute | solution.py:198
  44.2 0.0 collective-permute-done.4.refs_5_
  44.2 1.2 %couple.1 = (f32[2048,128]{1,0:T(8,128)S(1)}, f32[8,128]{1,0:T(8,128)S(1)}) custom-call(bf16[2,32,64,256]{3,2,1,0:T(8,128)(2,1)S(1)} %copy-done.2, bf16[2048,128]{1,0:T(8,128)(2,1)S(1)} %pack_couple.1.refs_0_, bf16[2048,128]{1,0:T(8,128)(2,1)S(1)} %collective-permute-done.refs_1_, bf16[2048,128]{1,0:T(8,128)(2,1)S(1)} %collective-permute-done.1.refs_2_, ...), custom_call_target="tpu_custom_call" | custom-call | bytes 1024 | tf_op jit(solution)/shard_map/couple/pallas_call | solution.py:281
  45.4 0.1 collective-permute-start.10
  45.5 1.2 %collective-permute-done.10 = f32[8,128]{1,0:T(8,128)S(1)} collective-permute-done((f32[8,128]{1,0:T(8,128)S(1)}, f32[8,128]{1,0:T(8,128)S(1)}, u32[]{:S(2)}, u32[]{:S(2)}) %collective-permute-start.10) | collective-permute-done | bytes 4128 | tf_op jit(solution)/shard_map/ppermute | solution.py:225
  46.6 1.3 %collective-permute-start.11 = (f32[8,128]{1,0:T(8,128)S(1)}, f32[8,128]{1,0:T(8,128)S(1)}, u32[]{:S(2)}, u32[]{:S(2)}) collective-permute-start(f32[8,128]{1,0:T(8,128)S(1)} %add.6), channel_id=1, source_target_pairs={{0,3},{1,2},{2,1},{3,0},{4,7},{5,6},{6,5},{7,4},{8,11},{9,10},{10,... | collective-permute-start | bytes 12296 | tf_op jit(solution)/shard_map/ppermute | solution.py:225
  47.9 1.8 %collective-permute-done.11 = f32[8,128]{1,0:T(8,128)S(1)} collective-permute-done((f32[8,128]{1,0:T(8,128)S(1)}, f32[8,128]{1,0:T(8,128)S(1)}, u32[]{:S(2)}, u32[]{:S(2)}) %collective-permute-start.11) | collective-permute-done | bytes 4128 | tf_op jit(solution)/shard_map/ppermute | solution.py:225
  49.7 2.0 %collective-permute-start.12 = (f32[8,128]{1,0:T(8,128)S(1)}, f32[8,128]{1,0:T(8,128)S(1)}, u32[]{:S(2)}, u32[]{:S(2)}) collective-permute-start(f32[8,128]{1,0:T(8,128)S(1)} %add.7.refs_0_), channel_id=1, source_target_pairs={{0,13},{1,12},{2,15},{3,14},{4,9},{5,8},{6,11},{7,10},{8,5},{9,4},... | collective-permute-start | bytes 12296 | tf_op jit(solution)/shard_map/ppermute | solution.py:309
  51.6 0.2 collective-permute-start.13
  51.8 1.7 %collective-permute-start.14 = (f32[8,128]{1,0:T(8,128)S(1)}, f32[8,128]{1,0:T(8,128)S(1)}, u32[]{:S(2)}, u32[]{:S(2)}) collective-permute-start(f32[8,128]{1,0:T(8,128)S(1)} %add.7.refs_0_), channel_id=1, source_target_pairs={{0,5},{1,4},{2,7},{3,6},{4,1},{5,0},{6,3},{7,2},{8,13},{9,12},{10,... | collective-permute-start | bytes 12296 | tf_op jit(solution)/shard_map/ppermute | solution.py:309
  53.6 1.7 %finish.1 = f32[2,2048,64]{2,1,0:T(8,128)} custom-call(f32[2048,128]{1,0:T(8,128)S(1)} %get-tuple-element.21.res_ref, f32[2048,128]{1,0:T(8,128)S(1)} %get-tuple-element.22.p_ref, f32[2048,128]{1,0:T(8,128)S(1)} %get-tuple-element.23.q_ref, f32[2048,128]{1,0:T(8,128)S(1)} %get-tuple-element.24.vel_ref), custom_call_target="tpu_custom_call" | custom-call | bytes 1024 | tf_op jit(solution)/shard_map/finish/pallas_call | solution.py:293
  55.2 0.0 collective-permute-done.12.refs_1_
  55.2 0.3 collective-permute-done.13.refs_2_
  55.6 0.0 collective-permute-done.14.refs_3_
  55.6 0.6 %rms.1 = f32[1]{0:T(128)} custom-call(f32[8,128]{1,0:T(8,128)S(1)} %add.7.refs_0_, f32[8,128]{1,0:T(8,128)S(1)} %collective-permute-done.12.refs_1_, f32[8,128]{1,0:T(8,128)S(1)} %collective-permute-done.13.refs_2_, f32[8,128]{1,0:T(8,128)S(1)} %collective-permute-done.14.refs_3_), custom_call_target="tpu_custom_call" | custom-call | tf_op jit(solution)/shard_map/rms/pallas_call | solution.py:314
  (7 shorter events, 0.0 us)
Async XLA Ops:
  0.6 24.0 %copy-start.6 = (f32[64]{0:T(128)S(1)}, f32[64]{0:T(128)}, u32[]{:S(2)}) copy-start(f32[64]{0:T(128)} %quad_ref.1) | copy-start | bytes 772
  0.6 24.0 %copy-start.7 = (f32[64]{0:T(128)S(1)}, f32[64]{0:T(128)}, u32[]{:S(2)}) copy-start(f32[64]{0:T(128)} %coul_ref.1) | copy-start | bytes 772
  0.7 1.6 %copy-start = (f32[2,32,64,64]{3,2,1,0:T(8,128)S(1)}, f32[2,32,64,64]{3,2,1,0:T(8,128)}, u32[]{:S(2)}) copy-start(f32[2,32,64,64]{3,2,1,0:T(8,128)} %param.7) | copy-start | bytes 3145732
  2.3 22.4 %copy-start.4 = (bf16[256,1536]{1,0:T(8,128)(2,1)S(1)}, bf16[256,1536]{1,0:T(8,128)(2,1)}, u32[]{:S(2)}) copy-start(bf16[256,1536]{1,0:T(8,128)(2,1)} %constant.5.clone.inv_ref) | copy-start | bytes 2359300
  2.3 30.5 %copy-start.3 = (f32[2,32,64,64]{3,2,1,0:T(8,128)S(1)}, f32[2,32,64,64]{3,2,1,0:T(8,128)}, u32[]{:S(2)}) copy-start(f32[2,32,64,64]{3,2,1,0:T(8,128)} %param.9) | copy-start | bytes 3145732
  2.5 30.3 %copy-start.1 = (f32[2,32,64,64]{3,2,1,0:T(8,128)S(1)}, f32[2,32,64,64]{3,2,1,0:T(8,128)}, u32[]{:S(2)}) copy-start(f32[2,32,64,64]{3,2,1,0:T(8,128)} %param.7) | copy-start | bytes 3145732
  2.5 30.3 %copy-start.2 = (bf16[2,32,64,256]{3,2,1,0:T(8,128)(2,1)S(1)}, bf16[2,32,64,256]{3,2,1,0:T(8,128)(2,1)}, u32[]{:S(2)}) copy-start(bf16[2,32,64,256]{3,2,1,0:T(8,128)(2,1)} %imped_ref.3) | copy-start | bytes 6291460
  2.5 13.4 %collective-permute-start.1 = (bf16[2048,128]{1,0:T(8,128)(2,1)S(1)}, bf16[2048,128]{1,0:T(8,128)(2,1)S(1)}, u32[]{:S(2)}, u32[]{:S(2)}) collective-permute-start(bf16[2048,128]{1,0:T(8,128)(2,1)S(1)} %pack_couple.1.refs_0_), channel_id=1, source_target_pairs={{4,8},{8,4},{5,9},{9,5},{6,10},{10,6},{7,11},{11,7},{20,24},{24,20... | collective-permute-start | bytes 1572872 | tf_op jit(solution)/shard_map/ppermute | solution.py:196
  3.3 18.4 %collective-permute-start = (bf16[2048,128]{1,0:T(8,128)(2,1)S(1)}, bf16[2048,128]{1,0:T(8,128)(2,1)S(1)}, u32[]{:S(2)}, u32[]{:S(2)}) collective-permute-start(bf16[2048,128]{1,0:T(8,128)(2,1)S(1)} %pack_couple.1.refs_0_), channel_id=1, source_target_pairs={{0,4},{4,0},{8,12},{12,8},{1,5},{5,1},{9,13},{13,9},{2,6},{6,2},{1... | collective-permute-start | bytes 1572872 | tf_op jit(solution)/shard_map/ppermute | solution.py:195
  10.7 1.9 %collective-permute-start.5 = (bf16[64,2048]{1,0:T(8,128)(2,1)S(1)}, bf16[64,2048]{1,0:T(8,128)(2,1)S(1)}, u32[]{:S(2)}, u32[]{:S(2)}) collective-permute-start(bf16[64,2048]{1,0:T(8,128)(2,1)S(1)} %get-tuple-element.16), channel_id=1, source_target_pairs={{0,1},{1,0},{2,3},{3,2},{4,5},{5,4},{6,7},{7,6},{8,9},{9,8},{10,11... | collective-permute-start | bytes 786440 | tf_op jit(solution)/shard_map/ppermute | solution.py:225
  10.8 11.6 %collective-permute-start.6 = (bf16[64,2048]{1,0:T(8,128)(2,1)S(1)}, bf16[64,2048]{1,0:T(8,128)(2,1)S(1)}, u32[]{:S(2)}, u32[]{:S(2)}) collective-permute-start(bf16[64,2048]{1,0:T(8,128)(2,1)S(1)} %get-tuple-element.15.own_ref), channel_id=1, source_target_pairs={{0,2},{1,3},{2,0},{3,1},{4,6},{5,7},{6,4},{7,5},{8,10},{9,11},{10,... | collective-permute-start | bytes 786440 | tf_op jit(solution)/shard_map/ppermute | solution.py:225
  12.4 12.3 %collective-permute-start.7 = (bf16[64,2048]{1,0:T(8,128)(2,1)S(1)}, bf16[64,2048]{1,0:T(8,128)(2,1)S(1)}, u32[]{:S(2)}, u32[]{:S(2)}) collective-permute-start(bf16[64,2048]{1,0:T(8,128)(2,1)S(1)} %get-tuple-element.16), channel_id=1, source_target_pairs={{0,3},{1,2},{2,1},{3,0},{4,7},{5,6},{6,5},{7,4},{8,11},{9,10},{10,... | collective-permute-start | bytes 786440 | tf_op jit(solution)/shard_map/ppermute | solution.py:225
  12.6 21.8 %collective-permute-start.2 = (bf16[2048,128]{1,0:T(8,128)(2,1)S(1)}, bf16[2048,128]{1,0:T(8,128)(2,1)S(1)}, u32[]{:S(2)}, u32[]{:S(2)}) collective-permute-start(bf16[2048,128]{1,0:T(8,128)(2,1)S(1)} %get-tuple-element.14), channel_id=1, source_target_pairs={{0,12},{12,0},{1,13},{13,1},{2,14},{14,2},{3,15},{15,3},{16,28},{2... | collective-permute-start | bytes 1572872 | tf_op jit(solution)/shard_map/ppermute | solution.py:197
  15.9 28.3 %collective-permute-start.3 = (bf16[2048,128]{1,0:T(8,128)(2,1)S(1)}, bf16[2048,128]{1,0:T(8,128)(2,1)S(1)}, u32[]{:S(2)}, u32[]{:S(2)}) collective-permute-start(bf16[2048,128]{1,0:T(8,128)(2,1)S(1)} %collective-permute-done.1.refs_2_), channel_id=1, source_target_pairs={{4,0},{8,12},{5,1},{9,13},{6,2},{10,14},{7,3},{11,15},{20,16},{24,... | collective-permute-start | bytes 1572872 | tf_op jit(solution)/shard_map/ppermute | solution.py:198
  21.7 22.5 %collective-permute-start.4 = (bf16[2048,128]{1,0:T(8,128)(2,1)S(1)}, bf16[2048,128]{1,0:T(8,128)(2,1)S(1)}, u32[]{:S(2)}, u32[]{:S(2)}) collective-permute-start(bf16[2048,128]{1,0:T(8,128)(2,1)S(1)} %collective-permute-done.refs_1_), channel_id=1, source_target_pairs={{4,8},{8,4},{5,9},{9,5},{6,10},{10,6},{7,11},{11,7},{20,24},{24,20... | collective-permute-start | bytes 1572872 | tf_op jit(solution)/shard_map/ppermute | solution.py:199
  24.7 1.0 %copy-start.5 = (bf16[512,512]{1,0:T(8,128)(2,1)S(1)}, bf16[512,512]{1,0:T(8,128)(2,1)}, u32[]{:S(2)}) copy-start(bf16[512,512]{1,0:T(8,128)(2,1)} %constant.4.clone.fwd_ref) | copy-start | bytes 1572868
  30.5 2.3 %collective-permute-start.9 = (f32[40,2048]{1,0:T(8,128)S(1)}, f32[40,2048]{1,0:T(8,128)S(1)}, u32[]{:S(2)}, u32[]{:S(2)}) collective-permute-start(f32[40,2048]{1,0:T(8,128)S(1)} %get-tuple-element.19), channel_id=1, source_target_pairs={{0,1},{1,0},{2,3},{3,2},{4,5},{5,4},{6,7},{7,6},{8,9},{9,8},{10,11... | collective-permute-start | bytes 983048 | tf_op jit(solution)/shard_map/ppermute | solution.py:225
  31.1 1.6 %collective-permute-start.8 = (f32[32,2048]{1,0:T(8,128)S(1)}, f32[32,2048]{1,0:T(8,128)S(1)}, u32[]{:S(2)}, u32[]{:S(2)}) collective-permute-start(f32[32,2048]{1,0:T(8,128)S(1)} %get-tuple-element.18), channel_id=1, source_target_pairs={{0,1},{1,0},{2,3},{3,2},{4,5},{5,4},{6,7},{7,6},{8,9},{9,8},{10,11... | collective-permute-start | bytes 786440 | tf_op jit(solution)/shard_map/ppermute | solution.py:225
  45.4 1.2 %collective-permute-start.10 = (f32[8,128]{1,0:T(8,128)S(1)}, f32[8,128]{1,0:T(8,128)S(1)}, u32[]{:S(2)}, u32[]{:S(2)}) collective-permute-start(f32[8,128]{1,0:T(8,128)S(1)} %get-tuple-element.25), channel_id=1, source_target_pairs={{0,1},{1,0},{2,3},{3,2},{4,5},{5,4},{6,7},{7,6},{8,9},{9,8},{10,11... | collective-permute-start | bytes 12296 | tf_op jit(solution)/shard_map/ppermute | solution.py:225
  46.6 3.0 %collective-permute-start.11 = (f32[8,128]{1,0:T(8,128)S(1)}, f32[8,128]{1,0:T(8,128)S(1)}, u32[]{:S(2)}, u32[]{:S(2)}) collective-permute-start(f32[8,128]{1,0:T(8,128)S(1)} %add.6), channel_id=1, source_target_pairs={{0,3},{1,2},{2,1},{3,0},{4,7},{5,6},{6,5},{7,4},{8,11},{9,10},{10,... | collective-permute-start | bytes 12296 | tf_op jit(solution)/shard_map/ppermute | solution.py:225
  49.7 5.5 %collective-permute-start.12 = (f32[8,128]{1,0:T(8,128)S(1)}, f32[8,128]{1,0:T(8,128)S(1)}, u32[]{:S(2)}, u32[]{:S(2)}) collective-permute-start(f32[8,128]{1,0:T(8,128)S(1)} %add.7.refs_0_), channel_id=1, source_target_pairs={{0,13},{1,12},{2,15},{3,14},{4,9},{5,8},{6,11},{7,10},{8,5},{9,4},... | collective-permute-start | bytes 12296 | tf_op jit(solution)/shard_map/ppermute | solution.py:309
  51.6 3.9 %collective-permute-start.13 = (f32[8,128]{1,0:T(8,128)S(1)}, f32[8,128]{1,0:T(8,128)S(1)}, u32[]{:S(2)}, u32[]{:S(2)}) collective-permute-start(f32[8,128]{1,0:T(8,128)S(1)} %add.7.refs_0_), channel_id=1, source_target_pairs={{0,9},{1,8},{2,11},{3,10},{4,13},{5,12},{6,15},{7,14},{8,1},{9,0},... | collective-permute-start | bytes 12296 | tf_op jit(solution)/shard_map/ppermute | solution.py:309
  51.8 3.8 %collective-permute-start.14 = (f32[8,128]{1,0:T(8,128)S(1)}, f32[8,128]{1,0:T(8,128)S(1)}, u32[]{:S(2)}, u32[]{:S(2)}) collective-permute-start(f32[8,128]{1,0:T(8,128)S(1)} %add.7.refs_0_), channel_id=1, source_target_pairs={{0,5},{1,4},{2,7},{3,6},{4,1},{5,0},{6,3},{7,2},{8,13},{9,12},{10,... | collective-permute-start | bytes 12296 | tf_op jit(solution)/shard_map/ppermute | solution.py:309

commit v6 on v5

--- a/solution.py
+++ b/solution.py
@@ -151,26 +151,49 @@
         rest_ref[rows, :] = rest_ref[rows, :] - excite + slope * (vel - vel.astype(BF16).astype(F32))
 
 
-def couple_kernel(harm, bodies, reals, line, imped_ref, *refs):
-    pieces, (rest_ref, res_ref, total_ref, held_ref) = refs[:-4], refs[-4:]
+def coupling(imped, vels, bodies, reals):
+    sign = jnp.where(lax.broadcasted_iota(jnp.int32, (bodies, 2 * reals), 1) < reals, -1.0, 1.0)
+    out = jnp.dot(imped.reshape(2 * bodies, imped.shape[2]), vels, preferred_element_type=F32)
+    return out[:bodies] + sign * pltpu.roll(out[bodies:], reals, 1)
+
+
+def at_ends(me):
+    return jnp.logical_or(me == 0, me == 3)
+
+
+def partial_kernel(harm, bodies, reals, imped_ref, own_ref, near_ref, cross_ref, across_ref, rest_ref, out_ref, held_ref):
     me = lax.axis_index("body")
-    sign = jnp.where(lax.broadcasted_iota(jnp.int32, (bodies, 2 * reals), 1) < reals, -1.0, 1.0)
-    total = jnp.zeros((8, 2 * reals), F32)
-    ends = jnp.logical_or(me == 0, me == 3)
+    ends = at_ends(me)
+    held_ref[...] = jnp.zeros_like(held_ref)
     for h in range(harm):
         rows = pl.ds(h * bodies, bodies)
-        if not line:
+        slot = h % 4
+        for flip, value in ((0, own_ref[rows, :]), (1, near_ref[rows, :]),
+                            (3, jnp.where(ends, across_ref[rows, :], cross_ref[rows, :]))):
+            held_ref[slot, pl.ds(pl.multiple_of((me ^ flip) * bodies, bodies), bodies), :] = value
+        out_ref[rows, :] = rest_ref[rows, :] + coupling(imped_ref[:, h], held_ref[slot], bodies, reals)
+
+
+def couple_kernel(harm, bodies, reals, line, imped_ref, *refs):
+    pieces, (rest_ref, res_ref, total_ref) = refs[:-3], refs[-3:]
+    total = jnp.zeros((8, 2 * reals), F32)
+    if line:
+        me = lax.axis_index("body")
+        ends = at_ends(me)
+        source = me ^ 2
+        lower = source % 2 == 0
+        none = jnp.zeros((bodies, 2 * reals), BF16)
+        cols = pl.ds(pl.multiple_of((source // 2) * 2 * bodies, 2 * bodies), 2 * bodies)
+    for h in range(harm):
+        rows = pl.ds(h * bodies, bodies)
+        if line:
+            value = jnp.where(ends, pieces[0][rows, :], pieces[1][rows, :])
+            vels = jnp.concatenate([jnp.where(lower, value, none), jnp.where(lower, none, value)], axis=0)
+            imped = imped_ref[:, h, :, cols]
+        else:
             vels = pieces[0][:, h].reshape(-1, 2 * reals)
-        else:
-            slot = h % 4
-            held = [ref[rows, :] for ref in pieces]
-            for flip, value in ((0, held[0]), (1, held[1]), (3, jnp.where(ends, held[3], held[2])),
-                                (2, jnp.where(ends, held[4], held[5]))):
-                held_ref[slot, pl.ds(pl.multiple_of((me ^ flip) * bodies, bodies), bodies), :] = value
-            vels = held_ref[slot]
-        both = imped_ref[:, h].reshape(2 * bodies, imped_ref.shape[3])
-        out = jnp.dot(both, vels, preferred_element_type=F32)
-        res = out[:bodies] + sign * pltpu.roll(out[bodies:], reals, 1) + rest_ref[rows, :]
+            imped = imped_ref[:, h]
+        res = coupling(imped, vels, bodies, reals) + rest_ref[rows, :]
         res_ref[rows, :] = res
         total = total + jnp.sum((res * res).reshape(bodies // 8, 8, 2 * reals), axis=0)
     total_ref[...] = jnp.broadcast_to(jnp.sum(total), total_ref.shape)
@@ -278,11 +301,21 @@
             name="prepare",
         )(imped, mine, *other, flat_excite, flat)
 
+        if body_count == 4:
+            rest = pl.pallas_call(
+                functools.partial(partial_kernel, harm, bodies, reals),
+                in_specs=[VMEM] * 6,
+                out_shape=dense,
+                scratch_shapes=[pltpu.VMEM((4, everyone, group), BF16)],
+                compiler_params=params(),
+                cost_estimate=cost(0, 1 << 10),
+                name="partial",
+            )(imped, *pieces[:4], rest)
+            pieces = pieces[4:]
         res, total = pl.pallas_call(
             functools.partial(couple_kernel, harm, bodies, reals, body_count == 4),
             in_specs=[VMEM] * (2 + len(pieces)),
             out_shape=(dense, jax.ShapeDtypeStruct((8, 128), F32)),
-            scratch_shapes=[pltpu.VMEM((4, everyone, group), BF16)],
             compiler_params=params(),
             cost_estimate=cost(0, 1 << 10),
             name="couple",

time: 56.4 us -> 55.9 us (level)
  waiting for transfers between devices: 21.4 us -> 20.5 us
    ppermute x1, waiting for transfers between devices: 9.84 us -> 8.91 us  [gather_line(): outer = lax.ppermute(cross, axis, [(1, 0), (2, 3)])]
    pallas_call x0 -> x1, Pallas kernels: none -> 0.9 us  [local(): pl.pallas_call(functools.partial(partial_kernel, harm, bodies, reals), in...]
  transfers between devices with their start and end apart: 15 -> 15, of which waited for: 7 -> 7; matrix products, arithmetic and copies ran while one was open for 0% -> 0% of each run, Pallas kernels for 17% -> 19%
where the time goes in v6:
time: 55.9 us; the launch traced here: 55.7 us
  waiting for transfers between devices  20.5 us (37%)
  starting transfers between devices  19.9 us (36%)
  Pallas kernels  11.8 us (21%)
  local copies, waits for them, and re-layouts  2.66 us (5%)
  between operations  0.82 us (1%)
    ppermute x1, waiting for transfers between devices, gather_line(): outer = lax.ppermute(cross, axis, [(1, 0), (2, 3)])  8.91 us
    ppermute x7, waiting for transfers between devices, flipped(): return lax.ppermute(x, 'harm', [(i, i ^ flip) for i in range(4)])  6.7 us
    ppermute x1, starting transfers between devices, gather_line(): near = lax.ppermute(x, axis, [(0, 1), (1, 0), (2, 3), (3, 2)])  6.01 us
    pallas_call x1, Pallas kernels, local(): pl.pallas_call(functools.partial(time_kernel, harm, bodies, reals), grid=...  4.77 us
    ppermute x1, waiting for transfers between devices, gather_line(): near = lax.ppermute(x, axis, [(0, 1), (1, 0), (2, 3), (3, 2)])  4.5 us
    ppermute x7, starting transfers between devices, flipped(): return lax.ppermute(x, 'harm', [(i, i ^ flip) for i in range(4)])  4.01 us
    ppermute x3, starting transfers between devices, crossed(): return lax.ppermute(total, ('body', 'harm'), pairs)  3.88 us
    ppermute x1, starting transfers between devices, gather_line(): across = lax.ppermute(again, axis, [(0, 3), (3, 0)])  3.25 us
  transfers between devices with their start and end apart: 15, of which 7 were waited for; matrix products, arithmetic and copies ran while one was open for 0% of the time, Pallas kernels for 19%

profile of v6, /device:TPU:0, one launch (start us, length us, event | category | flops | bytes accessed | tf_op | source)
XLA Modules:
  0.0 55.7 jit_solution(10370859994953065870)
XLA Ops:
  0.6 0.0 copy-start.6
  0.6 0.0 copy-start.7
  0.7 0.0 copy-start.1
  0.7 1.6 %copy-done.1 = f32[2,32,64,64]{3,2,1,0:T(8,128)S(1)} copy-done((f32[2,32,64,64]{3,2,1,0:T(8,128)S(1)}, f32[2,32,64,64]{3,2,1,0:T(8,128)}, u32[]{:S(2)}) %copy-start.1) | copy-done | bytes 1048600
  2.3 0.2 pack_couple.1.own_ref
  2.5 0.0 copy-start
  2.5 0.0 copy-start.2
  2.5 0.8 %collective-permute-start = (bf16[2048,128]{1,0:T(8,128)(2,1)S(1)}, bf16[2048,128]{1,0:T(8,128)(2,1)S(1)}, u32[]{:S(2)}, u32[]{:S(2)}) collective-permute-start(bf16[2048,128]{1,0:T(8,128)(2,1)S(1)} %pack_couple.1.own_ref), channel_id=1, source_target_pairs={{4,8},{8,4},{5,9},{9,5},{6,10},{10,6},{7,11},{11,7},{20,24},{24,20... | collective-permute-start | bytes 1572872 | tf_op jit(solution)/shard_map/ppermute | solution.py:219
  3.3 6.0 %collective-permute-start.2 = (bf16[2048,128]{1,0:T(8,128)(2,1)S(1)}, bf16[2048,128]{1,0:T(8,128)(2,1)S(1)}, u32[]{:S(2)}, u32[]{:S(2)}) collective-permute-start(bf16[2048,128]{1,0:T(8,128)(2,1)S(1)} %pack_couple.1.own_ref), channel_id=1, source_target_pairs={{0,4},{4,0},{8,12},{12,8},{1,5},{5,1},{9,13},{13,9},{2,6},{6,2},{1... | collective-permute-start | bytes 1572872 | tf_op jit(solution)/shard_map/ppermute | solution.py:218
  9.3 1.3 %pack_time.1 = (bf16[64,2048]{1,0:T(8,128)(2,1)S(1)}, bf16[64,2048]{1,0:T(8,128)(2,1)S(1)}, bf16[2048,128]{1,0:T(8,128)(2,1)S(1)}) custom-call(f32[4096,64]{1,0:T(8,128)S(1)} %bitcast.4), custom_call_target="tpu_custom_call" | custom-call | bytes 1024 | tf_op jit(solution)/shard_map/pack_time/pallas_call | solution.py:258
  10.7 0.1 collective-permute-start.5
  10.8 1.6 %collective-permute-start.6 = (bf16[64,2048]{1,0:T(8,128)(2,1)S(1)}, bf16[64,2048]{1,0:T(8,128)(2,1)S(1)}, u32[]{:S(2)}, u32[]{:S(2)}) collective-permute-start(bf16[64,2048]{1,0:T(8,128)(2,1)S(1)} %get-tuple-element.15.own_ref), channel_id=1, source_target_pairs={{0,2},{1,3},{2,0},{3,1},{4,6},{5,7},{6,4},{7,5},{8,10},{9,11},{10,... | collective-permute-start | bytes 786440 | tf_op jit(solution)/shard_map/ppermute | solution.py:248
  12.4 0.3 collective-permute-start.7
  12.6 0.0 collective-permute-done.5.core_ref
  12.6 3.2 %collective-permute-start.4 = (bf16[2048,128]{1,0:T(8,128)(2,1)S(1)}, bf16[2048,128]{1,0:T(8,128)(2,1)S(1)}, u32[]{:S(2)}, u32[]{:S(2)}) collective-permute-start(bf16[2048,128]{1,0:T(8,128)(2,1)S(1)} %get-tuple-element.14), channel_id=1, source_target_pairs={{0,12},{12,0},{1,13},{13,1},{2,14},{14,2},{3,15},{15,3},{16,28},{2... | collective-permute-start | bytes 1572872 | tf_op jit(solution)/shard_map/ppermute | solution.py:220
  15.9 0.0 collective-permute-done.cross_ref
  15.9 1.3 %collective-permute-start.1 = (bf16[2048,128]{1,0:T(8,128)(2,1)S(1)}, bf16[2048,128]{1,0:T(8,128)(2,1)S(1)}, u32[]{:S(2)}, u32[]{:S(2)}) collective-permute-start(bf16[2048,128]{1,0:T(8,128)(2,1)S(1)} %collective-permute-done.cross_ref), channel_id=1, source_target_pairs={{4,0},{8,12},{5,1},{9,13},{6,2},{10,14},{7,3},{11,15},{20,16},{24,... | collective-permute-start | bytes 1572872 | tf_op jit(solution)/shard_map/ppermute | solution.py:221
  17.2 4.5 %collective-permute-done.2.near_ref = bf16[2048,128]{1,0:T(8,128)(2,1)S(1)} collective-permute-done((bf16[2048,128]{1,0:T(8,128)(2,1)S(1)}, bf16[2048,128]{1,0:T(8,128)(2,1)S(1)}, u32[]{:S(2)}, u32[]{:S(2)}) %collective-permute-start.2) | collective-permute-done | bytes 524320 | tf_op jit(solution)/shard_map/ppermute | solution.py:218
  21.7 0.7 %collective-permute-start.3 = (bf16[2048,128]{1,0:T(8,128)(2,1)S(1)}, bf16[2048,128]{1,0:T(8,128)(2,1)S(1)}, u32[]{:S(2)}, u32[]{:S(2)}) collective-permute-start(bf16[2048,128]{1,0:T(8,128)(2,1)S(1)} %collective-permute-done.2.near_ref), channel_id=1, source_target_pairs={{4,8},{8,4},{5,9},{9,5},{6,10},{10,6},{7,11},{11,7},{20,24},{24,20... | collective-permute-start | bytes 1572872 | tf_op jit(solution)/shard_map/ppermute | solution.py:222
  22.4 0.0 collective-permute-done.6.far_ref
  22.4 2.3 %collective-permute-done.7.far_core_ref = bf16[64,2048]{1,0:T(8,128)(2,1)S(1)} collective-permute-done((bf16[64,2048]{1,0:T(8,128)(2,1)S(1)}, bf16[64,2048]{1,0:T(8,128)(2,1)S(1)}, u32[]{:S(2)}, u32[]{:S(2)}) %collective-permute-start.7) | collective-permute-done | bytes 262176 | tf_op jit(solution)/shard_map/ppermute | solution.py:248
  24.7 0.0 copy-done.7
  24.7 0.0 copy-start.5
  24.7 1.0 %copy-done.5 = bf16[512,512]{1,0:T(8,128)(2,1)S(1)} copy-done((bf16[512,512]{1,0:T(8,128)(2,1)S(1)}, bf16[512,512]{1,0:T(8,128)(2,1)}, u32[]{:S(2)}) %copy-start.5) | copy-done | bytes 524312
  25.7 4.8 %time_kernel.1 = (f32[72,2048]{1,0:T(8,128)S(1)}, f32[32,2048]{1,0:T(8,128)S(1)}, f32[40,2048]{1,0:T(8,128)S(1)}) custom-call(f32[64]{0:T(128)S(1)} %copy-done.6, f32[64]{0:T(128)S(1)} %copy-done.7, bf16[64,2048]{1,0:T(8,128)(2,1)S(1)} %get-tuple-element.15.own_ref, bf16[64,2048]{1,0:T(8,128)(2,1)S(1)} %collective-permute-done.5.core_ref, ...), custom_call_target="tpu_custom_call" | custom-call | bytes 1024 | tf_op jit(solution)/shard_map/time_kernel/pallas_call | solution.py:281
  30.5 0.6 %collective-permute-start.9 = (f32[40,2048]{1,0:T(8,128)S(1)}, f32[40,2048]{1,0:T(8,128)S(1)}, u32[]{:S(2)}, u32[]{:S(2)}) collective-permute-start(f32[40,2048]{1,0:T(8,128)S(1)} %get-tuple-element.19), channel_id=1, source_target_pairs={{0,1},{1,0},{2,3},{3,2},{4,5},{5,4},{6,7},{7,6},{8,9},{9,8},{10,11... | collective-permute-start | bytes 983048 | tf_op jit(solution)/shard_map/ppermute | solution.py:248
  31.1 0.1 collective-permute-start.8
  31.2 1.6 %collective-permute-done.8.other_re_ref = f32[32,2048]{1,0:T(8,128)S(1)} collective-permute-done((f32[32,2048]{1,0:T(8,128)S(1)}, f32[32,2048]{1,0:T(8,128)S(1)}, u32[]{:S(2)}, u32[]{:S(2)}) %collective-permute-start.8) | collective-permute-done | bytes 262176 | tf_op jit(solution)/shard_map/ppermute | solution.py:248
  32.8 0.0 collective-permute-done.9.other_im_ref
  32.8 0.0 copy-done.2
  32.8 1.6 %prepare.1 = (f32[2048,128]{1,0:T(8,128)S(1)}, f32[2048,128]{1,0:T(8,128)S(1)}, f32[2048,128]{1,0:T(8,128)S(1)}, f32[2048,128]{1,0:T(8,128)S(1)}) custom-call(bf16[2,32,64,256]{3,2,1,0:T(8,128)(2,1)S(1)} %copy-done, f32[72,2048]{1,0:T(8,128)S(1)} %get-tuple-element.17.mine_ref, f32[32,2048]{1,0:T(8,128)S(1)} %collective-permute-done.8.other_re_ref, ...), custom_call_target="tpu_custom_call" | custom-call | bytes 1024 | tf_op jit(solution)/shard_map/prepare/pallas_call | solution.py:294
  34.4 0.0 collective-permute-done.4.across_ref
  34.4 0.9 %partial.1.refs_2_ = f32[2048,128]{1,0:T(8,128)S(1)} custom-call(bf16[2,32,64,256]{3,2,1,0:T(8,128)(2,1)S(1)} %copy-done, bf16[2048,128]{1,0:T(8,128)(2,1)S(1)} %pack_couple.1.own_ref, bf16[2048,128]{1,0:T(8,128)(2,1)S(1)} %collective-permute-done.2.near_ref, bf16[2048,128]{1,0:T(8,128)(2,1)S(1)} %collective-permute-done.cross_ref, ...), custom_call_target="tpu_custom_call" | custom-call | bytes 1024 | tf_op jit(solution)/shard_map/partial/pallas_call | solution.py:305
  35.3 8.9 %collective-permute-done.1.refs_0_ = bf16[2048,128]{1,0:T(8,128)(2,1)S(1)} collective-permute-done((bf16[2048,128]{1,0:T(8,128)(2,1)S(1)}, bf16[2048,128]{1,0:T(8,128)(2,1)S(1)}, u32[]{:S(2)}, u32[]{:S(2)}) %collective-permute-start.1) | collective-permute-done | bytes 524320 | tf_op jit(solution)/shard_map/ppermute | solution.py:221
  44.2 0.0 collective-permute-done.3.refs_1_
  44.2 0.7 %couple.1 = (f32[2048,128]{1,0:T(8,128)S(1)}, f32[8,128]{1,0:T(8,128)S(1)}) custom-call(bf16[2,32,64,256]{3,2,1,0:T(8,128)(2,1)S(1)} %copy-done, bf16[2048,128]{1,0:T(8,128)(2,1)S(1)} %collective-permute-done.1.refs_0_, bf16[2048,128]{1,0:T(8,128)(2,1)S(1)} %collective-permute-done.3.refs_1_, f32[2048,128]{1,0:T(8,128)S(1)} %partial.1.refs_2_), custom_call_target="tpu_custom_call" | custom-call | bytes 1024 | tf_op jit(solution)/shard_map/couple/pallas_call | solution.py:315
  45.0 0.1 collective-permute-start.10
  45.0 1.2 %collective-permute-done.10 = f32[8,128]{1,0:T(8,128)S(1)} collective-permute-done((f32[8,128]{1,0:T(8,128)S(1)}, f32[8,128]{1,0:T(8,128)S(1)}, u32[]{:S(2)}, u32[]{:S(2)}) %collective-permute-start.10) | collective-permute-done | bytes 4128 | tf_op jit(solution)/shard_map/ppermute | solution.py:248
  46.2 1.3 %collective-permute-start.11 = (f32[8,128]{1,0:T(8,128)S(1)}, f32[8,128]{1,0:T(8,128)S(1)}, u32[]{:S(2)}, u32[]{:S(2)}) collective-permute-start(f32[8,128]{1,0:T(8,128)S(1)} %add.6), channel_id=1, source_target_pairs={{0,3},{1,2},{2,1},{3,0},{4,7},{5,6},{6,5},{7,4},{8,11},{9,10},{10,... | collective-permute-start | bytes 12296 | tf_op jit(solution)/shard_map/ppermute | solution.py:248
  47.5 1.7 %collective-permute-done.11 = f32[8,128]{1,0:T(8,128)S(1)} collective-permute-done((f32[8,128]{1,0:T(8,128)S(1)}, f32[8,128]{1,0:T(8,128)S(1)}, u32[]{:S(2)}, u32[]{:S(2)}) %collective-permute-start.11) | collective-permute-done | bytes 4128 | tf_op jit(solution)/shard_map/ppermute | solution.py:248
  49.2 1.9 %collective-permute-start.12 = (f32[8,128]{1,0:T(8,128)S(1)}, f32[8,128]{1,0:T(8,128)S(1)}, u32[]{:S(2)}, u32[]{:S(2)}) collective-permute-start(f32[8,128]{1,0:T(8,128)S(1)} %add.7.refs_0_), channel_id=1, source_target_pairs={{0,13},{1,12},{2,15},{3,14},{4,9},{5,8},{6,11},{7,10},{8,5},{9,4},... | collective-permute-start | bytes 12296 | tf_op jit(solution)/shard_map/ppermute | solution.py:342
  51.2 0.2 collective-permute-start.13
  51.4 1.7 %collective-permute-start.14 = (f32[8,128]{1,0:T(8,128)S(1)}, f32[8,128]{1,0:T(8,128)S(1)}, u32[]{:S(2)}, u32[]{:S(2)}) collective-permute-start(f32[8,128]{1,0:T(8,128)S(1)} %add.7.refs_0_), channel_id=1, source_target_pairs={{0,5},{1,4},{2,7},{3,6},{4,1},{5,0},{6,3},{7,2},{8,13},{9,12},{10,... | collective-permute-start | bytes 12296 | tf_op jit(solution)/shard_map/ppermute | solution.py:342
  53.1 1.7 %finish.1 = f32[2,2048,64]{2,1,0:T(8,128)} custom-call(f32[2048,128]{1,0:T(8,128)S(1)} %get-tuple-element.21.res_ref, f32[2048,128]{1,0:T(8,128)S(1)} %get-tuple-element.22.p_ref, f32[2048,128]{1,0:T(8,128)S(1)} %get-tuple-element.23.q_ref, f32[2048,128]{1,0:T(8,128)S(1)} %get-tuple-element.24.vel_ref), custom_call_target="tpu_custom_call" | custom-call | bytes 1024 | tf_op jit(solution)/shard_map/finish/pallas_call | solution.py:326
  54.8 0.0 collective-permute-done.12.refs_1_
  54.8 0.3 collective-permute-done.13.refs_2_
  55.1 0.0 collective-permute-done.14.refs_3_
  55.1 0.6 %rms.1 = f32[1]{0:T(128)} custom-call(f32[8,128]{1,0:T(8,128)S(1)} %add.7.refs_0_, f32[8,128]{1,0:T(8,128)S(1)} %collective-permute-done.12.refs_1_, f32[8,128]{1,0:T(8,128)S(1)} %collective-permute-done.13.refs_2_, f32[8,128]{1,0:T(8,128)S(1)} %collective-permute-done.14.refs_3_), custom_call_target="tpu_custom_call" | custom-call | tf_op jit(solution)/shard_map/rms/pallas_call | solution.py:347
  (8 shorter events, 0.0 us)
Async XLA Ops:
  0.6 24.0 %copy-start.6 = (f32[64]{0:T(128)S(1)}, f32[64]{0:T(128)}, u32[]{:S(2)}) copy-start(f32[64]{0:T(128)} %quad_ref.1) | copy-start | bytes 772
  0.6 24.0 %copy-start.7 = (f32[64]{0:T(128)S(1)}, f32[64]{0:T(128)}, u32[]{:S(2)}) copy-start(f32[64]{0:T(128)} %coul_ref.1) | copy-start | bytes 772
  0.7 1.6 %copy-start.1 = (f32[2,32,64,64]{3,2,1,0:T(8,128)S(1)}, f32[2,32,64,64]{3,2,1,0:T(8,128)}, u32[]{:S(2)}) copy-start(f32[2,32,64,64]{3,2,1,0:T(8,128)} %param.7) | copy-start | bytes 3145732
  2.3 22.4 %copy-start.4 = (bf16[256,1536]{1,0:T(8,128)(2,1)S(1)}, bf16[256,1536]{1,0:T(8,128)(2,1)}, u32[]{:S(2)}) copy-start(bf16[256,1536]{1,0:T(8,128)(2,1)} %constant.5.clone.inv_ref) | copy-start | bytes 2359300
  2.3 30.5 %copy-start.3 = (f32[2,32,64,64]{3,2,1,0:T(8,128)S(1)}, f32[2,32,64,64]{3,2,1,0:T(8,128)}, u32[]{:S(2)}) copy-start(f32[2,32,64,64]{3,2,1,0:T(8,128)} %param.9) | copy-start | bytes 3145732
  2.5 30.3 %copy-start = (bf16[2,32,64,256]{3,2,1,0:T(8,128)(2,1)S(1)}, bf16[2,32,64,256]{3,2,1,0:T(8,128)(2,1)}, u32[]{:S(2)}) copy-start(bf16[2,32,64,256]{3,2,1,0:T(8,128)(2,1)} %imped_ref.5) | copy-start | bytes 6291460
  2.5 30.3 %copy-start.2 = (f32[2,32,64,64]{3,2,1,0:T(8,128)S(1)}, f32[2,32,64,64]{3,2,1,0:T(8,128)}, u32[]{:S(2)}) copy-start(f32[2,32,64,64]{3,2,1,0:T(8,128)} %param.7) | copy-start | bytes 3145732
  2.5 13.4 %collective-permute-start = (bf16[2048,128]{1,0:T(8,128)(2,1)S(1)}, bf16[2048,128]{1,0:T(8,128)(2,1)S(1)}, u32[]{:S(2)}, u32[]{:S(2)}) collective-permute-start(bf16[2048,128]{1,0:T(8,128)(2,1)S(1)} %pack_couple.1.own_ref), channel_id=1, source_target_pairs={{4,8},{8,4},{5,9},{9,5},{6,10},{10,6},{7,11},{11,7},{20,24},{24,20... | collective-permute-start | bytes 1572872 | tf_op jit(solution)/shard_map/ppermute | solution.py:219
  3.3 18.4 %collective-permute-start.2 = (bf16[2048,128]{1,0:T(8,128)(2,1)S(1)}, bf16[2048,128]{1,0:T(8,128)(2,1)S(1)}, u32[]{:S(2)}, u32[]{:S(2)}) collective-permute-start(bf16[2048,128]{1,0:T(8,128)(2,1)S(1)} %pack_couple.1.own_ref), channel_id=1, source_target_pairs={{0,4},{4,0},{8,12},{12,8},{1,5},{5,1},{9,13},{13,9},{2,6},{6,2},{1... | collective-permute-start | bytes 1572872 | tf_op jit(solution)/shard_map/ppermute | solution.py:218
  10.7 1.9 %collective-permute-start.5 = (bf16[64,2048]{1,0:T(8,128)(2,1)S(1)}, bf16[64,2048]{1,0:T(8,128)(2,1)S(1)}, u32[]{:S(2)}, u32[]{:S(2)}) collective-permute-start(bf16[64,2048]{1,0:T(8,128)(2,1)S(1)} %get-tuple-element.16), channel_id=1, source_target_pairs={{0,1},{1,0},{2,3},{3,2},{4,5},{5,4},{6,7},{7,6},{8,9},{9,8},{10,11... | collective-permute-start | bytes 786440 | tf_op jit(solution)/shard_map/ppermute | solution.py:248
  10.8 11.6 %collective-permute-start.6 = (bf16[64,2048]{1,0:T(8,128)(2,1)S(1)}, bf16[64,2048]{1,0:T(8,128)(2,1)S(1)}, u32[]{:S(2)}, u32[]{:S(2)}) collective-permute-start(bf16[64,2048]{1,0:T(8,128)(2,1)S(1)} %get-tuple-element.15.own_ref), channel_id=1, source_target_pairs={{0,2},{1,3},{2,0},{3,1},{4,6},{5,7},{6,4},{7,5},{8,10},{9,11},{10,... | collective-permute-start | bytes 786440 | tf_op jit(solution)/shard_map/ppermute | solution.py:248
  12.4 12.3 %collective-permute-start.7 = (bf16[64,2048]{1,0:T(8,128)(2,1)S(1)}, bf16[64,2048]{1,0:T(8,128)(2,1)S(1)}, u32[]{:S(2)}, u32[]{:S(2)}) collective-permute-start(bf16[64,2048]{1,0:T(8,128)(2,1)S(1)} %get-tuple-element.16), channel_id=1, source_target_pairs={{0,3},{1,2},{2,1},{3,0},{4,7},{5,6},{6,5},{7,4},{8,11},{9,10},{10,... | collective-permute-start | bytes 786440 | tf_op jit(solution)/shard_map/ppermute | solution.py:248
  12.6 21.8 %collective-permute-start.4 = (bf16[2048,128]{1,0:T(8,128)(2,1)S(1)}, bf16[2048,128]{1,0:T(8,128)(2,1)S(1)}, u32[]{:S(2)}, u32[]{:S(2)}) collective-permute-start(bf16[2048,128]{1,0:T(8,128)(2,1)S(1)} %get-tuple-element.14), channel_id=1, source_target_pairs={{0,12},{12,0},{1,13},{13,1},{2,14},{14,2},{3,15},{15,3},{16,28},{2... | collective-permute-start | bytes 1572872 | tf_op jit(solution)/shard_map/ppermute | solution.py:220
  15.9 28.3 %collective-permute-start.1 = (bf16[2048,128]{1,0:T(8,128)(2,1)S(1)}, bf16[2048,128]{1,0:T(8,128)(2,1)S(1)}, u32[]{:S(2)}, u32[]{:S(2)}) collective-permute-start(bf16[2048,128]{1,0:T(8,128)(2,1)S(1)} %collective-permute-done.cross_ref), channel_id=1, source_target_pairs={{4,0},{8,12},{5,1},{9,13},{6,2},{10,14},{7,3},{11,15},{20,16},{24,... | collective-permute-start | bytes 1572872 | tf_op jit(solution)/shard_map/ppermute | solution.py:221
  21.7 22.5 %collective-permute-start.3 = (bf16[2048,128]{1,0:T(8,128)(2,1)S(1)}, bf16[2048,128]{1,0:T(8,128)(2,1)S(1)}, u32[]{:S(2)}, u32[]{:S(2)}) collective-permute-start(bf16[2048,128]{1,0:T(8,128)(2,1)S(1)} %collective-permute-done.2.near_ref), channel_id=1, source_target_pairs={{4,8},{8,4},{5,9},{9,5},{6,10},{10,6},{7,11},{11,7},{20,24},{24,20... | collective-permute-start | bytes 1572872 | tf_op jit(solution)/shard_map/ppermute | solution.py:222
  24.7 1.0 %copy-start.5 = (bf16[512,512]{1,0:T(8,128)(2,1)S(1)}, bf16[512,512]{1,0:T(8,128)(2,1)}, u32[]{:S(2)}) copy-start(bf16[512,512]{1,0:T(8,128)(2,1)} %constant.4.clone.fwd_ref) | copy-start | bytes 1572868
  30.5 2.3 %collective-permute-start.9 = (f32[40,2048]{1,0:T(8,128)S(1)}, f32[40,2048]{1,0:T(8,128)S(1)}, u32[]{:S(2)}, u32[]{:S(2)}) collective-permute-start(f32[40,2048]{1,0:T(8,128)S(1)} %get-tuple-element.19), channel_id=1, source_target_pairs={{0,1},{1,0},{2,3},{3,2},{4,5},{5,4},{6,7},{7,6},{8,9},{9,8},{10,11... | collective-permute-start | bytes 983048 | tf_op jit(solution)/shard_map/ppermute | solution.py:248
  31.1 1.6 %collective-permute-start.8 = (f32[32,2048]{1,0:T(8,128)S(1)}, f32[32,2048]{1,0:T(8,128)S(1)}, u32[]{:S(2)}, u32[]{:S(2)}) collective-permute-start(f32[32,2048]{1,0:T(8,128)S(1)} %get-tuple-element.18), channel_id=1, source_target_pairs={{0,1},{1,0},{2,3},{3,2},{4,5},{5,4},{6,7},{7,6},{8,9},{9,8},{10,11... | collective-permute-start | bytes 786440 | tf_op jit(solution)/shard_map/ppermute | solution.py:248
  45.0 1.2 %collective-permute-start.10 = (f32[8,128]{1,0:T(8,128)S(1)}, f32[8,128]{1,0:T(8,128)S(1)}, u32[]{:S(2)}, u32[]{:S(2)}) collective-permute-start(f32[8,128]{1,0:T(8,128)S(1)} %get-tuple-element.25), channel_id=1, source_target_pairs={{0,1},{1,0},{2,3},{3,2},{4,5},{5,4},{6,7},{7,6},{8,9},{9,8},{10,11... | collective-permute-start | bytes 12296 | tf_op jit(solution)/shard_map/ppermute | solution.py:248
  46.2 3.0 %collective-permute-start.11 = (f32[8,128]{1,0:T(8,128)S(1)}, f32[8,128]{1,0:T(8,128)S(1)}, u32[]{:S(2)}, u32[]{:S(2)}) collective-permute-start(f32[8,128]{1,0:T(8,128)S(1)} %add.6), channel_id=1, source_target_pairs={{0,3},{1,2},{2,1},{3,0},{4,7},{5,6},{6,5},{7,4},{8,11},{9,10},{10,... | collective-permute-start | bytes 12296 | tf_op jit(solution)/shard_map/ppermute | solution.py:248
  49.2 5.5 %collective-permute-start.12 = (f32[8,128]{1,0:T(8,128)S(1)}, f32[8,128]{1,0:T(8,128)S(1)}, u32[]{:S(2)}, u32[]{:S(2)}) collective-permute-start(f32[8,128]{1,0:T(8,128)S(1)} %add.7.refs_0_), channel_id=1, source_target_pairs={{0,13},{1,12},{2,15},{3,14},{4,9},{5,8},{6,11},{7,10},{8,5},{9,4},... | collective-permute-start | bytes 12296 | tf_op jit(solution)/shard_map/ppermute | solution.py:342
  51.2 3.9 %collective-permute-start.13 = (f32[8,128]{1,0:T(8,128)S(1)}, f32[8,128]{1,0:T(8,128)S(1)}, u32[]{:S(2)}, u32[]{:S(2)}) collective-permute-start(f32[8,128]{1,0:T(8,128)S(1)} %add.7.refs_0_), channel_id=1, source_target_pairs={{0,9},{1,8},{2,11},{3,10},{4,13},{5,12},{6,15},{7,14},{8,1},{9,0},... | collective-permute-start | bytes 12296 | tf_op jit(solution)/shard_map/ppermute | solution.py:342
  51.4 3.7 %collective-permute-start.14 = (f32[8,128]{1,0:T(8,128)S(1)}, f32[8,128]{1,0:T(8,128)S(1)}, u32[]{:S(2)}, u32[]{:S(2)}) collective-permute-start(f32[8,128]{1,0:T(8,128)S(1)} %add.7.refs_0_), channel_id=1, source_target_pairs={{0,5},{1,4},{2,7},{3,6},{4,1},{5,0},{6,3},{7,2},{8,13},{9,12},{10,... | collective-permute-start | bytes 12296 | tf_op jit(solution)/shard_map/ppermute | solution.py:342

commit v7 on v6

--- a/solution.py
+++ b/solution.py
@@ -43,7 +43,7 @@
         out_ref[rows, :] = jnp.concatenate([re, im], axis=1).astype(BF16)
 
 
-def pack_time(harm, bodies, reals, vel_ref, own_ref, send_ref, again_ref):
+def pack_time(harm, bodies, reals, vel_ref, own_ref, send_ref):
     core = lax.axis_index("harm") % 2
     half = bodies // 2
     pair = bodies // 4
@@ -52,7 +52,6 @@
             one = vel_ref[pl.ds(which * half + j, 2 * harm, stride=bodies), :]
             two = vel_ref[pl.ds(which * half + pair + j, 2 * harm, stride=bodies), :]
             out_ref[:, pl.ds(j * 2 * reals, 2 * reals)] = jnp.concatenate([one, two], axis=1).astype(BF16)
-    pack_couple(harm, bodies, reals, vel_ref, again_ref)
 
 
 def time_kernel(harm, bodies, reals, quad_ref, coul_ref, own_ref, core_ref, far_ref, far_core_ref, fwd_ref, inv_ref,
@@ -214,10 +213,10 @@
     out_ref[0] = jnp.sqrt(mean)[0, 0]
 
 
-def gather_line(x, again, axis):
+def gather_line(x, axis):
     near = lax.ppermute(x, axis, [(0, 1), (1, 0), (2, 3), (3, 2)])
     cross = lax.ppermute(x, axis, [(1, 2), (2, 1)])
-    across = lax.ppermute(again, axis, [(0, 3), (3, 0)])
+    across = lax.ppermute(x, axis, [(0, 3), (3, 0)])
     outer = lax.ppermute(cross, axis, [(1, 0), (2, 3)])
     inner = lax.ppermute(near, axis, [(1, 2), (2, 1)])
     return x, near, cross, across, outer, inner
@@ -255,19 +254,18 @@
             name="pack_couple",
         )(flat)
         columns = bodies * reals // 2
-        own, send, again = pl.pallas_call(
+        own, send = pl.pallas_call(
             functools.partial(pack_time, harm, bodies, reals),
             in_specs=[VMEM],
             out_shape=(
                 *[jax.ShapeDtypeStruct((2 * harm, columns), BF16)] * 2,
-                jax.ShapeDtypeStruct((total_rows, group), BF16),
             ),
             compiler_params=params(),
             cost_estimate=cost(0, 1 << 10),
             name="pack_time",
         )(flat)
         if body_count == 4:
-            pieces = gather_line(low, again, "body")
+            pieces = gather_line(low, "body")
         else:
             pieces = (lax.all_gather(low, "body").reshape(body_count, harm, bodies, group),)
 
@@ -334,8 +332,7 @@
             name="finish",
         )(res, factor_p, factor_q, vel_dense)
 
-        total = total + flipped(total, 1)
-        total = total + flipped(total, 3)
+        total = total + sum(flipped(total, flip) for flip in (3, 2, 1))
 
         def crossed(flip):
             pairs = [(4 * i + j, 4 * (i ^ flip) + (j ^ 1)) for i in range(body_count) for j in range(4)]

time: 55.9 us -> 55.9 us (level)
    ppermute x7 -> x8, waiting for transfers between devices: 6.7 us -> 6.09 us  [flipped(): return lax.ppermute(x, 'harm', [(i, i ^ flip) for i in range(4)])]
    ppermute x7 -> x8, starting transfers between devices: 4.01 us -> 4.58 us  [flipped(): return lax.ppermute(x, 'harm', [(i, i ^ flip) for i in range(4)])]
  transfers between devices with their start and end apart: 15 -> 16, of which waited for: 7 -> 7; matrix products, arithmetic and copies ran while one was open for 0% -> 0% of each run, Pallas kernels for 19% -> 18%
where the time goes in v7:
time: 55.9 us; the launch traced here: 55.6 us
  waiting for transfers between devices  20.4 us (36%)
  starting transfers between devices  20.2 us (36%)
  Pallas kernels  11.6 us (21%)
  local copies, waits for them, and re-layouts  2.66 us (5%)
  between operations  0.81 us (1%)
    ppermute x1, waiting for transfers between devices, gather_line(): outer = lax.ppermute(cross, axis, [(1, 0), (2, 3)])  9.09 us
    ppermute x8, waiting for transfers between devices, flipped(): return lax.ppermute(x, 'harm', [(i, i ^ flip) for i in range(4)])  6.09 us
    ppermute x1, starting transfers between devices, gather_line(): near = lax.ppermute(x, axis, [(0, 1), (1, 0), (2, 3), (3, 2)])  6.01 us
    pallas_call x1, Pallas kernels, local(): pl.pallas_call(functools.partial(time_kernel, harm, bodies, reals), grid=...  4.77 us
    ppermute x1, waiting for transfers between devices, gather_line(): near = lax.ppermute(x, axis, [(0, 1), (1, 0), (2, 3), (3, 2)])  4.68 us
    ppermute x8, starting transfers between devices, flipped(): return lax.ppermute(x, 'harm', [(i, i ^ flip) for i in range(4)])  4.58 us
    ppermute x3, starting transfers between devices, crossed(): return lax.ppermute(total, ('body', 'harm'), pairs)  3.55 us
    ppermute x1, starting transfers between devices, gather_line(): across = lax.ppermute(x, axis, [(0, 3), (3, 0)])  3.25 us
  transfers between devices with their start and end apart: 16, of which 7 were waited for; matrix products, arithmetic and copies ran while one was open for 0% of the time, Pallas kernels for 18%

profile of v7, /device:TPU:0, one launch (start us, length us, event | category | flops | bytes accessed | tf_op | source)
XLA Modules:
  0.0 55.6 jit_solution(13559936467031748806)
XLA Ops:
  0.6 0.0 copy-start.6
  0.7 0.0 copy-start.1
  0.7 1.6 %copy-done.1 = f32[2,32,64,64]{3,2,1,0:T(8,128)S(1)} copy-done((f32[2,32,64,64]{3,2,1,0:T(8,128)S(1)}, f32[2,32,64,64]{3,2,1,0:T(8,128)}, u32[]{:S(2)}) %copy-start.1) | copy-done | bytes 1048600
  2.3 0.2 pack_couple.1.own_ref
  2.5 0.0 copy-start
  2.5 0.0 copy-start.2
  2.5 0.8 %collective-permute-start = (bf16[2048,128]{1,0:T(8,128)(2,1)S(1)}, bf16[2048,128]{1,0:T(8,128)(2,1)S(1)}, u32[]{:S(2)}, u32[]{:S(2)}) collective-permute-start(bf16[2048,128]{1,0:T(8,128)(2,1)S(1)} %pack_couple.1.own_ref), channel_id=1, source_target_pairs={{4,8},{8,4},{5,9},{9,5},{6,10},{10,6},{7,11},{11,7},{20,24},{24,20... | collective-permute-start | bytes 1572872 | tf_op jit(solution)/shard_map/ppermute | solution.py:218
  3.3 6.0 %collective-permute-start.2 = (bf16[2048,128]{1,0:T(8,128)(2,1)S(1)}, bf16[2048,128]{1,0:T(8,128)(2,1)S(1)}, u32[]{:S(2)}, u32[]{:S(2)}) collective-permute-start(bf16[2048,128]{1,0:T(8,128)(2,1)S(1)} %pack_couple.1.own_ref), channel_id=1, source_target_pairs={{0,4},{4,0},{8,12},{12,8},{1,5},{5,1},{9,13},{13,9},{2,6},{6,2},{1... | collective-permute-start | bytes 1572872 | tf_op jit(solution)/shard_map/ppermute | solution.py:217
  9.3 1.2 %pack_time.1 = (bf16[64,2048]{1,0:T(8,128)(2,1)S(1)}, bf16[64,2048]{1,0:T(8,128)(2,1)S(1)}) custom-call(f32[4096,64]{1,0:T(8,128)S(1)} %bitcast.4), custom_call_target="tpu_custom_call" | custom-call | bytes 1024 | tf_op jit(solution)/shard_map/pack_time/pallas_call | solution.py:257
  10.5 0.1 collective-permute-start.5
  10.6 1.6 %collective-permute-start.6 = (bf16[64,2048]{1,0:T(8,128)(2,1)S(1)}, bf16[64,2048]{1,0:T(8,128)(2,1)S(1)}, u32[]{:S(2)}, u32[]{:S(2)}) collective-permute-start(bf16[64,2048]{1,0:T(8,128)(2,1)S(1)} %get-tuple-element.13.own_ref), channel_id=1, source_target_pairs={{0,2},{1,3},{2,0},{3,1},{4,6},{5,7},{6,4},{7,5},{8,10},{9,11},{10,... | collective-permute-start | bytes 786440 | tf_op jit(solution)/shard_map/ppermute | solution.py:247
  12.2 0.3 collective-permute-start.7
  12.5 0.0 collective-permute-done.5.core_ref
  12.5 3.2 %collective-permute-start.4 = (bf16[2048,128]{1,0:T(8,128)(2,1)S(1)}, bf16[2048,128]{1,0:T(8,128)(2,1)S(1)}, u32[]{:S(2)}, u32[]{:S(2)}) collective-permute-start(bf16[2048,128]{1,0:T(8,128)(2,1)S(1)} %pack_couple.1.own_ref), channel_id=1, source_target_pairs={{0,12},{12,0},{1,13},{13,1},{2,14},{14,2},{3,15},{15,3},{16,28},{2... | collective-permute-start | bytes 1572872 | tf_op jit(solution)/shard_map/ppermute | solution.py:219
  15.7 0.0 collective-permute-done.cross_ref
  15.7 1.3 %collective-permute-start.1 = (bf16[2048,128]{1,0:T(8,128)(2,1)S(1)}, bf16[2048,128]{1,0:T(8,128)(2,1)S(1)}, u32[]{:S(2)}, u32[]{:S(2)}) collective-permute-start(bf16[2048,128]{1,0:T(8,128)(2,1)S(1)} %collective-permute-done.cross_ref), channel_id=1, source_target_pairs={{4,0},{8,12},{5,1},{9,13},{6,2},{10,14},{7,3},{11,15},{20,16},{24,... | collective-permute-start | bytes 1572872 | tf_op jit(solution)/shard_map/ppermute | solution.py:220
  17.0 4.7 %collective-permute-done.2.near_ref = bf16[2048,128]{1,0:T(8,128)(2,1)S(1)} collective-permute-done((bf16[2048,128]{1,0:T(8,128)(2,1)S(1)}, bf16[2048,128]{1,0:T(8,128)(2,1)S(1)}, u32[]{:S(2)}, u32[]{:S(2)}) %collective-permute-start.2) | collective-permute-done | bytes 524320 | tf_op jit(solution)/shard_map/ppermute | solution.py:217
  21.7 0.7 %collective-permute-start.3 = (bf16[2048,128]{1,0:T(8,128)(2,1)S(1)}, bf16[2048,128]{1,0:T(8,128)(2,1)S(1)}, u32[]{:S(2)}, u32[]{:S(2)}) collective-permute-start(bf16[2048,128]{1,0:T(8,128)(2,1)S(1)} %collective-permute-done.2.near_ref), channel_id=1, source_target_pairs={{4,8},{8,4},{5,9},{9,5},{6,10},{10,6},{7,11},{11,7},{20,24},{24,20... | collective-permute-start | bytes 1572872 | tf_op jit(solution)/shard_map/ppermute | solution.py:221
  22.4 0.0 collective-permute-done.6.far_ref
  22.4 2.1 %collective-permute-done.7.far_core_ref = bf16[64,2048]{1,0:T(8,128)(2,1)S(1)} collective-permute-done((bf16[64,2048]{1,0:T(8,128)(2,1)S(1)}, bf16[64,2048]{1,0:T(8,128)(2,1)S(1)}, u32[]{:S(2)}, u32[]{:S(2)}) %collective-permute-start.7) | collective-permute-done | bytes 262176 | tf_op jit(solution)/shard_map/ppermute | solution.py:247
  24.5 0.0 copy-start.5
  24.5 1.0 %copy-done.5 = bf16[512,512]{1,0:T(8,128)(2,1)S(1)} copy-done((bf16[512,512]{1,0:T(8,128)(2,1)S(1)}, bf16[512,512]{1,0:T(8,128)(2,1)}, u32[]{:S(2)}) %copy-start.5) | copy-done | bytes 524312
  25.5 4.8 %time_kernel.1 = (f32[72,2048]{1,0:T(8,128)S(1)}, f32[32,2048]{1,0:T(8,128)S(1)}, f32[40,2048]{1,0:T(8,128)S(1)}) custom-call(f32[64]{0:T(128)S(1)} %copy-done.6, f32[64]{0:T(128)S(1)} %copy-done.7, bf16[64,2048]{1,0:T(8,128)(2,1)S(1)} %get-tuple-element.13.own_ref, bf16[64,2048]{1,0:T(8,128)(2,1)S(1)} %collective-permute-done.5.core_ref, ...), custom_call_target="tpu_custom_call" | custom-call | bytes 1024 | tf_op jit(solution)/shard_map/time_kernel/pallas_call | solution.py:279
  30.3 0.6 %collective-permute-start.9 = (f32[40,2048]{1,0:T(8,128)S(1)}, f32[40,2048]{1,0:T(8,128)S(1)}, u32[]{:S(2)}, u32[]{:S(2)}) collective-permute-start(f32[40,2048]{1,0:T(8,128)S(1)} %get-tuple-element.17), channel_id=1, source_target_pairs={{0,1},{1,0},{2,3},{3,2},{4,5},{5,4},{6,7},{7,6},{8,9},{9,8},{10,11... | collective-permute-start | bytes 983048 | tf_op jit(solution)/shard_map/ppermute | solution.py:247
  30.9 0.1 collective-permute-start.8
  31.0 1.6 %collective-permute-done.8.other_re_ref = f32[32,2048]{1,0:T(8,128)S(1)} collective-permute-done((f32[32,2048]{1,0:T(8,128)S(1)}, f32[32,2048]{1,0:T(8,128)S(1)}, u32[]{:S(2)}, u32[]{:S(2)}) %collective-permute-start.8) | collective-permute-done | bytes 262176 | tf_op jit(solution)/shard_map/ppermute | solution.py:247
  32.6 0.0 collective-permute-done.9.other_im_ref
  32.6 0.0 copy-done
  32.6 1.6 %prepare.1 = (f32[2048,128]{1,0:T(8,128)S(1)}, f32[2048,128]{1,0:T(8,128)S(1)}, f32[2048,128]{1,0:T(8,128)S(1)}, f32[2048,128]{1,0:T(8,128)S(1)}) custom-call(bf16[2,32,64,256]{3,2,1,0:T(8,128)(2,1)S(1)} %copy-done, f32[72,2048]{1,0:T(8,128)S(1)} %get-tuple-element.15.mine_ref, f32[32,2048]{1,0:T(8,128)S(1)} %collective-permute-done.8.other_re_ref, ...), custom_call_target="tpu_custom_call" | custom-call | bytes 1024 | tf_op jit(solution)/shard_map/prepare/pallas_call | solution.py:292
  34.2 0.0 collective-permute-done.4.across_ref
  34.2 0.9 %partial.1.refs_2_ = f32[2048,128]{1,0:T(8,128)S(1)} custom-call(bf16[2,32,64,256]{3,2,1,0:T(8,128)(2,1)S(1)} %copy-done, bf16[2048,128]{1,0:T(8,128)(2,1)S(1)} %pack_couple.1.own_ref, bf16[2048,128]{1,0:T(8,128)(2,1)S(1)} %collective-permute-done.2.near_ref, bf16[2048,128]{1,0:T(8,128)(2,1)S(1)} %collective-permute-done.cross_ref, ...), custom_call_target="tpu_custom_call" | custom-call | bytes 1024 | tf_op jit(solution)/shard_map/partial/pallas_call | solution.py:303
  35.2 9.1 %collective-permute-done.1.refs_0_ = bf16[2048,128]{1,0:T(8,128)(2,1)S(1)} collective-permute-done((bf16[2048,128]{1,0:T(8,128)(2,1)S(1)}, bf16[2048,128]{1,0:T(8,128)(2,1)S(1)}, u32[]{:S(2)}, u32[]{:S(2)}) %collective-permute-start.1) | collective-permute-done | bytes 524320 | tf_op jit(solution)/shard_map/ppermute | solution.py:220
  44.2 0.0 collective-permute-done.3.refs_1_
  44.2 0.7 %couple.1 = (f32[2048,128]{1,0:T(8,128)S(1)}, f32[8,128]{1,0:T(8,128)S(1)}) custom-call(bf16[2,32,64,256]{3,2,1,0:T(8,128)(2,1)S(1)} %copy-done, bf16[2048,128]{1,0:T(8,128)(2,1)S(1)} %collective-permute-done.1.refs_0_, bf16[2048,128]{1,0:T(8,128)(2,1)S(1)} %collective-permute-done.3.refs_1_, f32[2048,128]{1,0:T(8,128)S(1)} %partial.1.refs_2_), custom_call_target="tpu_custom_call" | custom-call | bytes 1024 | tf_op jit(solution)/shard_map/couple/pallas_call | solution.py:313
  45.0 0.8 %collective-permute-start.10 = (f32[8,128]{1,0:T(8,128)S(1)}, f32[8,128]{1,0:T(8,128)S(1)}, u32[]{:S(2)}, u32[]{:S(2)}) collective-permute-start(f32[8,128]{1,0:T(8,128)S(1)} %get-tuple-element.23), channel_id=1, source_target_pairs={{0,3},{1,2},{2,1},{3,0},{4,7},{5,6},{6,5},{7,4},{8,11},{9,10},{10,... | collective-permute-start | bytes 12296 | tf_op jit(solution)/shard_map/ppermute | solution.py:247
  45.7 0.9 %collective-permute-start.11 = (f32[8,128]{1,0:T(8,128)S(1)}, f32[8,128]{1,0:T(8,128)S(1)}, u32[]{:S(2)}, u32[]{:S(2)}) collective-permute-start(f32[8,128]{1,0:T(8,128)S(1)} %get-tuple-element.23), channel_id=1, source_target_pairs={{0,2},{1,3},{2,0},{3,1},{4,6},{5,7},{6,4},{7,5},{8,10},{9,11},{10,... | collective-permute-start | bytes 12296 | tf_op jit(solution)/shard_map/ppermute | solution.py:247
  46.6 0.3 collective-permute-start.12
  46.9 1.2 %collective-permute-done.10 = f32[8,128]{1,0:T(8,128)S(1)} collective-permute-done((f32[8,128]{1,0:T(8,128)S(1)}, f32[8,128]{1,0:T(8,128)S(1)}, u32[]{:S(2)}, u32[]{:S(2)}) %collective-permute-start.10) | collective-permute-done | bytes 4128 | tf_op jit(solution)/shard_map/ppermute | solution.py:247
  48.1 1.3 %collective-permute-done.11 = f32[8,128]{1,0:T(8,128)S(1)} collective-permute-done((f32[8,128]{1,0:T(8,128)S(1)}, f32[8,128]{1,0:T(8,128)S(1)}, u32[]{:S(2)}, u32[]{:S(2)}) %collective-permute-start.11) | collective-permute-done | bytes 4128 | tf_op jit(solution)/shard_map/ppermute | solution.py:247
  49.3 0.0 collective-permute-done.12
  49.3 1.8 %collective-permute-start.13 = (f32[8,128]{1,0:T(8,128)S(1)}, f32[8,128]{1,0:T(8,128)S(1)}, u32[]{:S(2)}, u32[]{:S(2)}) collective-permute-start(f32[8,128]{1,0:T(8,128)S(1)} %add_add_fusion.refs_0_), channel_id=1, source_target_pairs={{0,13},{1,12},{2,15},{3,14},{4,9},{5,8},{6,11},{7,10},{8,5},{9,4},... | collective-permute-start | bytes 12296 | tf_op jit(solution)/shard_map/ppermute | solution.py:339
  51.1 0.8 %collective-permute-start.14 = (f32[8,128]{1,0:T(8,128)S(1)}, f32[8,128]{1,0:T(8,128)S(1)}, u32[]{:S(2)}, u32[]{:S(2)}) collective-permute-start(f32[8,128]{1,0:T(8,128)S(1)} %add_add_fusion.refs_0_), channel_id=1, source_target_pairs={{0,9},{1,8},{2,11},{3,10},{4,13},{5,12},{6,15},{7,14},{8,1},{9,0},... | collective-permute-start | bytes 12296 | tf_op jit(solution)/shard_map/ppermute | solution.py:339
  52.0 0.9 %collective-permute-start.15 = (f32[8,128]{1,0:T(8,128)S(1)}, f32[8,128]{1,0:T(8,128)S(1)}, u32[]{:S(2)}, u32[]{:S(2)}) collective-permute-start(f32[8,128]{1,0:T(8,128)S(1)} %add_add_fusion.refs_0_), channel_id=1, source_target_pairs={{0,5},{1,4},{2,7},{3,6},{4,1},{5,0},{6,3},{7,2},{8,13},{9,12},{10,... | collective-permute-start | bytes 12296 | tf_op jit(solution)/shard_map/ppermute | solution.py:339
  52.9 1.7 %finish.1 = f32[2,2048,64]{2,1,0:T(8,128)} custom-call(f32[2048,128]{1,0:T(8,128)S(1)} %get-tuple-element.19.res_ref, f32[2048,128]{1,0:T(8,128)S(1)} %get-tuple-element.20.p_ref, f32[2048,128]{1,0:T(8,128)S(1)} %get-tuple-element.21.q_ref, f32[2048,128]{1,0:T(8,128)S(1)} %get-tuple-element.22.vel_ref), custom_call_target="tpu_custom_call" | custom-call | bytes 1024 | tf_op jit(solution)/shard_map/finish/pallas_call | solution.py:324
  54.6 0.0 collective-permute-done.13.refs_1_
  54.6 0.5 collective-permute-done.14.refs_2_
  55.0 0.0 collective-permute-done.15.refs_3_
  55.0 0.6 %rms.1 = f32[1]{0:T(128)} custom-call(f32[8,128]{1,0:T(8,128)S(1)} %add_add_fusion.refs_0_, f32[8,128]{1,0:T(8,128)S(1)} %collective-permute-done.13.refs_1_, f32[8,128]{1,0:T(8,128)S(1)} %collective-permute-done.14.refs_2_, f32[8,128]{1,0:T(8,128)S(1)} %collective-permute-done.15.refs_3_), custom_call_target="tpu_custom_call" | custom-call | tf_op jit(solution)/shard_map/rms/pallas_call | solution.py:344
  (9 shorter events, 0.0 us)
Async XLA Ops:
  0.6 23.9 %copy-start.6 = (f32[64]{0:T(128)S(1)}, f32[64]{0:T(128)}, u32[]{:S(2)}) copy-start(f32[64]{0:T(128)} %quad_ref.1) | copy-start | bytes 772
  0.6 23.8 %copy-start.7 = (f32[64]{0:T(128)S(1)}, f32[64]{0:T(128)}, u32[]{:S(2)}) copy-start(f32[64]{0:T(128)} %coul_ref.1) | copy-start | bytes 772
  0.7 1.6 %copy-start.1 = (f32[2,32,64,64]{3,2,1,0:T(8,128)S(1)}, f32[2,32,64,64]{3,2,1,0:T(8,128)}, u32[]{:S(2)}) copy-start(f32[2,32,64,64]{3,2,1,0:T(8,128)} %param.7) | copy-start | bytes 3145732
  2.3 22.2 %copy-start.4 = (bf16[256,1536]{1,0:T(8,128)(2,1)S(1)}, bf16[256,1536]{1,0:T(8,128)(2,1)}, u32[]{:S(2)}) copy-start(bf16[256,1536]{1,0:T(8,128)(2,1)} %constant.5.clone.inv_ref) | copy-start | bytes 2359300
  2.3 30.3 %copy-start.3 = (f32[2,32,64,64]{3,2,1,0:T(8,128)S(1)}, f32[2,32,64,64]{3,2,1,0:T(8,128)}, u32[]{:S(2)}) copy-start(f32[2,32,64,64]{3,2,1,0:T(8,128)} %param.9) | copy-start | bytes 3145732
  2.5 30.1 %copy-start = (bf16[2,32,64,256]{3,2,1,0:T(8,128)(2,1)S(1)}, bf16[2,32,64,256]{3,2,1,0:T(8,128)(2,1)}, u32[]{:S(2)}) copy-start(bf16[2,32,64,256]{3,2,1,0:T(8,128)(2,1)} %imped_ref.5) | copy-start | bytes 6291460
  2.5 30.1 %copy-start.2 = (f32[2,32,64,64]{3,2,1,0:T(8,128)S(1)}, f32[2,32,64,64]{3,2,1,0:T(8,128)}, u32[]{:S(2)}) copy-start(f32[2,32,64,64]{3,2,1,0:T(8,128)} %param.7) | copy-start | bytes 3145732
  2.5 13.2 %collective-permute-start = (bf16[2048,128]{1,0:T(8,128)(2,1)S(1)}, bf16[2048,128]{1,0:T(8,128)(2,1)S(1)}, u32[]{:S(2)}, u32[]{:S(2)}) collective-permute-start(bf16[2048,128]{1,0:T(8,128)(2,1)S(1)} %pack_couple.1.own_ref), channel_id=1, source_target_pairs={{4,8},{8,4},{5,9},{9,5},{6,10},{10,6},{7,11},{11,7},{20,24},{24,20... | collective-permute-start | bytes 1572872 | tf_op jit(solution)/shard_map/ppermute | solution.py:218
  3.3 18.4 %collective-permute-start.2 = (bf16[2048,128]{1,0:T(8,128)(2,1)S(1)}, bf16[2048,128]{1,0:T(8,128)(2,1)S(1)}, u32[]{:S(2)}, u32[]{:S(2)}) collective-permute-start(bf16[2048,128]{1,0:T(8,128)(2,1)S(1)} %pack_couple.1.own_ref), channel_id=1, source_target_pairs={{0,4},{4,0},{8,12},{12,8},{1,5},{5,1},{9,13},{13,9},{2,6},{6,2},{1... | collective-permute-start | bytes 1572872 | tf_op jit(solution)/shard_map/ppermute | solution.py:217
  10.5 1.9 %collective-permute-start.5 = (bf16[64,2048]{1,0:T(8,128)(2,1)S(1)}, bf16[64,2048]{1,0:T(8,128)(2,1)S(1)}, u32[]{:S(2)}, u32[]{:S(2)}) collective-permute-start(bf16[64,2048]{1,0:T(8,128)(2,1)S(1)} %get-tuple-element.14), channel_id=1, source_target_pairs={{0,1},{1,0},{2,3},{3,2},{4,5},{5,4},{6,7},{7,6},{8,9},{9,8},{10,11... | collective-permute-start | bytes 786440 | tf_op jit(solution)/shard_map/ppermute | solution.py:247
  10.6 11.8 %collective-permute-start.6 = (bf16[64,2048]{1,0:T(8,128)(2,1)S(1)}, bf16[64,2048]{1,0:T(8,128)(2,1)S(1)}, u32[]{:S(2)}, u32[]{:S(2)}) collective-permute-start(bf16[64,2048]{1,0:T(8,128)(2,1)S(1)} %get-tuple-element.13.own_ref), channel_id=1, source_target_pairs={{0,2},{1,3},{2,0},{3,1},{4,6},{5,7},{6,4},{7,5},{8,10},{9,11},{10,... | collective-permute-start | bytes 786440 | tf_op jit(solution)/shard_map/ppermute | solution.py:247
  12.2 12.3 %collective-permute-start.7 = (bf16[64,2048]{1,0:T(8,128)(2,1)S(1)}, bf16[64,2048]{1,0:T(8,128)(2,1)S(1)}, u32[]{:S(2)}, u32[]{:S(2)}) collective-permute-start(bf16[64,2048]{1,0:T(8,128)(2,1)S(1)} %get-tuple-element.14), channel_id=1, source_target_pairs={{0,3},{1,2},{2,1},{3,0},{4,7},{5,6},{6,5},{7,4},{8,11},{9,10},{10,... | collective-permute-start | bytes 786440 | tf_op jit(solution)/shard_map/ppermute | solution.py:247
  12.5 21.8 %collective-permute-start.4 = (bf16[2048,128]{1,0:T(8,128)(2,1)S(1)}, bf16[2048,128]{1,0:T(8,128)(2,1)S(1)}, u32[]{:S(2)}, u32[]{:S(2)}) collective-permute-start(bf16[2048,128]{1,0:T(8,128)(2,1)S(1)} %pack_couple.1.own_ref), channel_id=1, source_target_pairs={{0,12},{12,0},{1,13},{13,1},{2,14},{14,2},{3,15},{15,3},{16,28},{2... | collective-permute-start | bytes 1572872 | tf_op jit(solution)/shard_map/ppermute | solution.py:219
  15.7 28.5 %collective-permute-start.1 = (bf16[2048,128]{1,0:T(8,128)(2,1)S(1)}, bf16[2048,128]{1,0:T(8,128)(2,1)S(1)}, u32[]{:S(2)}, u32[]{:S(2)}) collective-permute-start(bf16[2048,128]{1,0:T(8,128)(2,1)S(1)} %collective-permute-done.cross_ref), channel_id=1, source_target_pairs={{4,0},{8,12},{5,1},{9,13},{6,2},{10,14},{7,3},{11,15},{20,16},{24,... | collective-permute-start | bytes 1572872 | tf_op jit(solution)/shard_map/ppermute | solution.py:220
  21.7 22.5 %collective-permute-start.3 = (bf16[2048,128]{1,0:T(8,128)(2,1)S(1)}, bf16[2048,128]{1,0:T(8,128)(2,1)S(1)}, u32[]{:S(2)}, u32[]{:S(2)}) collective-permute-start(bf16[2048,128]{1,0:T(8,128)(2,1)S(1)} %collective-permute-done.2.near_ref), channel_id=1, source_target_pairs={{4,8},{8,4},{5,9},{9,5},{6,10},{10,6},{7,11},{11,7},{20,24},{24,20... | collective-permute-start | bytes 1572872 | tf_op jit(solution)/shard_map/ppermute | solution.py:221
  24.5 1.0 %copy-start.5 = (bf16[512,512]{1,0:T(8,128)(2,1)S(1)}, bf16[512,512]{1,0:T(8,128)(2,1)}, u32[]{:S(2)}) copy-start(bf16[512,512]{1,0:T(8,128)(2,1)} %constant.4.clone.fwd_ref) | copy-start | bytes 1572868
  30.3 2.3 %collective-permute-start.9 = (f32[40,2048]{1,0:T(8,128)S(1)}, f32[40,2048]{1,0:T(8,128)S(1)}, u32[]{:S(2)}, u32[]{:S(2)}) collective-permute-start(f32[40,2048]{1,0:T(8,128)S(1)} %get-tuple-element.17), channel_id=1, source_target_pairs={{0,1},{1,0},{2,3},{3,2},{4,5},{5,4},{6,7},{7,6},{8,9},{9,8},{10,11... | collective-permute-start | bytes 983048 | tf_op jit(solution)/shard_map/ppermute | solution.py:247
  30.9 1.6 %collective-permute-start.8 = (f32[32,2048]{1,0:T(8,128)S(1)}, f32[32,2048]{1,0:T(8,128)S(1)}, u32[]{:S(2)}, u32[]{:S(2)}) collective-permute-start(f32[32,2048]{1,0:T(8,128)S(1)} %get-tuple-element.16), channel_id=1, source_target_pairs={{0,1},{1,0},{2,3},{3,2},{4,5},{5,4},{6,7},{7,6},{8,9},{9,8},{10,11... | collective-permute-start | bytes 786440 | tf_op jit(solution)/shard_map/ppermute | solution.py:247
  45.0 3.1 %collective-permute-start.10 = (f32[8,128]{1,0:T(8,128)S(1)}, f32[8,128]{1,0:T(8,128)S(1)}, u32[]{:S(2)}, u32[]{:S(2)}) collective-permute-start(f32[8,128]{1,0:T(8,128)S(1)} %get-tuple-element.23), channel_id=1, source_target_pairs={{0,3},{1,2},{2,1},{3,0},{4,7},{5,6},{6,5},{7,4},{8,11},{9,10},{10,... | collective-permute-start | bytes 12296 | tf_op jit(solution)/shard_map/ppermute | solution.py:247
  45.7 3.6 %collective-permute-start.11 = (f32[8,128]{1,0:T(8,128)S(1)}, f32[8,128]{1,0:T(8,128)S(1)}, u32[]{:S(2)}, u32[]{:S(2)}) collective-permute-start(f32[8,128]{1,0:T(8,128)S(1)} %get-tuple-element.23), channel_id=1, source_target_pairs={{0,2},{1,3},{2,0},{3,1},{4,6},{5,7},{6,4},{7,5},{8,10},{9,11},{10,... | collective-permute-start | bytes 12296 | tf_op jit(solution)/shard_map/ppermute | solution.py:247
  46.6 2.7 %collective-permute-start.12 = (f32[8,128]{1,0:T(8,128)S(1)}, f32[8,128]{1,0:T(8,128)S(1)}, u32[]{:S(2)}, u32[]{:S(2)}) collective-permute-start(f32[8,128]{1,0:T(8,128)S(1)} %get-tuple-element.23), channel_id=1, source_target_pairs={{0,1},{1,0},{2,3},{3,2},{4,5},{5,4},{6,7},{7,6},{8,9},{9,8},{10,11... | collective-permute-start | bytes 12296 | tf_op jit(solution)/shard_map/ppermute | solution.py:247
  49.3 5.2 %collective-permute-start.13 = (f32[8,128]{1,0:T(8,128)S(1)}, f32[8,128]{1,0:T(8,128)S(1)}, u32[]{:S(2)}, u32[]{:S(2)}) collective-permute-start(f32[8,128]{1,0:T(8,128)S(1)} %add_add_fusion.refs_0_), channel_id=1, source_target_pairs={{0,13},{1,12},{2,15},{3,14},{4,9},{5,8},{6,11},{7,10},{8,5},{9,4},... | collective-permute-start | bytes 12296 | tf_op jit(solution)/shard_map/ppermute | solution.py:339
  51.1 3.9 %collective-permute-start.14 = (f32[8,128]{1,0:T(8,128)S(1)}, f32[8,128]{1,0:T(8,128)S(1)}, u32[]{:S(2)}, u32[]{:S(2)}) collective-permute-start(f32[8,128]{1,0:T(8,128)S(1)} %add_add_fusion.refs_0_), channel_id=1, source_target_pairs={{0,9},{1,8},{2,11},{3,10},{4,13},{5,12},{6,15},{7,14},{8,1},{9,0},... | collective-permute-start | bytes 12296 | tf_op jit(solution)/shard_map/ppermute | solution.py:339
  52.0 3.1 %collective-permute-start.15 = (f32[8,128]{1,0:T(8,128)S(1)}, f32[8,128]{1,0:T(8,128)S(1)}, u32[]{:S(2)}, u32[]{:S(2)}) collective-permute-start(f32[8,128]{1,0:T(8,128)S(1)} %add_add_fusion.refs_0_), channel_id=1, source_target_pairs={{0,5},{1,4},{2,7},{3,6},{4,1},{5,0},{6,3},{7,2},{8,13},{9,12},{10,... | collective-permute-start | bytes 12296 | tf_op jit(solution)/shard_map/ppermute | solution.py:339

commit v8 on v6

--- a/solution.py
+++ b/solution.py
@@ -211,7 +211,7 @@
 def rms_kernel(scale, *refs):
     *parts, out_ref = refs
     mean = sum(part[...] for part in parts) * scale
-    out_ref[0] = jnp.sqrt(mean)[0, 0]
+    out_ref[...] = jnp.sqrt(mean)[:1, :1]
 
 
 def gather_line(x, again, axis):
@@ -347,12 +347,12 @@
         rms = pl.pallas_call(
             functools.partial(rms_kernel, 1.0 / (2.0 * H * everyone * reals)),
             in_specs=[VMEM] * (1 + len(got)),
-            out_specs=SMEM,
-            out_shape=jax.ShapeDtypeStruct((1,), F32),
+            out_specs=VMEM,
+            out_shape=jax.ShapeDtypeStruct((1, 1), F32),
             compiler_params=params(),
             name="rms",
         )(total, *got)
-        return new.reshape(vel.shape), rms
+        return new.reshape(vel.shape), rms.reshape(1)
 
     return local
 

time: 55.9 us -> 55.9 us (level)
  no operation moved by 1% of the time
where the time goes in v8:
time: 55.9 us; the launch traced here: 55.6 us
  waiting for transfers between devices  20.5 us (37%)
  starting transfers between devices  19.9 us (36%)
  Pallas kernels  11.7 us (21%)
  local copies, waits for them, and re-layouts  2.66 us (5%)
  between operations  0.82 us (1%)
    ppermute x1, waiting for transfers between devices, gather_line(): outer = lax.ppermute(cross, axis, [(1, 0), (2, 3)])  8.91 us
    ppermute x7, waiting for transfers between devices, flipped(): return lax.ppermute(x, 'harm', [(i, i ^ flip) for i in range(4)])  6.7 us
    ppermute x1, starting transfers between devices, gather_line(): near = lax.ppermute(x, axis, [(0, 1), (1, 0), (2, 3), (3, 2)])  6.01 us
    pallas_call x1, Pallas kernels, local(): pl.pallas_call(functools.partial(time_kernel, harm, bodies, reals), grid=...  4.77 us
    ppermute x1, waiting for transfers between devices, gather_line(): near = lax.ppermute(x, axis, [(0, 1), (1, 0), (2, 3), (3, 2)])  4.5 us
    ppermute x7, starting transfers between devices, flipped(): return lax.ppermute(x, 'harm', [(i, i ^ flip) for i in range(4)])  4.01 us
    ppermute x3, starting transfers between devices, crossed(): return lax.ppermute(total, ('body', 'harm'), pairs)  3.88 us
    ppermute x1, starting transfers between devices, gather_line(): across = lax.ppermute(again, axis, [(0, 3), (3, 0)])  3.25 us
  transfers between devices with their start and end apart: 15, of which 7 were waited for; matrix products, arithmetic and copies ran while one was open for 0% of the time, Pallas kernels for 19%

profile of v8, /device:TPU:0, one launch (start us, length us, event | category | flops | bytes accessed | tf_op | source)
XLA Modules:
  0.0 55.6 jit_solution(14198009535586498110)
XLA Ops:
  0.6 0.0 copy-start.6
  0.6 0.0 copy-start.7
  0.7 0.0 copy-start.1
  0.7 1.6 %copy-done.1 = f32[2,32,64,64]{3,2,1,0:T(8,128)S(1)} copy-done((f32[2,32,64,64]{3,2,1,0:T(8,128)S(1)}, f32[2,32,64,64]{3,2,1,0:T(8,128)}, u32[]{:S(2)}) %copy-start.1) | copy-done | bytes 1048600
  2.3 0.2 pack_couple.1.own_ref
  2.5 0.0 copy-start
  2.5 0.0 copy-start.2
  2.5 0.8 %collective-permute-start = (bf16[2048,128]{1,0:T(8,128)(2,1)S(1)}, bf16[2048,128]{1,0:T(8,128)(2,1)S(1)}, u32[]{:S(2)}, u32[]{:S(2)}) collective-permute-start(bf16[2048,128]{1,0:T(8,128)(2,1)S(1)} %pack_couple.1.own_ref), channel_id=1, source_target_pairs={{4,8},{8,4},{5,9},{9,5},{6,10},{10,6},{7,11},{11,7},{20,24},{24,20... | collective-permute-start | bytes 1572872 | tf_op jit(solution)/shard_map/ppermute | solution.py:219
  3.3 6.0 %collective-permute-start.2 = (bf16[2048,128]{1,0:T(8,128)(2,1)S(1)}, bf16[2048,128]{1,0:T(8,128)(2,1)S(1)}, u32[]{:S(2)}, u32[]{:S(2)}) collective-permute-start(bf16[2048,128]{1,0:T(8,128)(2,1)S(1)} %pack_couple.1.own_ref), channel_id=1, source_target_pairs={{0,4},{4,0},{8,12},{12,8},{1,5},{5,1},{9,13},{13,9},{2,6},{6,2},{1... | collective-permute-start | bytes 1572872 | tf_op jit(solution)/shard_map/ppermute | solution.py:218
  9.3 1.3 %pack_time.1 = (bf16[64,2048]{1,0:T(8,128)(2,1)S(1)}, bf16[64,2048]{1,0:T(8,128)(2,1)S(1)}, bf16[2048,128]{1,0:T(8,128)(2,1)S(1)}) custom-call(f32[4096,64]{1,0:T(8,128)S(1)} %bitcast.5), custom_call_target="tpu_custom_call" | custom-call | bytes 1024 | tf_op jit(solution)/shard_map/pack_time/pallas_call | solution.py:258
  10.7 0.1 collective-permute-start.5
  10.8 1.6 %collective-permute-start.6 = (bf16[64,2048]{1,0:T(8,128)(2,1)S(1)}, bf16[64,2048]{1,0:T(8,128)(2,1)S(1)}, u32[]{:S(2)}, u32[]{:S(2)}) collective-permute-start(bf16[64,2048]{1,0:T(8,128)(2,1)S(1)} %get-tuple-element.15.own_ref), channel_id=1, source_target_pairs={{0,2},{1,3},{2,0},{3,1},{4,6},{5,7},{6,4},{7,5},{8,10},{9,11},{10,... | collective-permute-start | bytes 786440 | tf_op jit(solution)/shard_map/ppermute | solution.py:248
  12.4 0.3 collective-permute-start.7
  12.6 0.0 collective-permute-done.5.core_ref
  12.6 3.2 %collective-permute-start.4 = (bf16[2048,128]{1,0:T(8,128)(2,1)S(1)}, bf16[2048,128]{1,0:T(8,128)(2,1)S(1)}, u32[]{:S(2)}, u32[]{:S(2)}) collective-permute-start(bf16[2048,128]{1,0:T(8,128)(2,1)S(1)} %get-tuple-element.14), channel_id=1, source_target_pairs={{0,12},{12,0},{1,13},{13,1},{2,14},{14,2},{3,15},{15,3},{16,28},{2... | collective-permute-start | bytes 1572872 | tf_op jit(solution)/shard_map/ppermute | solution.py:220
  15.9 0.0 collective-permute-done.cross_ref
  15.9 1.3 %collective-permute-start.1 = (bf16[2048,128]{1,0:T(8,128)(2,1)S(1)}, bf16[2048,128]{1,0:T(8,128)(2,1)S(1)}, u32[]{:S(2)}, u32[]{:S(2)}) collective-permute-start(bf16[2048,128]{1,0:T(8,128)(2,1)S(1)} %collective-permute-done.cross_ref), channel_id=1, source_target_pairs={{4,0},{8,12},{5,1},{9,13},{6,2},{10,14},{7,3},{11,15},{20,16},{24,... | collective-permute-start | bytes 1572872 | tf_op jit(solution)/shard_map/ppermute | solution.py:221
  17.2 4.5 %collective-permute-done.2.near_ref = bf16[2048,128]{1,0:T(8,128)(2,1)S(1)} collective-permute-done((bf16[2048,128]{1,0:T(8,128)(2,1)S(1)}, bf16[2048,128]{1,0:T(8,128)(2,1)S(1)}, u32[]{:S(2)}, u32[]{:S(2)}) %collective-permute-start.2) | collective-permute-done | bytes 524320 | tf_op jit(solution)/shard_map/ppermute | solution.py:218
  21.7 0.7 %collective-permute-start.3 = (bf16[2048,128]{1,0:T(8,128)(2,1)S(1)}, bf16[2048,128]{1,0:T(8,128)(2,1)S(1)}, u32[]{:S(2)}, u32[]{:S(2)}) collective-permute-start(bf16[2048,128]{1,0:T(8,128)(2,1)S(1)} %collective-permute-done.2.near_ref), channel_id=1, source_target_pairs={{4,8},{8,4},{5,9},{9,5},{6,10},{10,6},{7,11},{11,7},{20,24},{24,20... | collective-permute-start | bytes 1572872 | tf_op jit(solution)/shard_map/ppermute | solution.py:222
  22.4 0.0 collective-permute-done.6.far_ref
  22.4 2.3 %collective-permute-done.7.far_core_ref = bf16[64,2048]{1,0:T(8,128)(2,1)S(1)} collective-permute-done((bf16[64,2048]{1,0:T(8,128)(2,1)S(1)}, bf16[64,2048]{1,0:T(8,128)(2,1)S(1)}, u32[]{:S(2)}, u32[]{:S(2)}) %collective-permute-start.7) | collective-permute-done | bytes 262176 | tf_op jit(solution)/shard_map/ppermute | solution.py:248
  24.7 0.0 copy-done.4
  24.7 0.0 copy-start.5
  24.7 1.0 %copy-done.5 = bf16[512,512]{1,0:T(8,128)(2,1)S(1)} copy-done((bf16[512,512]{1,0:T(8,128)(2,1)S(1)}, bf16[512,512]{1,0:T(8,128)(2,1)}, u32[]{:S(2)}) %copy-start.5) | copy-done | bytes 524312
  25.7 4.8 %time_kernel.1 = (f32[72,2048]{1,0:T(8,128)S(1)}, f32[32,2048]{1,0:T(8,128)S(1)}, f32[40,2048]{1,0:T(8,128)S(1)}) custom-call(f32[64]{0:T(128)S(1)} %copy-done.6, f32[64]{0:T(128)S(1)} %copy-done.7, bf16[64,2048]{1,0:T(8,128)(2,1)S(1)} %get-tuple-element.15.own_ref, bf16[64,2048]{1,0:T(8,128)(2,1)S(1)} %collective-permute-done.5.core_ref, ...), custom_call_target="tpu_custom_call" | custom-call | bytes 1024 | tf_op jit(solution)/shard_map/time_kernel/pallas_call | solution.py:281
  30.5 0.6 %collective-permute-start.9 = (f32[40,2048]{1,0:T(8,128)S(1)}, f32[40,2048]{1,0:T(8,128)S(1)}, u32[]{:S(2)}, u32[]{:S(2)}) collective-permute-start(f32[40,2048]{1,0:T(8,128)S(1)} %get-tuple-element.19), channel_id=1, source_target_pairs={{0,1},{1,0},{2,3},{3,2},{4,5},{5,4},{6,7},{7,6},{8,9},{9,8},{10,11... | collective-permute-start | bytes 983048 | tf_op jit(solution)/shard_map/ppermute | solution.py:248
  31.1 0.1 collective-permute-start.8
  31.2 1.6 %collective-permute-done.8.other_re_ref = f32[32,2048]{1,0:T(8,128)S(1)} collective-permute-done((f32[32,2048]{1,0:T(8,128)S(1)}, f32[32,2048]{1,0:T(8,128)S(1)}, u32[]{:S(2)}, u32[]{:S(2)}) %collective-permute-start.8) | collective-permute-done | bytes 262176 | tf_op jit(solution)/shard_map/ppermute | solution.py:248
  32.8 0.0 collective-permute-done.9.other_im_ref
  32.8 0.0 copy-done.3
  32.8 1.6 %prepare.1 = (f32[2048,128]{1,0:T(8,128)S(1)}, f32[2048,128]{1,0:T(8,128)S(1)}, f32[2048,128]{1,0:T(8,128)S(1)}, f32[2048,128]{1,0:T(8,128)S(1)}) custom-call(bf16[2,32,64,256]{3,2,1,0:T(8,128)(2,1)S(1)} %copy-done, f32[72,2048]{1,0:T(8,128)S(1)} %get-tuple-element.17.mine_ref, f32[32,2048]{1,0:T(8,128)S(1)} %collective-permute-done.8.other_re_ref, ...), custom_call_target="tpu_custom_call" | custom-call | bytes 1024 | tf_op jit(solution)/shard_map/prepare/pallas_call | solution.py:294
  34.4 0.0 collective-permute-done.4.across_ref
  34.4 0.9 %partial.1.refs_2_ = f32[2048,128]{1,0:T(8,128)S(1)} custom-call(bf16[2,32,64,256]{3,2,1,0:T(8,128)(2,1)S(1)} %copy-done, bf16[2048,128]{1,0:T(8,128)(2,1)S(1)} %pack_couple.1.own_ref, bf16[2048,128]{1,0:T(8,128)(2,1)S(1)} %collective-permute-done.2.near_ref, bf16[2048,128]{1,0:T(8,128)(2,1)S(1)} %collective-permute-done.cross_ref, ...), custom_call_target="tpu_custom_call" | custom-call | bytes 1024 | tf_op jit(solution)/shard_map/partial/pallas_call | solution.py:305
  35.3 8.9 %collective-permute-done.1.refs_0_ = bf16[2048,128]{1,0:T(8,128)(2,1)S(1)} collective-permute-done((bf16[2048,128]{1,0:T(8,128)(2,1)S(1)}, bf16[2048,128]{1,0:T(8,128)(2,1)S(1)}, u32[]{:S(2)}, u32[]{:S(2)}) %collective-permute-start.1) | collective-permute-done | bytes 524320 | tf_op jit(solution)/shard_map/ppermute | solution.py:221
  44.2 0.0 collective-permute-done.3.refs_1_
  44.2 0.7 %couple.1 = (f32[2048,128]{1,0:T(8,128)S(1)}, f32[8,128]{1,0:T(8,128)S(1)}) custom-call(bf16[2,32,64,256]{3,2,1,0:T(8,128)(2,1)S(1)} %copy-done, bf16[2048,128]{1,0:T(8,128)(2,1)S(1)} %collective-permute-done.1.refs_0_, bf16[2048,128]{1,0:T(8,128)(2,1)S(1)} %collective-permute-done.3.refs_1_, f32[2048,128]{1,0:T(8,128)S(1)} %partial.1.refs_2_), custom_call_target="tpu_custom_call" | custom-call | bytes 1024 | tf_op jit(solution)/shard_map/couple/pallas_call | solution.py:315
  45.0 0.1 collective-permute-start.10
  45.0 1.2 %collective-permute-done.10 = f32[8,128]{1,0:T(8,128)S(1)} collective-permute-done((f32[8,128]{1,0:T(8,128)S(1)}, f32[8,128]{1,0:T(8,128)S(1)}, u32[]{:S(2)}, u32[]{:S(2)}) %collective-permute-start.10) | collective-permute-done | bytes 4128 | tf_op jit(solution)/shard_map/ppermute | solution.py:248
  46.2 1.3 %collective-permute-start.11 = (f32[8,128]{1,0:T(8,128)S(1)}, f32[8,128]{1,0:T(8,128)S(1)}, u32[]{:S(2)}, u32[]{:S(2)}) collective-permute-start(f32[8,128]{1,0:T(8,128)S(1)} %add.6), channel_id=1, source_target_pairs={{0,3},{1,2},{2,1},{3,0},{4,7},{5,6},{6,5},{7,4},{8,11},{9,10},{10,... | collective-permute-start | bytes 12296 | tf_op jit(solution)/shard_map/ppermute | solution.py:248
  47.5 1.7 %collective-permute-done.11 = f32[8,128]{1,0:T(8,128)S(1)} collective-permute-done((f32[8,128]{1,0:T(8,128)S(1)}, f32[8,128]{1,0:T(8,128)S(1)}, u32[]{:S(2)}, u32[]{:S(2)}) %collective-permute-start.11) | collective-permute-done | bytes 4128 | tf_op jit(solution)/shard_map/ppermute | solution.py:248
  49.2 1.9 %collective-permute-start.12 = (f32[8,128]{1,0:T(8,128)S(1)}, f32[8,128]{1,0:T(8,128)S(1)}, u32[]{:S(2)}, u32[]{:S(2)}) collective-permute-start(f32[8,128]{1,0:T(8,128)S(1)} %add.7.refs_0_), channel_id=1, source_target_pairs={{0,13},{1,12},{2,15},{3,14},{4,9},{5,8},{6,11},{7,10},{8,5},{9,4},... | collective-permute-start | bytes 12296 | tf_op jit(solution)/shard_map/ppermute | solution.py:342
  51.2 0.2 collective-permute-start.13
  51.4 1.7 %collective-permute-start.14 = (f32[8,128]{1,0:T(8,128)S(1)}, f32[8,128]{1,0:T(8,128)S(1)}, u32[]{:S(2)}, u32[]{:S(2)}) collective-permute-start(f32[8,128]{1,0:T(8,128)S(1)} %add.7.refs_0_), channel_id=1, source_target_pairs={{0,5},{1,4},{2,7},{3,6},{4,1},{5,0},{6,3},{7,2},{8,13},{9,12},{10,... | collective-permute-start | bytes 12296 | tf_op jit(solution)/shard_map/ppermute | solution.py:342
  53.1 1.7 %finish.1 = f32[2,2048,64]{2,1,0:T(8,128)} custom-call(f32[2048,128]{1,0:T(8,128)S(1)} %get-tuple-element.21.res_ref, f32[2048,128]{1,0:T(8,128)S(1)} %get-tuple-element.22.p_ref, f32[2048,128]{1,0:T(8,128)S(1)} %get-tuple-element.23.q_ref, f32[2048,128]{1,0:T(8,128)S(1)} %get-tuple-element.24.vel_ref), custom_call_target="tpu_custom_call" | custom-call | bytes 1024 | tf_op jit(solution)/shard_map/finish/pallas_call | solution.py:326
  54.8 0.0 collective-permute-done.12.refs_1_
  54.8 0.3 collective-permute-done.13.refs_2_
  55.1 0.0 collective-permute-done.14.refs_3_
  55.1 0.5 rms.1
  (8 shorter events, 0.0 us)
Async XLA Ops:
  0.6 24.0 %copy-start.6 = (f32[64]{0:T(128)S(1)}, f32[64]{0:T(128)}, u32[]{:S(2)}) copy-start(f32[64]{0:T(128)} %quad_ref.1) | copy-start | bytes 772
  0.6 24.0 %copy-start.7 = (f32[64]{0:T(128)S(1)}, f32[64]{0:T(128)}, u32[]{:S(2)}) copy-start(f32[64]{0:T(128)} %coul_ref.1) | copy-start | bytes 772
  0.7 1.6 %copy-start.1 = (f32[2,32,64,64]{3,2,1,0:T(8,128)S(1)}, f32[2,32,64,64]{3,2,1,0:T(8,128)}, u32[]{:S(2)}) copy-start(f32[2,32,64,64]{3,2,1,0:T(8,128)} %param.7) | copy-start | bytes 3145732
  2.3 22.4 %copy-start.4 = (bf16[256,1536]{1,0:T(8,128)(2,1)S(1)}, bf16[256,1536]{1,0:T(8,128)(2,1)}, u32[]{:S(2)}) copy-start(bf16[256,1536]{1,0:T(8,128)(2,1)} %constant.5.clone.inv_ref) | copy-start | bytes 2359300
  2.3 30.5 %copy-start.3 = (f32[2,32,64,64]{3,2,1,0:T(8,128)S(1)}, f32[2,32,64,64]{3,2,1,0:T(8,128)}, u32[]{:S(2)}) copy-start(f32[2,32,64,64]{3,2,1,0:T(8,128)} %param.9) | copy-start | bytes 3145732
  2.5 30.3 %copy-start = (bf16[2,32,64,256]{3,2,1,0:T(8,128)(2,1)S(1)}, bf16[2,32,64,256]{3,2,1,0:T(8,128)(2,1)}, u32[]{:S(2)}) copy-start(bf16[2,32,64,256]{3,2,1,0:T(8,128)(2,1)} %imped_ref.5) | copy-start | bytes 6291460
  2.5 30.3 %copy-start.2 = (f32[2,32,64,64]{3,2,1,0:T(8,128)S(1)}, f32[2,32,64,64]{3,2,1,0:T(8,128)}, u32[]{:S(2)}) copy-start(f32[2,32,64,64]{3,2,1,0:T(8,128)} %param.7) | copy-start | bytes 3145732
  2.5 13.4 %collective-permute-start = (bf16[2048,128]{1,0:T(8,128)(2,1)S(1)}, bf16[2048,128]{1,0:T(8,128)(2,1)S(1)}, u32[]{:S(2)}, u32[]{:S(2)}) collective-permute-start(bf16[2048,128]{1,0:T(8,128)(2,1)S(1)} %pack_couple.1.own_ref), channel_id=1, source_target_pairs={{4,8},{8,4},{5,9},{9,5},{6,10},{10,6},{7,11},{11,7},{20,24},{24,20... | collective-permute-start | bytes 1572872 | tf_op jit(solution)/shard_map/ppermute | solution.py:219
  3.3 18.4 %collective-permute-start.2 = (bf16[2048,128]{1,0:T(8,128)(2,1)S(1)}, bf16[2048,128]{1,0:T(8,128)(2,1)S(1)}, u32[]{:S(2)}, u32[]{:S(2)}) collective-permute-start(bf16[2048,128]{1,0:T(8,128)(2,1)S(1)} %pack_couple.1.own_ref), channel_id=1, source_target_pairs={{0,4},{4,0},{8,12},{12,8},{1,5},{5,1},{9,13},{13,9},{2,6},{6,2},{1... | collective-permute-start | bytes 1572872 | tf_op jit(solution)/shard_map/ppermute | solution.py:218
  10.7 1.9 %collective-permute-start.5 = (bf16[64,2048]{1,0:T(8,128)(2,1)S(1)}, bf16[64,2048]{1,0:T(8,128)(2,1)S(1)}, u32[]{:S(2)}, u32[]{:S(2)}) collective-permute-start(bf16[64,2048]{1,0:T(8,128)(2,1)S(1)} %get-tuple-element.16), channel_id=1, source_target_pairs={{0,1},{1,0},{2,3},{3,2},{4,5},{5,4},{6,7},{7,6},{8,9},{9,8},{10,11... | collective-permute-start | bytes 786440 | tf_op jit(solution)/shard_map/ppermute | solution.py:248
  10.8 11.6 %collective-permute-start.6 = (bf16[64,2048]{1,0:T(8,128)(2,1)S(1)}, bf16[64,2048]{1,0:T(8,128)(2,1)S(1)}, u32[]{:S(2)}, u32[]{:S(2)}) collective-permute-start(bf16[64,2048]{1,0:T(8,128)(2,1)S(1)} %get-tuple-element.15.own_ref), channel_id=1, source_target_pairs={{0,2},{1,3},{2,0},{3,1},{4,6},{5,7},{6,4},{7,5},{8,10},{9,11},{10,... | collective-permute-start | bytes 786440 | tf_op jit(solution)/shard_map/ppermute | solution.py:248
  12.4 12.3 %collective-permute-start.7 = (bf16[64,2048]{1,0:T(8,128)(2,1)S(1)}, bf16[64,2048]{1,0:T(8,128)(2,1)S(1)}, u32[]{:S(2)}, u32[]{:S(2)}) collective-permute-start(bf16[64,2048]{1,0:T(8,128)(2,1)S(1)} %get-tuple-element.16), channel_id=1, source_target_pairs={{0,3},{1,2},{2,1},{3,0},{4,7},{5,6},{6,5},{7,4},{8,11},{9,10},{10,... | collective-permute-start | bytes 786440 | tf_op jit(solution)/shard_map/ppermute | solution.py:248
  12.6 21.8 %collective-permute-start.4 = (bf16[2048,128]{1,0:T(8,128)(2,1)S(1)}, bf16[2048,128]{1,0:T(8,128)(2,1)S(1)}, u32[]{:S(2)}, u32[]{:S(2)}) collective-permute-start(bf16[2048,128]{1,0:T(8,128)(2,1)S(1)} %get-tuple-element.14), channel_id=1, source_target_pairs={{0,12},{12,0},{1,13},{13,1},{2,14},{14,2},{3,15},{15,3},{16,28},{2... | collective-permute-start | bytes 1572872 | tf_op jit(solution)/shard_map/ppermute | solution.py:220
  15.9 28.3 %collective-permute-start.1 = (bf16[2048,128]{1,0:T(8,128)(2,1)S(1)}, bf16[2048,128]{1,0:T(8,128)(2,1)S(1)}, u32[]{:S(2)}, u32[]{:S(2)}) collective-permute-start(bf16[2048,128]{1,0:T(8,128)(2,1)S(1)} %collective-permute-done.cross_ref), channel_id=1, source_target_pairs={{4,0},{8,12},{5,1},{9,13},{6,2},{10,14},{7,3},{11,15},{20,16},{24,... | collective-permute-start | bytes 1572872 | tf_op jit(solution)/shard_map/ppermute | solution.py:221
  21.7 22.5 %collective-permute-start.3 = (bf16[2048,128]{1,0:T(8,128)(2,1)S(1)}, bf16[2048,128]{1,0:T(8,128)(2,1)S(1)}, u32[]{:S(2)}, u32[]{:S(2)}) collective-permute-start(bf16[2048,128]{1,0:T(8,128)(2,1)S(1)} %collective-permute-done.2.near_ref), channel_id=1, source_target_pairs={{4,8},{8,4},{5,9},{9,5},{6,10},{10,6},{7,11},{11,7},{20,24},{24,20... | collective-permute-start | bytes 1572872 | tf_op jit(solution)/shard_map/ppermute | solution.py:222
  24.7 1.0 %copy-start.5 = (bf16[512,512]{1,0:T(8,128)(2,1)S(1)}, bf16[512,512]{1,0:T(8,128)(2,1)}, u32[]{:S(2)}) copy-start(bf16[512,512]{1,0:T(8,128)(2,1)} %constant.4.clone.fwd_ref) | copy-start | bytes 1572868
  30.5 2.3 %collective-permute-start.9 = (f32[40,2048]{1,0:T(8,128)S(1)}, f32[40,2048]{1,0:T(8,128)S(1)}, u32[]{:S(2)}, u32[]{:S(2)}) collective-permute-start(f32[40,2048]{1,0:T(8,128)S(1)} %get-tuple-element.19), channel_id=1, source_target_pairs={{0,1},{1,0},{2,3},{3,2},{4,5},{5,4},{6,7},{7,6},{8,9},{9,8},{10,11... | collective-permute-start | bytes 983048 | tf_op jit(solution)/shard_map/ppermute | solution.py:248
  31.1 1.6 %collective-permute-start.8 = (f32[32,2048]{1,0:T(8,128)S(1)}, f32[32,2048]{1,0:T(8,128)S(1)}, u32[]{:S(2)}, u32[]{:S(2)}) collective-permute-start(f32[32,2048]{1,0:T(8,128)S(1)} %get-tuple-element.18), channel_id=1, source_target_pairs={{0,1},{1,0},{2,3},{3,2},{4,5},{5,4},{6,7},{7,6},{8,9},{9,8},{10,11... | collective-permute-start | bytes 786440 | tf_op jit(solution)/shard_map/ppermute | solution.py:248
  45.0 1.2 %collective-permute-start.10 = (f32[8,128]{1,0:T(8,128)S(1)}, f32[8,128]{1,0:T(8,128)S(1)}, u32[]{:S(2)}, u32[]{:S(2)}) collective-permute-start(f32[8,128]{1,0:T(8,128)S(1)} %get-tuple-element.25), channel_id=1, source_target_pairs={{0,1},{1,0},{2,3},{3,2},{4,5},{5,4},{6,7},{7,6},{8,9},{9,8},{10,11... | collective-permute-start | bytes 12296 | tf_op jit(solution)/shard_map/ppermute | solution.py:248
  46.2 3.0 %collective-permute-start.11 = (f32[8,128]{1,0:T(8,128)S(1)}, f32[8,128]{1,0:T(8,128)S(1)}, u32[]{:S(2)}, u32[]{:S(2)}) collective-permute-start(f32[8,128]{1,0:T(8,128)S(1)} %add.6), channel_id=1, source_target_pairs={{0,3},{1,2},{2,1},{3,0},{4,7},{5,6},{6,5},{7,4},{8,11},{9,10},{10,... | collective-permute-start | bytes 12296 | tf_op jit(solution)/shard_map/ppermute | solution.py:248
  49.2 5.5 %collective-permute-start.12 = (f32[8,128]{1,0:T(8,128)S(1)}, f32[8,128]{1,0:T(8,128)S(1)}, u32[]{:S(2)}, u32[]{:S(2)}) collective-permute-start(f32[8,128]{1,0:T(8,128)S(1)} %add.7.refs_0_), channel_id=1, source_target_pairs={{0,13},{1,12},{2,15},{3,14},{4,9},{5,8},{6,11},{7,10},{8,5},{9,4},... | collective-permute-start | bytes 12296 | tf_op jit(solution)/shard_map/ppermute | solution.py:342
  51.2 3.9 %collective-permute-start.13 = (f32[8,128]{1,0:T(8,128)S(1)}, f32[8,128]{1,0:T(8,128)S(1)}, u32[]{:S(2)}, u32[]{:S(2)}) collective-permute-start(f32[8,128]{1,0:T(8,128)S(1)} %add.7.refs_0_), channel_id=1, source_target_pairs={{0,9},{1,8},{2,11},{3,10},{4,13},{5,12},{6,15},{7,14},{8,1},{9,0},... | collective-permute-start | bytes 12296 | tf_op jit(solution)/shard_map/ppermute | solution.py:342
  51.4 3.7 %collective-permute-start.14 = (f32[8,128]{1,0:T(8,128)S(1)}, f32[8,128]{1,0:T(8,128)S(1)}, u32[]{:S(2)}, u32[]{:S(2)}) collective-permute-start(f32[8,128]{1,0:T(8,128)S(1)} %add.7.refs_0_), channel_id=1, source_target_pairs={{0,5},{1,4},{2,7},{3,6},{4,1},{5,0},{6,3},{7,2},{8,13},{9,12},{10,... | collective-permute-start | bytes 12296 | tf_op jit(solution)/shard_map/ppermute | solution.py:342
